TPU v7x, 128 devices: a whole 4x4x4 slice. The times are simulated.
128 devices in a mesh: view: 8 (over x, core), depth: 16 (over y, z).
Axes of the slice: x: 4, y: 4, z: 4, core: 2. Of those that a mesh axis runs over, the one named last changes fastest.
Arguments:
- features: float32 [8, 16, 32, 3, 4096], P('view', 'depth'), may hold values from -6 to 6
- spacing: float32 [8, 16, 3, 4096], P('view', 'depth'), may hold values from 0.01 to 0.15
- counts: int32 [8, 16, 4096], P('view', 'depth'), may hold values from 0 to 3
- depth_rank: int32 [8, 16], P('view', 'depth'), may hold values from 0 to 15, as said below
- target: float32 [8, 64, 4096], P('view', None, 'depth'), may hold values from 0 to 1
- first_weight: float32 [32, 256], replicated, may hold values from -1 to 1
- first_bias: float32 [256], replicated, may hold values from -3 to 3
- second_weight: float32 [256, 256], replicated, may hold values from -0.375 to 0.375
- second_bias: float32 [256], replicated, may hold values from -3 to 3
- last_weight: float32 [256, 65], replicated, may hold values from -0.375 to 0.375
- last_bias: float32 [65], replicated, may hold values from -3 to 3
Outputs:
- pixels: float32 [8, 64, 4096], P('view', None, 'depth')
- first_update: float32 [32, 256], replicated
- first_shift: float32 [256], replicated
- second_update: float32 [256, 256], replicated
- second_shift: float32 [256], replicated
- last_update: float32 [256, 65], replicated
- last_shift: float32 [65], replicated
Inputs may be any that keep to these rules, and one draw needn't show every extreme that they name: depth_rank[v, d] equals d XOR a number fixed for view group v, so each view group's ranks are a permutation in which every aligned block of 2^k regions takes consecutive positions. Sample slots s with s < counts[v, d, r] are live.
All inputs are finite; a program needn't handle non-finite values.
Results may differ from a plain program's by a relative error of at most 0.0003.
Values sent between devices are 32-bit elements; how exact they have to be, the bound alone decides.
No kernel may reach another device: no remote copies, remote signals or barrier semaphores. Data moves between devices by JAX's collectives and lax.ppermute only.
A program may use at most 128 MiB of HBM per device.

v0:
```python
import jax
import jax.numpy as jnp
from jax import lax
from jax.sharding import PartitionSpec as P

precise = lax.Precision.HIGHEST
epsilon = 1e-05


def partner(value, axis, distance):
    mask = 2**distance
    pairs = [(source, source ^ mask) for source in range(lax.axis_size(axis))]
    return lax.ppermute(value, axis, pairs)


def project(weight, inputs):
    return lax.dot_general(
        weight,
        inputs,
        (((0,), (0,)), ((), ())),
        precision=precise,
        preferred_element_type=jnp.float32,
    )


def render(params, sample_feats, sample_spacing, live_mask):
    first_weight, first_bias, second_weight, second_bias, last_weight, last_bias = params
    columns = sample_feats.reshape(sample_feats.shape[0], -1)
    first_act = jax.nn.relu(project(first_weight, columns) + first_bias[:, None])
    second_act = jax.nn.relu(project(second_weight, first_act) + second_bias[:, None])
    raw_output = project(last_weight, second_act) + last_bias[:, None]
    raw_output = raw_output.reshape(
        raw_output.shape[0], sample_spacing.shape[0], sample_spacing.shape[1]
    )
    channels = raw_output.shape[0] - 1
    sample_color = jax.nn.sigmoid(raw_output[:channels])
    density = jax.nn.softplus(raw_output[channels])
    optical = density * sample_spacing * live_mask
    before = jnp.cumsum(optical, axis=0) - optical
    weight = jnp.exp(-before) * (1.0 - jnp.exp(-optical))
    region_color = jnp.sum(weight[None] * sample_color, axis=1)
    region_depth = jnp.sum(optical, axis=0)
    return (region_color, region_depth)


def normalize(gradient):
    return gradient / jnp.sqrt(jnp.mean(gradient * gradient) + epsilon)


def binary_compose(region_color, region_depth, my_index, my_rank, goal_pixels, regions, segment):
    channels = region_color.shape[0]
    colors = region_color.reshape(channels, regions, segment)
    depths = region_depth.reshape(regions, segment)
    levels = regions.bit_length() - 1
    stored = []
    for bit_level in range(levels):
        pair_count = colors.shape[1] // 2
        pair_colors = colors.reshape(channels, pair_count, 2, segment)
        pair_depths = depths.reshape(pair_count, 2, segment)
        is_upper = my_index >> bit_level & 1 == 1
        keep_color = jnp.where(is_upper, pair_colors[:, :, 1], pair_colors[:, :, 0])
        send_color = jnp.where(is_upper, pair_colors[:, :, 0], pair_colors[:, :, 1])
        keep_depth = jnp.where(is_upper, pair_depths[:, 1], pair_depths[:, 0])
        send_depth = jnp.where(is_upper, pair_depths[:, 0], pair_depths[:, 1])
        got_color, got_depth = partner((send_color, send_depth), "depth", bit_level)
        behind = my_rank >> bit_level & 1 == 1
        front_color = jnp.where(behind, got_color, keep_color)
        back_color = jnp.where(behind, keep_color, got_color)
        front_depth = jnp.where(behind, got_depth, keep_depth)
        back_depth = jnp.where(behind, keep_depth, got_depth)
        passed = jnp.exp(-front_depth)
        stored.append((back_color, passed, behind, is_upper))
        colors = front_color + passed[None] * back_color
        depths = front_depth + back_depth
    pixels = colors[:, 0, :]
    color_grad = (pixels - goal_pixels)[:, None, :]
    depth_grad = jnp.zeros_like(depths)
    for bit_level in reversed(range(levels)):
        back_color, passed, behind, is_upper = stored[bit_level]
        front_cgrad = color_grad
        front_dgrad = depth_grad - passed * jnp.sum(color_grad * back_color, axis=0)
        back_cgrad = passed[None] * color_grad
        back_dgrad = depth_grad
        keep_cgrad = jnp.where(behind, back_cgrad, front_cgrad)
        sent_cgrad = jnp.where(behind, front_cgrad, back_cgrad)
        keep_dgrad = jnp.where(behind, back_dgrad, front_dgrad)
        sent_dgrad = jnp.where(behind, front_dgrad, back_dgrad)
        got_cgrad, got_dgrad = partner((sent_cgrad, sent_dgrad), "depth", bit_level)
        color_grad = jnp.where(
            is_upper,
            jnp.stack([got_cgrad, keep_cgrad], axis=2),
            jnp.stack([keep_cgrad, got_cgrad], axis=2),
        ).reshape(channels, -1, segment)
        depth_grad = jnp.where(
            is_upper,
            jnp.stack([got_dgrad, keep_dgrad], axis=1),
            jnp.stack([keep_dgrad, got_dgrad], axis=1),
        ).reshape(-1, segment)
    return (pixels, color_grad.reshape(channels, -1), depth_grad.reshape(-1))


def local(
    features,
    spacing,
    counts,
    depth_rank,
    target,
    first_weight,
    first_bias,
    second_weight,
    second_bias,
    last_weight,
    last_bias,
):
    params = (first_weight, first_bias, second_weight, second_bias, last_weight, last_bias)
    sample_feats = features[0, 0]
    sample_spacing = spacing[0, 0]
    sample_ids = jnp.arange(sample_spacing.shape[0], dtype=jnp.int32)
    live_mask = (sample_ids[:, None] < counts[0, 0][None, :]).astype(jnp.float32)
    outputs, pullback = jax.vjp(
        lambda weights: render(weights, sample_feats, sample_spacing, live_mask), params
    )
    region_color, region_depth = outputs
    regions = lax.axis_size("depth")
    segment = region_color.shape[1] // regions
    goal_pixels = target[0]
    my_index = lax.axis_index("depth")
    my_rank = depth_rank[0, 0]
    pixels, color_grad, depth_grad = binary_compose(
        region_color, region_depth, my_index, my_rank, goal_pixels, regions, segment
    )
    gradients = pullback((color_grad, depth_grad))[0]
    totals = lax.psum(
        (gradients[0], gradients[1], gradients[2], gradients[3], gradients[4], gradients[5]),
        ("view", "depth"),
    )
    results = tuple((normalize(member) for member in totals))
    return (pixels[None], results[0], results[1], results[2], results[3], results[4], results[5])


def solution(mesh):
    return jax.shard_map(
        local,
        mesh=mesh,
        in_specs=(
            P("view", "depth", None, None, None),
            P("view", "depth", None, None),
            P("view", "depth", None),
            P("view", "depth"),
            P("view", None, "depth"),
            P(),
            P(),
            P(),
            P(),
            P(),
            P(),
        ),
        out_specs=(P("view", None, "depth"), P(), P(), P(), P(), P(), P()),
        check_vma=False,
    )
```

profile of v0, /device:TPU:1, one launch (start us, length us, event | category | flops | bytes accessed | tf_op | source)
XLA Modules:
  0.0 487.7 jit_solution(960481464850501577)
XLA Ops:
  7.3 2.5 copy.69
  10.7 10.2 %convolution_add_fusion = f32[256,12288]{1,0:T(8,128)S(1)} fusion(f32[32,256]{1,0:T(8,128)S(1)} %copy-done.13, f32[32,12288]{1,0:T(8,128)S(1)} %bitcast.214, f32[256]{0:T(256)S(1)} %copy-done.14), kind=kOutput, calls=%fused_computation.1 | convolution fusion | flops 1211105280 | bytes 14189568 | tf_op jit(solution)/shard_map/jvp()/dot_general | solution.py:17
  21.0 22.7 %convolution_add_fusion.1 = f32[12288,256]{1,0:T(8,128)} fusion(f32[256,256]{1,0:T(8,128)S(1)} %copy-done, f32[256,12288]{1,0:T(8,128)S(1)} %convolution_add_fusion, f32[256]{0:T(256)S(1)} %copy-done.15), kind=kOutput, calls=%fused_computation.3 | convolution fusion | flops 9669967872 | bytes 25428992 | tf_op jit(solution)/shard_map/jvp()/dot_general | solution.py:17
  43.7 15.5 %fusion.1 = f32[65,12288]{1,0:T(8,128)S(1)} fusion(f32[256,65]{0,1:T(8,128)S(1)} %copy-done.7, f32[12288,256]{1,0:T(8,128)} %convolution_add_fusion.1, f32[65]{0:T(128)S(1)} %copy-done.16), kind=kOutput, calls=%fused_computation.6 | convolution fusion | flops 2457612288 | bytes 15844612 | tf_op jit(solution)/shard_map/jvp()/dot_general | solution.py:17
  59.2 1.8 copy-done.2
  61.8 2.7 collective-permute-start.1
  64.5 4.3 fusion.15
  69.0 5.5 %div.62 = f32[64,3,4096]{2,1,0:T(4,128)} reshape(f32[64,12288]{1,0:T(8,128)} %fusion.15) | data formatting | bytes 6291456 | tf_op jit(solution)/shard_map/jvp()/div | solution.py:36
  74.5 5.1 %multiply_reduce_fusion = f32[64,4096]{1,0:T(8,128)S(1)} fusion(f32[64,3,4096]{2,1,0:T(4,128)} %div.62, f32[3,4096]{1,0:T(4,128)S(1)} %subtract_multiply_fusion.1), kind=kLoop, calls=%fused_computation.20 | loop fusion | flops 1310720 | bytes 4243456 | tf_op jit(solution)/shard_map/jvp()/reduce_sum | solution.py:41
  79.6 1.9 reshape_reshape.8
  81.5 2.7 broadcast_select_fusion
  86.6 3.5 collective-permute-start.3
  90.1 9.5 %collective-permute-done.3 = f32[4,256]{1,0:T(4,128)S(1)} collective-permute-done((f32[4,256]{1,0:T(4,128)S(1)}, f32[4,256]{1,0:T(4,128)S(1)}, u32[]{:S(2)}, u32[]{:S(2)}) %collective-permute-start.3) | collective-permute-done | bytes 4128 | tf_op jit(solution)/shard_map/ppermute | solution.py:13
  100.7 1.5 collective-permute-start.2
  102.8 1.3 collective-permute-start.5
  104.1 1.4 squeeze.13
  106.1 2.0 collective-permute-done.2
  109.2 1.4 collective-permute-start.4
  110.6 2.6 collective-permute-start.7
  113.2 2.9 collective-permute-start.6
  116.1 2.1 collective-permute-done.6
  120.7 2.5 collective-permute-start.9
  123.7 1.6 collective-permute-done.9
  130.3 2.2 collective-permute-done.11
  133.6 1.7 fusion.19
  137.1 2.2 collective-permute-start.13
  140.1 4.1 collective-permute-done.13
  144.9 1.3 maximum_select_fusion.1
  146.7 1.4 collective-permute-start.14
  148.5 9.1 %collective-permute-done.14 = f32[8,256]{1,0:T(8,128)S(1)} collective-permute-done((f32[8,256]{1,0:T(8,128)S(1)}, f32[8,256]{1,0:T(8,128)S(1)}, u32[]{:S(2)}, u32[]{:S(2)}) %collective-permute-start.14) | collective-permute-done | bytes 8224 | tf_op jit(solution)/shard_map/ppermute | solution.py:13
  157.7 1.8 copy.108
  159.6 2.1 select_n.629
  161.6 5.0 %fusion.12 = f32[64,3,4096]{2,1,0:T(4,128)} fusion(f32[64,3,4096]{2,1,0:T(4,128)} %div.62, f32[64,4096]{1,0:T(8,128)S(1)} %select_n.629, f32[3,4096]{1,0:T(4,128)S(1)} %subtract_multiply_fusion.1), kind=kLoop, calls=%fused_computation.19 | loop fusion | flops 3145728 | bytes 7389184 | tf_op jit(solution)/shard_map/transpose(jvp())/mul | solution.py:36
  166.6 1.2 broadcast_in_dim.10
  167.8 1.8 copy.125
  171.2 3.6 fusion.52
  175.7 2.1 copy.126
  177.8 11.8 %fusion.2 = f32[256,65]{0,1:T(8,128)} fusion(f32[65,12288]{1,0:T(8,128)S(1)} %bitcast.210, f32[12288,256]{1,0:T(8,128)} %convolution_add_fusion.1), kind=kOutput, calls=%fused_computation.7 | convolution fusion | flops 2456813568 | bytes 15844352 | tf_op jit(solution)/shard_map/transpose(jvp())/dot_general | solution.py:17
  189.7 14.9 %fusion.58 = (f32[256]{0:T(256)S(1)}, f32[12288,256]{1,0:T(8,128)}) fusion(f32[65,12288]{1,0:T(8,128)S(1)} %bitcast.211, f32[256,65]{0,1:T(8,128)S(1)} %copy-done.8, f32[12288,256]{1,0:T(8,128)} %convolution_add_fusion.1), kind=kOutput, calls=%fused_computation.158 | convolution fusion | flops 2463104768 | bytes 28428288 | tf_op jit(solution)/shard_map/transpose(jvp())/dot_general | solution.py:17
  204.6 14.2 %fusion.5 = f32[256,256]{1,0:T(8,128)} fusion(f32[12288,256]{1,0:T(8,128)} %get-tuple-element.58, f32[256,12288]{1,0:T(8,128)S(1)} %bitcast.209), kind=kOutput, calls=%fused_computation.10 | convolution fusion | flops 9666822144 | bytes 25427968 | tf_op jit(solution)/shard_map/transpose(jvp())/dot_general | solution.py:17
  218.8 18.8 %fusion.57 = (f32[256]{0:T(256)S(1)}, f32[256,12288]{1,0:T(8,128)}) fusion(f32[12288,256]{1,0:T(8,128)} %get-tuple-element.58, f32[256,256]{1,0:T(8,128)S(1)} %copy-done, f32[256,12288]{1,0:T(8,128)} %copy-done.1), kind=kOutput, calls=%fused_computation.157 | convolution fusion | flops 9673113600 | bytes 38011904 | tf_op jit(solution)/shard_map/transpose(jvp())/dot_general | solution.py:17
  237.6 13.7 %convolution_bitcast_fusion.1 = f32[32,256]{1,0:T(8,128)S(1)} fusion(f32[256,12288]{1,0:T(8,128)} %get-tuple-element.56, f32[32,12288]{1,0:T(8,128)S(1)} %bitcast.215), kind=kOutput, calls=%fused_computation.26 | convolution fusion | flops 1207959552 | bytes 14188544 | tf_op jit(solution)/shard_map/transpose(jvp())/dot_general | solution.py:17
  251.4 74.3 %all-reduce.2 = (f32[32,256]{1,0:T(8,128)S(1)}, f32[256]{0:T(256)S(1)}, f32[256]{0:T(256)S(1)}, f32[65]{0:T(128)S(1)}) all-reduce(f32[32,256]{1,0:T(8,128)S(1)} %convolution_bitcast_fusion.1, f32[256]{0:T(256)S(1)} %get-tuple-element.55, f32[256]{0:T(256)S(1)} %get-tuple-element.57, ...), channel_id=1, replica_groups=mesh['view'=8,'depth'=16] {'view','depth'}, use_global_device_ids=true, to_apply=%region_9.10 | all-reduce | flops 8769 | bytes 70152 | tf_op jit(solution)/shard_map/psum | solution.py:133
  332.5 140.4 %all-reduce.6.cloned.1.call-done = (f32[256,256]{1,0:T(8,128)}, f32[256,65]{0,1:T(8,128)}) async-done(((f32[256,256]{1,0:T(8,128)}, f32[256,65]{0,1:T(8,128)}), (f32[256,256]{1,0:T(8,128)}, f32[256,65]{0,1:T(8,128)})) %all-reduce.6.cloned.1.call-update) | async-done | bytes 328720 | tf_op jit(solution)/shard_map/psum | solution.py:133
  472.9 1.5 multiply_reduce_fusion.5
  475.1 1.6 multiply_reduce_fusion.3
  477.5 1.7 broadcast_divide_fusion
  479.1 1.5 broadcast_divide_fusion.1
  (122 shorter events, 26.6 us)
Async XLA Ops:
  7.2 13.7 %copy-start = (f32[256,256]{1,0:T(8,128)S(1)}, f32[256,256]{1,0:T(8,128)}, u32[]{:S(2)}) copy-start(f32[256,256]{1,0:T(8,128)} %param.18) | copy-start | bytes 786436
  7.2 3.5 copy-start.14
  7.2 3.5 copy-start.13
  7.2 465.7 %all-reduce.6.cloned.1.call-start = ((), (), s32[]{:S(2)}) async-start(), calls=%async_computation | async-start | bytes 671744 | tf_op jit(solution)/shard_map/psum | solution.py:133
  10.7 10.2 %copy-start.15 = (f32[256]{0:T(256)S(1)}, f32[256]{0:T(256)}, u32[]{:S(2)}) copy-start(f32[256]{0:T(256)} %param.19) | copy-start | bytes 3076
  20.9 22.7 %copy-start.1 = (f32[256,12288]{1,0:T(8,128)}, f32[256,12288]{1,0:T(8,128)S(1)}, u32[]{:S(2)}) copy-start(f32[256,12288]{1,0:T(8,128)S(1)} %convolution_add_fusion) | copy-start | bytes 37748740
  20.9 22.7 %copy-start.7 = (f32[256,65]{0,1:T(8,128)S(1)}, f32[256,65]{0,1:T(8,128)}, u32[]{:S(2)}) copy-start(f32[256,65]{0,1:T(8,128)} %param.20) | copy-start | bytes 199684
  20.9 22.7 %copy-start.16 = (f32[65]{0:T(128)S(1)}, f32[65]{0:T(128)}, u32[]{:S(2)}) copy-start(f32[65]{0:T(128)} %param.21) | copy-start | bytes 784
  43.6 18.0 %copy-start.5 = (f32[1,1,3,4096]{3,1,2,0:T(1,128)S(1)}, f32[1,1,3,4096]{3,1,2,0:T(1,128)}, u32[]{:S(2)}) copy-start(f32[1,1,3,4096]{3,1,2,0:T(1,128)} %param.12) | copy-start | bytes 147460
  43.6 18.0 %copy-start.11 = (s32[1,1,4096]{2,1,0:T(1,128)S(1)}, s32[1,1,4096]{2,1,0:T(1,128)}, u32[]{:S(2)}) copy-start(s32[1,1,4096]{2,1,0:T(1,128)} %param.13) | copy-start | bytes 49156
  59.2 1.8 copy-start.2
  61.8 24.1 %collective-permute-start.1 = (f32[8,256]{1,0:T(8,128)S(1)}, f32[8,256]{1,0:T(8,128)}, u32[]{:S(2)}, u32[]{:S(2)}) collective-permute-start(f32[8,256]{1,0:T(8,128)S(1)} %fusion.35), channel_id=1, source_target_pairs={{0,1},{1,0},{2,3},{3,2},{4,5},{5,4},{6,7},{7,6},{8,9},{9,8},{10,11... | collective-permute-start | bytes 24584 | tf_op jit(solution)/shard_map/ppermute | solution.py:13
  85.2 14.5 %collective-permute-start = (f32[64,8,256]{2,1,0:T(8,128)}, f32[64,8,256]{2,1,0:T(8,128)S(1)}, u32[]{:S(2)}, u32[]{:S(2)}) collective-permute-start(f32[64,8,256]{2,1,0:T(8,128)} %fusion.16), channel_id=1, source_target_pairs={{0,1},{1,0},{2,3},{3,2},{4,5},{5,4},{6,7},{7,6},{8,9},{9,8},{10,11... | collective-permute-start | bytes 1572872 | tf_op jit(solution)/shard_map/ppermute | solution.py:13
  86.6 13.0 %collective-permute-start.3 = (f32[4,256]{1,0:T(4,128)S(1)}, f32[4,256]{1,0:T(4,128)S(1)}, u32[]{:S(2)}, u32[]{:S(2)}) collective-permute-start(f32[4,256]{1,0:T(4,128)S(1)} %fusion.38), channel_id=1, source_target_pairs={{0,2},{1,3},{2,0},{3,1},{4,6},{5,7},{6,4},{7,5},{8,10},{9,11},{10,... | collective-permute-start | bytes 12296 | tf_op jit(solution)/shard_map/ppermute | solution.py:13
  100.7 7.5 %collective-permute-start.2 = (f32[64,4,256]{2,0,1:T(8,128)}, f32[64,4,256]{2,0,1:T(8,128)}, u32[]{:S(2)}, u32[]{:S(2)}) collective-permute-start(f32[64,4,256]{2,0,1:T(8,128)} %fusion.18), channel_id=1, source_target_pairs={{0,2},{1,3},{2,0},{3,1},{4,6},{5,7},{6,4},{7,5},{8,10},{9,11},{10,... | collective-permute-start | bytes 786440 | tf_op jit(solution)/shard_map/ppermute | solution.py:13
  102.8 2.7 collective-permute-start.5
  109.2 4.0 collective-permute-start.4
  110.6 5.6 %collective-permute-start.7 = (f32[1,256]{1,0:T(1,128)S(1)}, f32[1,256]{1,0:T(1,128)S(1)}, u32[]{:S(2)}, u32[]{:S(2)}) collective-permute-start(f32[1,256]{1,0:T(1,128)S(1)} %fusion.46), channel_id=1, source_target_pairs={{0,8},{1,9},{2,10},{3,11},{4,12},{5,13},{6,14},{7,15},{8,0},{9,1},... | collective-permute-start | bytes 3080 | tf_op jit(solution)/shard_map/ppermute | solution.py:13
  113.2 5.0 %collective-permute-start.6 = (f32[64,1,256]{2,0,1:T(8,128)S(1)}, f32[64,1,256]{2,0,1:T(8,128)S(1)}, u32[]{:S(2)}, u32[]{:S(2)}) collective-permute-start(f32[64,1,256]{2,0,1:T(8,128)S(1)} %select_bitcast_fusion), channel_id=1, source_target_pairs={{0,8},{1,9},{2,10},{3,11},{4,12},{5,13},{6,14},{7,15},{8,0},{9,1},... | collective-permute-start | bytes 196616 | tf_op jit(solution)/shard_map/ppermute | solution.py:13
  119.2 0.6 copy-start.9
  120.7 4.7 collective-permute-start.9
  123.2 3.9 collective-permute-start.8
  127.1 2.5 collective-permute-start.10
  127.6 4.8 collective-permute-start.11
  136.1 4.0 collective-permute-start.12
  137.1 7.1 %collective-permute-start.13 = (f32[64,4,256]{2,0,1:T(8,128)}, f32[64,4,256]{2,0,1:T(8,128)S(1)}, u32[]{:S(2)}, u32[]{:S(2)}) collective-permute-start(f32[64,4,256]{2,0,1:T(8,128)} %get-tuple-element.27), channel_id=1, source_target_pairs={{0,2},{1,3},{2,0},{3,1},{4,6},{5,7},{6,4},{7,5},{8,10},{9,11},{10,... | collective-permute-start | bytes 786440 | tf_op jit(solution)/shard_map/ppermute | solution.py:13
  144.2 0.7 copy-start.10
  146.6 11.0 %collective-permute-start.15 = (f32[64,8,256]{2,1,0:T(8,128)S(1)}, f32[64,8,256]{2,1,0:T(8,128)S(1)}, u32[]{:S(2)}, u32[]{:S(2)}) collective-permute-start(f32[64,8,256]{2,1,0:T(8,128)S(1)} %get-tuple-element.25), channel_id=1, source_target_pairs={{0,1},{1,0},{2,3},{3,2},{4,5},{5,4},{6,7},{7,6},{8,9},{9,8},{10,11... | collective-permute-start | bytes 1572872 | tf_op jit(solution)/shard_map/ppermute | solution.py:13
  146.7 10.9 %collective-permute-start.14 = (f32[8,256]{1,0:T(8,128)S(1)}, f32[8,256]{1,0:T(8,128)S(1)}, u32[]{:S(2)}, u32[]{:S(2)}) collective-permute-start(f32[8,256]{1,0:T(8,128)S(1)} %get-tuple-element.32), channel_id=1, source_target_pairs={{0,1},{1,0},{2,3},{3,2},{4,5},{5,4},{6,7},{7,6},{8,9},{9,8},{10,11... | collective-permute-start | bytes 24584 | tf_op jit(solution)/shard_map/ppermute | solution.py:13
  167.8 2.0 copy-start.3
  169.6 1.1 copy-start.4
  169.6 1.1 copy-start.6
  169.6 1.1 copy-start.12
  177.8 11.9 %copy-start.8 = (f32[256,65]{0,1:T(8,128)S(1)}, f32[256,65]{0,1:T(8,128)}, u32[]{:S(2)}) copy-start(f32[256,65]{0,1:T(8,128)} %param.20) | copy-start | bytes 199684
  177.8 26.7 %slice-start = ((s8[12582912]{0:T(1024)(128)(4,1)}), s8[4194304]{0:T(1024)(128)(4,1)S(1)}, s32[]{:S(2)}) async-start(s8[12582912]{0:T(1024)(128)(4,1)} %bitcast.208), calls=%async_computation.1 | async-start | bytes 8388608
  177.8 26.7 %slice-start.1 = ((s8[12582912]{0:T(1024)(128)(4,1)}), s8[4194304]{0:T(1024)(128)(4,1)S(1)}, s32[]{:S(2)}) async-start(s8[12582912]{0:T(1024)(128)(4,1)} %bitcast.208), calls=%async_computation.2 | async-start | bytes 8388608
  189.7 14.9 %slice-start.2 = ((s8[12582912]{0:T(1024)(128)(4,1)}), s8[4194304]{0:T(1024)(128)(4,1)S(1)}, s32[]{:S(2)}) async-start(s8[12582912]{0:T(1024)(128)(4,1)} %bitcast.208), calls=%async_computation.3 | async-start | bytes 8388608
Sparse Core Ops, SparseCore 0:
  332.1 140.7 all-reduce.5
where the time goes:
time: 497 us; the launch traced here: 488 us
  waiting for transfers between devices  173 us (35%)
  matrix products  122 us (25%)
  blocking collectives  74.3 us (15%)
  other arithmetic  47 us (9%)
  local copies, waits for them, and re-layouts  27.1 us (5%)
  starting transfers between devices  25.2 us (5%)
  between operations  19.6 us (4%)
    psum x1, waiting for transfers between devices, local(): lax.psum((gradients[0], gradients[1], gradients[2], gradients[3], gradien...  140 us
    dot_general x8, matrix products, project(): lax.dot_general(weight, inputs, (((0,), (0,)), ((), ())), precision=preci...  122 us
    psum x1, blocking collectives, local(): lax.psum((gradients[0], gradients[1], gradients[2], gradients[3], gradien...  74.3 us
    ppermute x16, waiting for transfers between devices, partner(): return lax.ppermute(value, axis, pairs)  32.3 us
    ppermute x16, starting transfers between devices, partner(): return lax.ppermute(value, axis, pairs)  25.2 us
    unnamed x46, local copies, waits for them, and re-layouts  11.6 us
  transfers between devices with their start and end apart: 17, of which 11 were waited for; matrix products, arithmetic and copies ran while one was open for 6% of the time, Pallas kernels for 0%

commit v1 on v0

v1 whole, which is shorter than its diff:
```python
import functools

import jax
import jax.numpy as jnp
from jax import lax
from jax.experimental import pallas as pl
from jax.experimental.pallas import tpu as pltpu
from jax.sharding import PartitionSpec as P

epsilon = 1e-05
f32 = jnp.float32
bf16 = jnp.bfloat16
FEAT, HIDDEN, CHANNELS, SAMPLES = 32, 256, 64, 3
OUT_ROWS = 80
ONES = 16


def split(value):
    high = value.astype(bf16)
    return high, (value - high.astype(f32)).astype(bf16)


def dot(left, right):
    return lax.dot_general(left, right, (((1,), (0,)), ((), ())), preferred_element_type=f32)


def dot_columns(left, right):
    return lax.dot_general(left, right, (((1,), (1,)), ((), ())), preferred_element_type=f32)


def sigmoid(value):
    return 0.5 * jnp.tanh(0.5 * value) + 0.5


def step_kernel(
    flip_ref,
    rays_ref,
    target_ref,
    first_t_ref,
    first_bias_ref,
    second_ref,
    second_t_ref,
    second_bias_ref,
    last_ref,
    last_t_ref,
    last_bias_ref,
    pixels_ref,
    grads_ref,
    first_k,
    second_h,
    second_l,
    second_th,
    second_tl,
    last_k,
    last_thl,
    act1_h,
    act1_l,
    act2_h,
    act2_l,
    colors,
    rows,
    misfit_ref,
    grad1,
    grad2,
    grad3,
    bias3,
):
    regions, _, segment = rays_ref.shape
    flip = flip_ref[0]
    columns = SAMPLES * segment

    high, low = split(first_t_ref[...])
    bias_h = first_bias_ref[...].astype(bf16)
    rest = first_bias_ref[...] - bias_h.astype(f32)
    bias_m = rest.astype(bf16)
    bias_l = (rest - bias_m.astype(f32)).astype(bf16)
    pad = jnp.zeros((HIDDEN, ONES - 3), bf16)
    first_k[...] = jnp.concatenate([high, high, low, bias_h, bias_m, bias_l, pad], axis=1)
    high, low = split(second_ref[...])
    second_h[...] = high
    second_l[...] = low
    high, low = split(second_t_ref[...])
    second_th[...] = high
    second_tl[...] = low
    high, low = split(last_ref[...])
    last_k[...] = jnp.concatenate([high, high, low], axis=1)
    high, low = split(last_t_ref[...])
    last_thl[...] = jnp.concatenate([high, low], axis=0)
    grad1[...] = jnp.zeros_like(grad1)
    grad2[...] = jnp.zeros_like(grad2)
    grad3[...] = jnp.zeros_like(grad3)
    bias3[...] = jnp.zeros_like(bias3)
    misfit_ref[...] = jnp.zeros_like(misfit_ref)
    ones = jnp.ones((ONES, columns), bf16)

    def part(value, s):
        return value[:, s * segment : (s + 1) * segment]

    def inputs(d):
        x = jnp.concatenate([rays_ref[d, s * FEAT : (s + 1) * FEAT, :] for s in range(SAMPLES)], axis=1)
        return split(x)

    def forward(position, cum):
        d = jnp.bitwise_xor(position, flip)
        xh, xl = inputs(d)
        a1 = jnp.maximum(dot(first_k[...], jnp.concatenate([xh, xl, xh, ones], axis=0)), 0.0)
        a1h, a1l = split(a1)
        act1_h[d, :HIDDEN] = a1h
        act1_h[d, HIDDEN:] = ones
        act1_l[d] = a1l
        z2 = dot(second_th[...], a1h) + (dot(second_tl[...], a1h) + dot(second_th[...], a1l))
        a2 = jnp.maximum(z2 + second_bias_ref[...], 0.0)
        a2h, a2l = split(a2)
        act2_h[d] = a2h
        act2_l[d] = a2l
        both = dot(last_thl[...], a2h)
        raw = both[:OUT_ROWS] + (both[OUT_ROWS:] + dot(last_thl[:OUT_ROWS], a2l)) + last_bias_ref[...]
        sc = sigmoid(raw[:CHANNELS])
        colors[d] = sc
        t = raw[CHANNELS : CHANNELS + 1]
        density = jnp.maximum(t, 0.0) + jnp.log1p(jnp.exp(-jnp.abs(t)))
        slope = sigmoid(t)
        passed = jnp.exp(-cum)
        before = jnp.ones_like(cum)
        total = jnp.zeros_like(cum)
        color = jnp.zeros((CHANNELS, segment), f32)
        for s in range(SAMPLES):
            length = rays_ref[d, SAMPLES * FEAT + s : SAMPLES * FEAT + s + 1, :]
            optical = part(density, s) * length
            weight = before * (1.0 - jnp.exp(-optical))
            total = total + optical
            before = jnp.exp(-total)
            color = color + weight * part(sc, s)
            rows[d, s : s + 1, :] = weight
            rows[d, SAMPLES + s : SAMPLES + s + 1, :] = before
            rows[d, 2 * SAMPLES + s : 2 * SAMPLES + s + 1, :] = part(slope, s) * length
        rows[d, 9:10, :] = passed
        misfit_ref[...] += passed * color
        return cum + total

    lax.fori_loop(0, regions, forward, jnp.zeros((1, segment), f32))
    pixels = misfit_ref[...]
    pixels_ref[...] = pixels
    misfit_ref[...] = pixels - target_ref[...]

    def backward(step, behind):
        d = jnp.bitwise_xor(regions - 1 - step, flip)
        misfit = misfit_ref[...]
        passed = rows[d, 9:10, :]
        weights = [rows[d, s : s + 1, :] for s in range(SAMPLES)]
        parts, weighted, dots = [], [], []
        for s in range(SAMPLES):
            sc = colors[d, :, s * segment : (s + 1) * segment]
            product = misfit * sc
            value = passed * jnp.sum(product, axis=0, keepdims=True)
            dots.append(value)
            weighted.append(weights[s] * value)
            parts.append((passed * weights[s]) * (product - product * sc))
        later = -behind
        slopes = [None] * SAMPLES
        for s in reversed(range(SAMPLES)):
            after = rows[d, SAMPLES + s : SAMPLES + s + 1, :]
            slopes[s] = (dots[s] * after + later) * rows[d, 2 * SAMPLES + s : 2 * SAMPLES + s + 1, :]
            later = later - weighted[s]
        d3 = jnp.concatenate(
            [
                jnp.concatenate(parts, axis=1),
                jnp.concatenate(slopes, axis=1),
                jnp.zeros((OUT_ROWS - CHANNELS - 1, columns), f32),
            ],
            axis=0,
        )
        bias3[...] += part(d3, 0) + (part(d3, 1) + part(d3, 2))
        d3h, d3l = split(d3)
        a2h = act2_h[d]
        d2 = dot(last_k[...], jnp.concatenate([d3h, d3l, d3h], axis=0))
        d2 = jnp.where(a2h > 0, d2, 0.0)
        d2h, d2l = split(d2)
        both = dot_columns(jnp.concatenate([d3h, d3l], axis=0), a2h)
        grad3[...] += both[:OUT_ROWS] + (both[OUT_ROWS:] + dot_columns(d3h, act2_l[d]))
        a1h = act1_h[d]
        d1 = dot(second_h[...], d2h) + (dot(second_l[...], d2h) + dot(second_h[...], d2l))
        d1 = jnp.where(a1h[:HIDDEN] > 0, d1, 0.0)
        grad2[...] += dot_columns(a1h, d2h) + dot_columns(a1h, d2l)
        grad2[:HIDDEN] += dot_columns(act1_l[d], d2h)
        d1h, d1l = split(d1)
        xh, xl = inputs(d)
        both = dot_columns(jnp.concatenate([xh, ones, xl], axis=0), d1h)
        other = dot_columns(jnp.concatenate([xh, ones], axis=0), d1l)
        grad1[...] += both[: FEAT + ONES] + other
        grad1[:FEAT] += both[FEAT + ONES :]
        return behind + (weighted[0] + (weighted[1] + weighted[2]))

    lax.fori_loop(0, regions, backward, jnp.zeros((1, segment), f32))

    half = HIDDEN // 2
    third = lax.dot_general(
        jnp.ones((8, segment), f32),
        jnp.concatenate([bias3[...], jnp.zeros((half - OUT_ROWS, segment), f32)], axis=0),
        (((1,), (1,)), ((), ())),
        precision=lax.Precision.HIGHEST,
        preferred_element_type=f32,
    )
    grads_ref[...] = jnp.zeros_like(grads_ref)
    for side in range(2):
        lanes = slice(side * half, (side + 1) * half)
        grads_ref[side * 256 : side * 256 + 256] = grad2[:HIDDEN, lanes]
        grads_ref[512 + side * 32 : 544 + side * 32] = grad1[:FEAT, lanes]
        grads_ref[576 + side * 80 : 656 + side * 80] = grad3[:, lanes]
        grads_ref[736 + side * 8 : 737 + side * 8] = grad1[FEAT : FEAT + 1, lanes]
        grads_ref[737 + side * 8 : 738 + side * 8] = grad2[HIDDEN : HIDDEN + 1, lanes]
    grads_ref[738:739] = third[0:1]


def finish_kernel(sums_ref, first_ref, first_b_ref, second_ref, second_b_ref, last_ref, last_b_ref):
    def scale(parts, count):
        squares = sum(jnp.sum(part * part, keepdims=True) for part in parts)
        return 1.0 / jnp.sqrt(squares / count + epsilon)

    def both(start, rows, stride):
        return [sums_ref[start : start + rows, :], sums_ref[start + stride : start + stride + rows, :]]

    parts = both(0, 256, 256)
    second_ref[...] = jnp.concatenate(parts, axis=1) * scale(parts, HIDDEN * HIDDEN)
    parts = both(512, 32, 32)
    first_ref[...] = jnp.concatenate(parts, axis=1) * scale(parts, FEAT * HIDDEN)
    parts = both(576, 80, 80)
    last = jnp.concatenate(parts, axis=1) * scale(parts, HIDDEN * (CHANNELS + 1))
    last = jnp.concatenate([last, jnp.zeros((128 - OUT_ROWS, HIDDEN), f32)], axis=0)
    last_ref[...] = jnp.transpose(last)[:, : CHANNELS + 1]
    parts = both(736, 1, 8)
    first_b_ref[...] = jnp.concatenate(parts, axis=1) * scale(parts, HIDDEN)
    parts = both(737, 1, 8)
    second_b_ref[...] = jnp.concatenate(parts, axis=1) * scale(parts, HIDDEN)
    part = sums_ref[738:739, :]
    last_b_ref[...] = (part * scale([part], CHANNELS + 1))[:, : CHANNELS + 1]


def local(
    features,
    spacing,
    counts,
    depth_rank,
    target,
    first_weight,
    first_bias,
    second_weight,
    second_bias,
    last_weight,
    last_bias,
):
    regions = lax.axis_size("depth")
    devices = regions * lax.axis_size("view")
    rays = features.shape[-1]
    segment = rays // regions
    flip = jnp.bitwise_xor(depth_rank[0, 0], lax.axis_index("depth")).reshape(1)

    sample_ids = jnp.arange(SAMPLES, dtype=jnp.int32)
    length = jnp.where(sample_ids[:, None] < counts[0, 0][None, :], spacing[0, 0], 0.0)
    sent = jnp.concatenate(
        [
            features[0, 0].transpose(1, 0, 2).reshape(SAMPLES * FEAT, rays),
            length,
            jnp.zeros((8 - SAMPLES, rays), f32),
        ],
        axis=0,
    )
    height = sent.shape[0]
    sent = sent.reshape(height, regions, segment).transpose(1, 0, 2)
    got = lax.all_to_all(sent, "depth", 0, 0)

    last_pad = jnp.pad(last_weight, ((0, 0), (0, OUT_ROWS - CHANNELS - 1)))
    columns = SAMPLES * segment
    vmem = pl.BlockSpec(memory_space=pltpu.VMEM)
    pixels, grads = pl.pallas_call(
        step_kernel,
        in_specs=[pl.BlockSpec(memory_space=pltpu.SMEM)] + [vmem] * 10,
        out_specs=[vmem] * 2,
        out_shape=[
            jax.ShapeDtypeStruct((CHANNELS, segment), f32),
            jax.ShapeDtypeStruct((1024, 128), f32),
        ],
        scratch_shapes=[
            pltpu.VMEM((HIDDEN, 3 * FEAT + ONES), bf16),
            pltpu.VMEM((HIDDEN, HIDDEN), bf16),
            pltpu.VMEM((HIDDEN, HIDDEN), bf16),
            pltpu.VMEM((HIDDEN, HIDDEN), bf16),
            pltpu.VMEM((HIDDEN, HIDDEN), bf16),
            pltpu.VMEM((HIDDEN, 3 * OUT_ROWS), bf16),
            pltpu.VMEM((2 * OUT_ROWS, HIDDEN), bf16),
            pltpu.VMEM((regions, HIDDEN + ONES, columns), bf16),
            pltpu.VMEM((regions, HIDDEN, columns), bf16),
            pltpu.VMEM((regions, HIDDEN, columns), bf16),
            pltpu.VMEM((regions, HIDDEN, columns), bf16),
            pltpu.VMEM((regions, CHANNELS, columns), f32),
            pltpu.VMEM((regions, 16, segment), f32),
            pltpu.VMEM((CHANNELS, segment), f32),
            pltpu.VMEM((FEAT + ONES, HIDDEN), f32),
            pltpu.VMEM((HIDDEN + ONES, HIDDEN), f32),
            pltpu.VMEM((OUT_ROWS, HIDDEN), f32),
            pltpu.VMEM((OUT_ROWS, segment), f32),
        ],
        compiler_params=pltpu.CompilerParams(vmem_limit_bytes=52 * 2**20),
        cost_estimate=pl.CostEstimate(
            flops=2 * 17 * 65536 * regions * columns, bytes_accessed=4 * 2**20, transcendentals=0
        ),
    )(
        flip,
        got,
        target[0],
        first_weight.T,
        first_bias[:, None],
        second_weight,
        second_weight.T,
        second_bias[:, None],
        last_pad,
        last_pad.T,
        jnp.pad(last_bias, (0, OUT_ROWS - CHANNELS - 1))[:, None],
    )

    axes = ("view", "depth")
    shares = lax.all_to_all(grads.reshape(devices, 1024 // devices, 128), axes, 0, 0)
    share = jnp.sum(shares, axis=0)
    sums = lax.all_to_all(jnp.broadcast_to(share[None], shares.shape), axes, 0, 0)
    first_u, first_s, second_u, second_s, last_u, last_s = pl.pallas_call(
        finish_kernel,
        in_specs=[vmem],
        out_specs=[vmem] * 6,
        out_shape=[
            jax.ShapeDtypeStruct((FEAT, HIDDEN), f32),
            jax.ShapeDtypeStruct((1, HIDDEN), f32),
            jax.ShapeDtypeStruct((HIDDEN, HIDDEN), f32),
            jax.ShapeDtypeStruct((1, HIDDEN), f32),
            jax.ShapeDtypeStruct((HIDDEN, CHANNELS + 1), f32),
            jax.ShapeDtypeStruct((1, CHANNELS + 1), f32),
        ],
    )(sums.reshape(1024, 128))
    return (pixels[None], first_u, first_s[0], second_u, second_s[0], last_u, last_s[0])


def solution(mesh):
    return jax.shard_map(
        local,
        mesh=mesh,
        in_specs=(
            P("view", "depth", None, None, None),
            P("view", "depth", None, None),
            P("view", "depth", None),
            P("view", "depth"),
            P("view", None, "depth"),
            P(),
            P(),
            P(),
            P(),
            P(),
            P(),
        ),
        out_specs=(P("view", None, "depth"), P(), P(), P(), P(), P(), P()),
        check_vma=False,
    )
```

time: 497 us -> 127 us (0.26); the launches traced: 488 us -> 127 us
  waiting for transfers between devices: 173 us -> 20.6 us
  matrix products: 122 us -> 0 us
  Pallas kernels: 0 us -> 44.6 us
  other arithmetic: 47 us -> 2.41 us
  blocking collectives: 74.3 us -> 42.1 us
  local copies, waits for them, and re-layouts: 27.1 us -> 7.05 us
  between operations: 19.6 us -> 1.49 us
  starting transfers between devices: 25.2 us -> 8.74 us
    psum x1 -> x0, waiting for transfers between devices: 140 us -> none  [local(): lax.psum((gradients[0], gradients[1], gradients[2], gradients[3], gradien...]
    dot_general x8 -> x0, matrix products: 122 us -> none  [project(): lax.dot_general(weight, inputs, (((0,), (0,)), ((), ())), precision=preci...]
    psum x1 -> x0, blocking collectives: 74.3 us -> none  [local(): lax.psum((gradients[0], gradients[1], gradients[2], gradients[3], gradien...]
    pallas_call x0 -> x2, Pallas kernels: none -> 44.6 us  [the longest x1 42.6 us: local(): pl.pallas_call(step_kernel, in_specs=[pl.BlockSpec(memory_space=pltpu.SME...]
    all_to_all x0 -> x2, blocking collectives: none -> 42.1 us  [the longest x1 23.8 us: local(): lax.all_to_all(grads.reshape(devices, 1024 // devices, 128), axes, 0, 0)]
    ppermute x16 -> x0, waiting for transfers between devices: 32.3 us -> none  [partner(): return lax.ppermute(value, axis, pairs)]
    ppermute x16 -> x0, starting transfers between devices: 25.2 us -> none  [partner(): return lax.ppermute(value, axis, pairs)]
    all_to_all x0 -> x1, waiting for transfers between devices: none -> 20.6 us  [local(): got = lax.all_to_all(sent, 'depth', 0, 0)]
  transfers between devices with their start and end apart: 17 -> 1, of which waited for: 11 -> 1; matrix products, arithmetic and copies ran while one was open for 6% -> 1% of each run, Pallas kernels for 0% -> 0%
where the time goes in v1:
time: 127 us
  Pallas kernels  44.6 us (35%)
  blocking collectives  42.1 us (33%)
  waiting for transfers between devices  20.6 us (16%)
  starting transfers between devices  8.74 us (7%)
  local copies, waits for them, and re-layouts  7.05 us (6%)
  other arithmetic  2.41 us (2%)
  between operations  1.49 us (1%)
    pallas_call x1, Pallas kernels, local(): pl.pallas_call(step_kernel, in_specs=[pl.BlockSpec(memory_space=pltpu.SME...  42.6 us
    all_to_all x1, blocking collectives, local(): lax.all_to_all(grads.reshape(devices, 1024 // devices, 128), axes, 0, 0)  23.8 us
    all_to_all x1, waiting for transfers between devices, local(): got = lax.all_to_all(sent, 'depth', 0, 0)  20.6 us
    all_to_all x1, blocking collectives, local(): lax.all_to_all(jnp.broadcast_to(share[None], shares.shape), axes, 0, 0)  18.3 us
    all_to_all x1, starting transfers between devices, local(): got = lax.all_to_all(sent, 'depth', 0, 0)  8.74 us
    unnamed x26, local copies, waits for them, and re-layouts  5.62 us
  transfers between devices with their start and end apart: 1, of which 1 were waited for; matrix products, arithmetic and copies ran while one was open for 1% of the time, Pallas kernels for 0%

profile of v1, /device:TPU:1, one launch (start us, length us, event | category | flops | bytes accessed | tf_op | source)
XLA Modules:
  0.0 126.9 jit_solution(7064334443345567686)
XLA Ops:
  0.6 1.9 %copy.32 = f32[12,8,16,256]{3,2,1,0:T(8,128)S(1)} copy(f32[12,8,16,256]{3,1,2,0:T(8,128)} %bitcast.33) | data formatting | bytes 3145728
  2.5 0.0 copy-start.6
  2.5 0.0 copy-start.4
  2.5 0.9 copy.24
  3.5 0.5 broadcast.18
  4.0 0.0 copy-done.6
  4.0 0.7 reduce.4
  4.7 0.0 copy-done.4
  4.7 0.1 reduce.1
  4.9 0.1 pad.12.clone
  5.0 1.4 %maximum_bitcast_fusion = f32[16,104,256]{2,1,0:T(8,128)} fusion(f32[3,16,256]{2,0,1:T(4,128)S(1)} %fusion, f32[96,16,256]{2,0,1:T(8,128)S(1)} %copy.24, f32[104]{0:T(128)S(1)} %pad.12.clone), kind=kLoop, calls=%fused_computation | loop fusion | flops 851968 | bytes 3326368 | tf_op jit(solution)/shard_map/transpose | solution.py:269
  6.4 0.0 copy-start
  6.4 0.0 copy-start.3
  6.4 0.0 copy-start.5
  6.4 0.0 copy-start.7
  6.4 0.0 copy-start.8
  6.4 0.0 copy-start.9
  6.4 0.0 copy-start.1
  6.4 8.7 %all-to-all-start = ((f32[16,104,256]{2,1,0:T(8,128)}), f32[16,104,256]{2,1,0:T(8,128)S(1)}, u32[]{:S(2)}, u32[]{:S(2)}) async-start(f32[16,104,256]{2,1,0:T(8,128)} %maximum_bitcast_fusion), calls=%async_computation | async-start | bytes 3407872 | tf_op jit(solution)/shard_map/all_to_all | solution.py:270
  15.2 0.0 copy-done
  15.2 0.1 copy.26
  15.3 0.0 copy-done.3
  15.3 0.1 copy.33
  15.5 0.0 copy-done.5
  15.5 0.1 copy.25
  15.6 0.0 copy-done.7
  15.6 0.1 copy.27.first_bias_ref
  15.7 0.0 copy-done.8
  15.7 0.1 copy.28.second_bias_ref
  15.9 0.0 copy-done.9
  15.9 0.1 copy.30.last_bias_ref
  16.7 20.6 %all-to-all-done.rays_ref = f32[16,104,256]{2,1,0:T(8,128)S(1)} async-done(((f32[16,104,256]{2,1,0:T(8,128)}), f32[16,104,256]{2,1,0:T(8,128)S(1)}, u32[]{:S(2)}, u32[]{:S(2)}) %all-to-all-start) | async-done | bytes 1703968 | tf_op jit(solution)/shard_map/all_to_all | solution.py:270
  37.2 0.0 copy-start.2
  37.2 1.2 copy-done.2
  38.4 0.0 copy-done.1
  38.4 42.6 %shard_map.162 = (f32[64,256]{1,0:T(8,128)}, f32[1024,128]{1,0:T(8,128)S(1)}) custom-call(s32[1]{0:T(128)} %bitcast.1.flip_ref, f32[16,104,256]{2,1,0:T(8,128)} %copy-done.2, f32[64,256]{1,0:T(8,128)S(1)} %bitcast.30, f32[256,32]{1,0:T(8,128)S(1)} %bitcast.29, f32[256,1]{1,0:T(8,128)S(1)} %copy.27.first_bias_ref, f32[256,256]{1,0:T(8,128)S(1)} %copy-done, ...), custom_call_target="tpu_custom_call" | custom-call | flops 27380416512 | bytes 4194304 | tf_op jit(solution)/shard_map/pallas_call | solution.py:275
  81.0 23.8 %all_to_all.15 = f32[128,8,128]{2,1,0:T(8,128)S(1)} all-to-all(f32[128,8,128]{2,1,0:T(8,128)S(1)} %bitcast.27), channel_id=1, replica_groups=mesh['view'=8,'depth'=16] {'view','depth'}, dimensions={0} | all-to-all | bytes 1048576 | tf_op jit(solution)/shard_map/all_to_all | solution.py:322
  104.8 0.1 reduce_sum.9
  105.0 18.3 %all_to_all.16 = f32[128,8,128]{2,1,0:T(8,128)} all-to-all(f32[128,8,128]{2,1,0:T(8,128)S(1)} %broadcast_in_dim.32), channel_id=1, replica_groups=mesh['view'=8,'depth'=16] {'view','depth'}, dimensions={0} | all-to-all | bytes 1048576 | tf_op jit(solution)/shard_map/all_to_all | solution.py:324
  123.2 2.0 %shard_map.163 = (f32[32,256]{1,0:T(8,128)}, f32[1,256]{1,0:T(1,128)}, f32[256,256]{1,0:T(8,128)}, f32[1,256]{1,0:T(1,128)}, f32[256,65]{1,0:T(8,128)}, /*index=5*/f32[1,65]{1,0:T(1,128)}) custom-call(f32[1024,128]{1,0:T(8,128)} %bitcast.32), custom_call_target="tpu_custom_call" | custom-call | tf_op jit(solution)/shard_map/pallas_call | solution.py:325
  125.2 1.6 %copy.31 = f32[256,65]{0,1:T(8,128)} copy(f32[256,65]{1,0:T(8,128)} %get-tuple-element.35) | data formatting | bytes 133120
  (7 shorter events, 0.1 us)
Async XLA Ops:
  2.5 1.5 %copy-start.6 = (s32[1,1,4096]{2,1,0:T(1,128)S(1)}, s32[1,1,4096]{2,1,0:T(1,128)}, u32[]{:S(2)}) copy-start(s32[1,1,4096]{2,1,0:T(1,128)} %param.13) | copy-start | bytes 49156
  2.5 2.2 %copy-start.4 = (f32[1,1,3,4096]{3,1,2,0:T(1,128)S(1)}, f32[1,1,3,4096]{3,1,2,0:T(1,128)}, u32[]{:S(2)}) copy-start(f32[1,1,3,4096]{3,1,2,0:T(1,128)} %param.12) | copy-start | bytes 147460
  6.4 8.8 %copy-start = (f32[256,256]{1,0:T(8,128)S(1)}, f32[256,256]{1,0:T(8,128)}, u32[]{:S(2)}) copy-start(f32[256,256]{1,0:T(8,128)} %second_ref.1) | copy-start | bytes 786436
  6.4 8.9 %copy-start.3 = (f32[256,65]{0,1:T(8,128)S(1)}, f32[256,65]{0,1:T(8,128)}, u32[]{:S(2)}) copy-start(f32[256,65]{0,1:T(8,128)} %param.20) | copy-start | bytes 199684
  6.4 9.1 %copy-start.5 = (f32[32,256]{1,0:T(8,128)S(1)}, f32[32,256]{1,0:T(8,128)}, u32[]{:S(2)}) copy-start(f32[32,256]{1,0:T(8,128)} %param.16) | copy-start | bytes 98308
  6.4 9.2 %copy-start.7 = (f32[256]{0:T(256)S(1)}, f32[256]{0:T(256)}, u32[]{:S(2)}) copy-start(f32[256]{0:T(256)} %param.17) | copy-start | bytes 3076
  6.4 9.3 %copy-start.8 = (f32[256]{0:T(256)S(1)}, f32[256]{0:T(256)}, u32[]{:S(2)}) copy-start(f32[256]{0:T(256)} %param.19) | copy-start | bytes 3076
  6.4 9.5 %copy-start.9 = (f32[65]{0:T(128)S(1)}, f32[65]{0:T(128)}, u32[]{:S(2)}) copy-start(f32[65]{0:T(128)} %param.21) | copy-start | bytes 784
  6.4 32.0 %copy-start.1 = (f32[1,64,256]{2,1,0:T(8,128)S(1)}, f32[1,64,256]{2,1,0:T(8,128)}, u32[]{:S(2)}) copy-start(f32[1,64,256]{2,1,0:T(8,128)} %param.15) | copy-start | bytes 196612
  6.4 30.8 %all-to-all-start = ((f32[16,104,256]{2,1,0:T(8,128)}), f32[16,104,256]{2,1,0:T(8,128)S(1)}, u32[]{:S(2)}, u32[]{:S(2)}) async-start(f32[16,104,256]{2,1,0:T(8,128)} %maximum_bitcast_fusion), calls=%async_computation | async-start | bytes 3407872 | tf_op jit(solution)/shard_map/all_to_all | solution.py:270
  37.2 1.2 copy-start.2

commit v2 on v1

v2 whole, which is shorter than its diff:
```python
import functools

import jax
import jax.numpy as jnp
from jax import lax
from jax.experimental import pallas as pl
from jax.experimental.pallas import tpu as pltpu
from jax.sharding import PartitionSpec as P

epsilon = 1e-05
f32 = jnp.float32
bf16 = jnp.bfloat16
FEAT, HIDDEN, CHANNELS, SAMPLES = 32, 256, 64, 3
OUT = CHANNELS + 1
OUT_ROWS = 80
ONES = 16
HEIGHT = 104
PARTS = 2
TOGETHER = 4
UNROLL = 1
PACKED = 1024


def split(value):
    high = value.astype(bf16)
    return high, (value - high.astype(f32)).astype(bf16)


def dot(left, right):
    return lax.dot_general(left, right, (((1,), (0,)), ((), ())), preferred_element_type=f32)


def dot_columns(left, right):
    return lax.dot_general(left, right, (((1,), (1,)), ((), ())), preferred_element_type=f32)


def sigmoid(value):
    return 0.5 * jnp.tanh(0.5 * value) + 0.5


def send_kernel(features_ref, spacing_ref, counts_ref, *sent_refs):
    regions = sent_refs[0].shape[0]
    parts = len(sent_refs)
    lanes = sent_refs[0].shape[2]
    lengths = [
        jnp.where(counts_ref[...] > s, spacing_ref[s], 0.0) for s in range(SAMPLES)
    ]
    wide = lanes // 128
    for j in range(regions):
        for i, sent_ref in enumerate(sent_refs):
            start = (j * parts + i) * lanes
            sent_ref[j, : SAMPLES * FEAT, :] = features_ref[:, start : start + lanes]
            row = (j * parts + i) * wide
            for k in range(wide):
                sent_ref[j, SAMPLES * FEAT :, k * 128 : (k + 1) * 128] = jnp.concatenate(
                    [v[row + k : row + k + 1] for v in lengths]
                    + [jnp.zeros((HEIGHT - SAMPLES * FEAT - SAMPLES, 128), f32)],
                    axis=0,
                )


def weights_kernel(
    first_ref,
    first_bias_ref,
    second_ref,
    second_bias_ref,
    last_t_ref,
    last_bias_ref,
    first_k,
    second_k,
    second_tk,
    second_b,
    last_k,
    last_thl,
    last_b,
):
    def column(row, size):
        return jnp.transpose(jnp.broadcast_to(row, (8, size)))[:, 0:1]

    high, low = split(jnp.transpose(first_ref[...]))
    bias = column(first_bias_ref[...], HIDDEN)
    bias_h = bias.astype(bf16)
    rest = bias - bias_h.astype(f32)
    bias_m = rest.astype(bf16)
    bias_l = (rest - bias_m.astype(f32)).astype(bf16)
    pad = jnp.zeros((HIDDEN, ONES - 3), bf16)
    first_k[...] = jnp.concatenate([high, high, low, bias_h, bias_m, bias_l, pad], axis=1)
    high, low = split(second_ref[...])
    second_k[...] = jnp.concatenate([high, low, high], axis=1)
    high, low = split(jnp.transpose(second_ref[...]))
    second_tk[...] = jnp.concatenate([high, low, high], axis=1)
    second_b[...] = column(second_bias_ref[...], HIDDEN)
    last_t = jnp.concatenate([last_t_ref[...], jnp.zeros((128 - OUT, HIDDEN), f32)], axis=0)
    high, low = split(last_t[:OUT_ROWS])
    last_thl[...] = jnp.concatenate([high, low], axis=0)
    high, low = split(jnp.transpose(last_t)[:, :OUT_ROWS])
    last_k[...] = jnp.concatenate([high, high, low], axis=1)
    row = jnp.concatenate([last_bias_ref[...], jnp.zeros((1, 128 - OUT), f32)], axis=1)
    last_b[...] = column(row, 128)[:OUT_ROWS]


def step_kernel(first, final, flip_ref, rays_ref, target_ref, *refs):
    first_k, second_k, second_tk, second_b, last_k, last_thl, last_b = refs[:7]
    refs = refs[7:]
    if not first:
        pixels_in, grad1_in, grad2_in, grad3_in, bias3_in = refs[:5]
        refs = refs[5:]
    if final:
        pixels_ref, grads_ref = refs[:2]
        grad1, grad2, grad3, bias3 = refs[2:6]
        refs = refs[6:]
    else:
        pixels_ref, grad1, grad2, grad3, bias3 = refs[:5]
        refs = refs[5:]
    act1_h, act1_l, act2_h, act2_l, colors, rows, misfit_ref = refs
    regions, _, segment = rays_ref.shape
    flip = flip_ref[0]
    pieces = [(g, s) for g in range(TOGETHER) for s in range(SAMPLES)]
    columns = len(pieces) * segment

    if first:
        grad1[...] = jnp.zeros_like(grad1)
        grad2[...] = jnp.zeros_like(grad2)
        grad3[...] = jnp.zeros_like(grad3)
        bias3[...] = jnp.zeros_like(bias3)
    else:
        grad1[...] = grad1_in[...]
        grad2[...] = grad2_in[...]
        grad3[...] = grad3_in[...]
        bias3[...] = bias3_in[...]
    misfit_ref[...] = jnp.zeros_like(misfit_ref)
    ones = jnp.ones((ONES, columns), bf16)

    def part(value, g, s):
        start = (g * SAMPLES + s) * segment
        return value[:, start : start + segment]

    def region(step, g):
        return jnp.bitwise_xor(step * TOGETHER + g, flip)

    def inputs(step):
        x = [rays_ref[region(step, g), s * FEAT : (s + 1) * FEAT, :] for g, s in pieces]
        return split(jnp.concatenate(x, axis=1))

    def forward(step, cum):
        xh, xl = inputs(step)
        a1 = jnp.maximum(dot(first_k[...], jnp.concatenate([xh, xl, xh, ones], axis=0)), 0.0)
        a1h, a1l = split(a1)
        act1_h[step, :HIDDEN] = a1h
        act1_h[step, HIDDEN:] = ones
        act1_l[step] = a1l
        z2 = dot(second_tk[...], jnp.concatenate([a1h, a1h, a1l], axis=0))
        a2h, a2l = split(jnp.maximum(z2 + second_b[...], 0.0))
        act2_h[step] = a2h
        act2_l[step] = a2l
        both = dot(last_thl[...], a2h)
        raw = both[:OUT_ROWS] + (both[OUT_ROWS:] + dot(last_thl[:OUT_ROWS], a2l)) + last_b[...]
        sc = sigmoid(raw[:CHANNELS])
        colors[step] = sc
        t = raw[CHANNELS : CHANNELS + 1]
        density = jnp.maximum(t, 0.0) + jnp.log1p(jnp.exp(-jnp.abs(t)))
        slope = sigmoid(t)
        image = misfit_ref[...]
        for g in range(TOGETHER):
            d = region(step, g)
            passed = jnp.exp(-cum)
            before = jnp.ones_like(cum)
            total = jnp.zeros_like(cum)
            rows[step, g, 9:10, :] = passed
            for s in range(SAMPLES):
                length = rays_ref[d, SAMPLES * FEAT + s : SAMPLES * FEAT + s + 1, :]
                optical = part(density, g, s) * length
                weight = before * (1.0 - jnp.exp(-optical))
                total = total + optical
                before = jnp.exp(-total)
                image = image + (passed * weight) * part(sc, g, s)
                rows[step, g, s : s + 1, :] = weight
                rows[step, g, SAMPLES + s : SAMPLES + s + 1, :] = before
                rows[step, g, 2 * SAMPLES + s : 2 * SAMPLES + s + 1, :] = part(slope, g, s) * length
            cum = cum + total
        misfit_ref[...] = image
        return cum

    steps = regions // TOGETHER
    lax.fori_loop(0, steps, forward, jnp.zeros((1, segment), f32), unroll=UNROLL)
    pixels = misfit_ref[...]
    misfit_ref[...] = pixels - target_ref[...]
    if first:
        pixels_ref[...] = pixels
    else:
        pixels_ref[...] = jnp.concatenate([pixels_in[...], pixels], axis=1)

    def backward(turn, behind):
        step = steps - 1 - turn
        misfit = misfit_ref[...]
        slopes = [None] * len(pieces)
        parts = [None] * len(pieces)
        for g in reversed(range(TOGETHER)):
            passed = rows[step, g, 9:10, :]
            later = -behind
            for s in reversed(range(SAMPLES)):
                i = g * SAMPLES + s
                weight = rows[step, g, s : s + 1, :]
                after = rows[step, g, SAMPLES + s : SAMPLES + s + 1, :]
                sc = colors[step, :, i * segment : (i + 1) * segment]
                product = misfit * sc
                value = passed * jnp.sum(product, axis=0, keepdims=True)
                parts[i] = (passed * weight) * (product - product * sc)
                slopes[i] = (value * after + later) * rows[step, g, 2 * SAMPLES + s : 2 * SAMPLES + s + 1, :]
                later = later - weight * value
            behind = -later
        d3 = jnp.concatenate(
            [
                jnp.concatenate(parts, axis=1),
                jnp.concatenate(slopes, axis=1),
                jnp.zeros((OUT_ROWS - OUT, columns), f32),
            ],
            axis=0,
        )
        bias3[...] += sum(part(d3, g, s) for g, s in pieces)
        d3h, d3l = split(d3)
        a2h = act2_h[step]
        d2 = dot(last_k[...], jnp.concatenate([d3h, d3l, d3h], axis=0))
        d2 = jnp.where(a2h > 0, d2, 0.0)
        d2h, d2l = split(d2)
        both = dot_columns(jnp.concatenate([d3h, d3l], axis=0), a2h)
        grad3[...] += both[:OUT_ROWS] + (both[OUT_ROWS:] + dot_columns(d3h, act2_l[step]))
        a1h = act1_h[step]
        d1 = dot(second_k[...], jnp.concatenate([d2h, d2h, d2l], axis=0))
        d1 = jnp.where(a1h[:HIDDEN] > 0, d1, 0.0)
        grad2[...] += dot_columns(a1h, d2h) + dot_columns(a1h, d2l)
        grad2[:HIDDEN] += dot_columns(act1_l[step], d2h)
        d1h, d1l = split(d1)
        xh, xl = inputs(step)
        both = dot_columns(jnp.concatenate([xh, ones, xl], axis=0), d1h)
        other = dot_columns(jnp.concatenate([xh, ones], axis=0), d1l)
        grad1[...] += both[: FEAT + ONES] + other
        grad1[:FEAT] += both[FEAT + ONES :]
        return behind

    lax.fori_loop(0, steps, backward, jnp.zeros((1, segment), f32), unroll=UNROLL)
    if not final:
        return

    half = HIDDEN // 2
    third = lax.dot_general(
        jnp.ones((8, segment), f32),
        jnp.concatenate([bias3[...], jnp.zeros((half - OUT_ROWS, segment), f32)], axis=0),
        (((1,), (1,)), ((), ())),
        precision=lax.Precision.HIGHEST,
        preferred_element_type=f32,
    )
    for side in range(2):
        lanes = slice(side * half, (side + 1) * half)
        grads_ref[side * 256 : side * 256 + 256] = grad2[:HIDDEN, lanes]
        grads_ref[512 + side * 32 : 544 + side * 32] = grad1[:FEAT, lanes]
        grads_ref[576 + side * 80 : 656 + side * 80] = grad3[:, lanes]
        misc = [grad1[FEAT : FEAT + 1, lanes], grad2[HIDDEN : HIDDEN + 1, lanes], third[0:1]]
        grads_ref[736 + side * 8 : 744 + side * 8] = jnp.concatenate(misc + [jnp.zeros((5, half), f32)], axis=0)
    grads_ref[752:] = jnp.zeros((PACKED - 752, half), f32)


def finish_kernel(sums_ref, first_ref, first_b_ref, second_ref, second_b_ref, last_t_ref, last_b_ref):
    def scale(parts, count):
        squares = sum(jnp.sum(part * part, keepdims=True) for part in parts)
        return 1.0 / jnp.sqrt(squares / count + epsilon)

    def both(start, rows, stride):
        return [sums_ref[start : start + rows, :], sums_ref[start + stride : start + stride + rows, :]]

    parts = both(0, 256, 256)
    second_ref[...] = jnp.concatenate(parts, axis=1) * scale(parts, HIDDEN * HIDDEN)
    parts = both(512, 32, 32)
    first_ref[...] = jnp.concatenate(parts, axis=1) * scale(parts, FEAT * HIDDEN)
    parts = both(576, 80, 80)
    last_t_ref[...] = jnp.concatenate(parts, axis=1)[:OUT] * scale(parts, HIDDEN * OUT)
    parts = both(736, 1, 8)
    first_b_ref[...] = jnp.concatenate(parts, axis=1) * scale(parts, HIDDEN)
    parts = both(737, 1, 8)
    second_b_ref[...] = jnp.concatenate(parts, axis=1) * scale(parts, HIDDEN)
    part = sums_ref[738:739, :]
    last_b_ref[...] = (part * scale([part], OUT))[:, :OUT]


vmem = pl.BlockSpec(memory_space=pltpu.VMEM)


def shaped(*shape, dtype=f32):
    return jax.ShapeDtypeStruct(shape, dtype)


def prepare_weights(first_weight, first_bias, second_weight, second_bias, last_weight, last_bias):
    return pl.pallas_call(
        weights_kernel,
        in_specs=[vmem] * 6,
        out_specs=[vmem] * 7,
        out_shape=[
            shaped(HIDDEN, 3 * FEAT + ONES, dtype=bf16),
            shaped(HIDDEN, 3 * HIDDEN, dtype=bf16),
            shaped(HIDDEN, 3 * HIDDEN, dtype=bf16),
            shaped(HIDDEN, 1),
            shaped(HIDDEN, 3 * OUT_ROWS, dtype=bf16),
            shaped(2 * OUT_ROWS, HIDDEN, dtype=bf16),
            shaped(OUT_ROWS, 1),
        ],
    )(first_weight, first_bias[None], second_weight, second_bias[None], last_weight.T, last_bias[None])


def step(first, final, flip, rays, target, weights, carried):
    regions, _, segment = rays.shape
    columns = TOGETHER * SAMPLES * segment
    steps = regions // TOGETHER
    sums = [
        shaped(FEAT + ONES, HIDDEN),
        shaped(HIDDEN + ONES, HIDDEN),
        shaped(OUT_ROWS, HIDDEN),
        shaped(OUT_ROWS, segment),
    ]
    scratch = [
        pltpu.VMEM((steps, HIDDEN + ONES, columns), bf16),
        pltpu.VMEM((steps, HIDDEN, columns), bf16),
        pltpu.VMEM((steps, HIDDEN, columns), bf16),
        pltpu.VMEM((steps, HIDDEN, columns), bf16),
        pltpu.VMEM((steps, CHANNELS, columns), f32),
        pltpu.VMEM((steps, TOGETHER, 16, segment), f32),
        pltpu.VMEM((CHANNELS, segment), f32),
    ]
    width = segment if first else 2 * segment
    if final:
        out_shape = [shaped(CHANNELS, width), shaped(PACKED, 128)]
        scratch = [pltpu.VMEM(s.shape, f32) for s in sums] + scratch
    else:
        out_shape = [shaped(CHANNELS, width)] + sums
    return pl.pallas_call(
        functools.partial(step_kernel, first, final),
        in_specs=[pl.BlockSpec(memory_space=pltpu.SMEM)] + [vmem] * (2 + len(weights) + len(carried)),
        out_specs=[vmem] * len(out_shape),
        out_shape=out_shape,
        scratch_shapes=scratch,
        compiler_params=pltpu.CompilerParams(vmem_limit_bytes=44 * 2**20),
        cost_estimate=pl.CostEstimate(
            flops=2 * 17 * 65536 * steps * columns, bytes_accessed=4 * 2**20, transcendentals=0
        ),
    )(flip, rays, target, *weights, *carried)


def local(
    features,
    spacing,
    counts,
    depth_rank,
    target,
    first_weight,
    first_bias,
    second_weight,
    second_bias,
    last_weight,
    last_bias,
):
    regions = lax.axis_size("depth")
    devices = regions * lax.axis_size("view")
    rays = features.shape[-1]
    lanes = rays // regions // PARTS
    flip = jnp.bitwise_xor(depth_rank[0, 0], lax.axis_index("depth")).reshape(1)

    sent = pl.pallas_call(
        send_kernel,
        in_specs=[vmem] * 3,
        out_specs=[vmem] * PARTS,
        out_shape=[shaped(regions, HEIGHT, lanes)] * PARTS,
    )(
        features[0, 0].transpose(1, 0, 2).reshape(SAMPLES * FEAT, rays),
        spacing[0, 0].reshape(SAMPLES, rays // 128, 128),
        counts[0, 0].reshape(rays // 128, 128),
    )
    got = [lax.all_to_all(part, "depth", 0, 0) for part in sent]
    weights = prepare_weights(first_weight, first_bias, second_weight, second_bias, last_weight, last_bias)
    carried = []
    for i in range(PARTS):
        goal = target[0, :, i * lanes : (i + 1) * lanes]
        carried = step(i == 0, i == PARTS - 1, flip, got[i], goal, weights, carried)
    pixels, grads = carried

    axes = ("view", "depth")
    shares = lax.all_to_all(grads.reshape(devices, PACKED // devices, 128), axes, 0, 0)
    share = jnp.sum(shares, axis=0)
    sums = lax.all_to_all(jnp.broadcast_to(share[None], shares.shape), axes, 0, 0)
    first_u, first_s, second_u, second_s, last_u, last_s = pl.pallas_call(
        finish_kernel,
        in_specs=[vmem],
        out_specs=[vmem] * 6,
        out_shape=[
            shaped(FEAT, HIDDEN),
            shaped(1, HIDDEN),
            shaped(HIDDEN, HIDDEN),
            shaped(1, HIDDEN),
            shaped(OUT, HIDDEN),
            shaped(1, OUT),
        ],
    )(sums.reshape(PACKED, 128))
    return (pixels[None], first_u, first_s[0], second_u, second_s[0], last_u.T, last_s[0])


def solution(mesh):
    return jax.shard_map(
        local,
        mesh=mesh,
        in_specs=(
            P("view", "depth", None, None, None),
            P("view", "depth", None, None),
            P("view", "depth", None),
            P("view", "depth"),
            P("view", None, "depth"),
            P(),
            P(),
            P(),
            P(),
            P(),
            P(),
        ),
        out_specs=(P("view", None, "depth"), P(), P(), P(), P(), P(), P()),
        check_vma=False,
    )
```

time: 127 us -> 110 us (0.87)
  waiting for transfers between devices: 20.6 us -> 10.2 us
  local copies, waits for them, and re-layouts: 7.05 us -> 0.09 us
  starting transfers between devices: 8.74 us -> 12.6 us
  Pallas kernels: 44.6 us -> 41.5 us
  other arithmetic: 2.41 us -> 0.14 us
  blocking collectives: 42.1 us -> 43.5 us
    all_to_all x1 -> x2, waiting for transfers between devices: 20.6 us -> 10.2 us  [local(): got = [lax.all_to_all(part, 'depth', 0, 0) for part in sent]]
    unnamed x26 -> x16, local copies, waits for them, and re-layouts: 5.62 us -> 0.04 us
    all_to_all x1 -> x2, starting transfers between devices: 8.74 us -> 12.6 us  [local(): got = [lax.all_to_all(part, 'depth', 0, 0) for part in sent]]
    pallas_call x1 -> x4, Pallas kernels: 42.6 us -> 39.5 us  [the longest x2 34.4 us: step(): pl.pallas_call(functools.partial(step_kernel, first, final), in_specs=[pl...]
    transpose x1 -> x0, other arithmetic: 1.44 us -> none  [local(): sent = sent.reshape(height, regions, segment).transpose(1, 0, 2)]
    all_to_all x1, blocking collectives: 23.8 us -> 25.2 us  [local(): lax.all_to_all(grads.reshape(devices, PACKED // devices, 128), axes, 0, 0)]
  transfers between devices with their start and end apart: 1 -> 2, of which waited for: 1 -> 1; matrix products, arithmetic and copies ran while one was open for 1% -> 0% of each run, Pallas kernels for 0% -> 18%
where the time goes in v2:
time: 110 us; the launch traced here: 109 us
  blocking collectives  43.5 us (40%)
  Pallas kernels  41.5 us (38%)
  starting transfers between devices  12.6 us (11%)
  waiting for transfers between devices  10.2 us (9%)
  between operations  1.45 us (1%)
    pallas_call x2, Pallas kernels, step(): pl.pallas_call(functools.partial(step_kernel, first, final), in_specs=[pl...  34.4 us
    all_to_all x1, blocking collectives, local(): lax.all_to_all(grads.reshape(devices, PACKED // devices, 128), axes, 0, 0)  25.2 us
    all_to_all x1, blocking collectives, local(): lax.all_to_all(jnp.broadcast_to(share[None], shares.shape), axes, 0, 0)  18.3 us
    all_to_all x2, starting transfers between devices, local(): got = [lax.all_to_all(part, 'depth', 0, 0) for part in sent]  12.6 us
    all_to_all x2, waiting for transfers between devices, local(): got = [lax.all_to_all(part, 'depth', 0, 0) for part in sent]  10.2 us
    pallas_call x1, Pallas kernels, local(): pl.pallas_call(send_kernel, in_specs=[vmem] * 3, out_specs=[vmem] * PARTS...  2.77 us
    pallas_call x1, Pallas kernels, prepare_weights(): pl.pallas_call(weights_kernel, in_specs=[vmem] * 6, out_specs=[vmem] * 7,...  2.4 us
  transfers between devices with their start and end apart: 2, of which 1 were waited for; matrix products, arithmetic and copies ran while one was open for 0% of the time, Pallas kernels for 18%

profile of v2, /device:TPU:1, one launch (start us, length us, event | category | flops | bytes accessed | tf_op | source)
XLA Modules:
  0.0 109.5 jit_solution(4174313474631485306)
XLA Ops:
  0.6 0.0 copy-start.7
  0.6 2.8 %shard_map.162 = (f32[16,104,128]{2,1,0:T(8,128)}, f32[16,104,128]{2,1,0:T(8,128)}) custom-call(f32[96,4096]{1,0:T(8,128)} %bitcast.27, f32[3,32,128]{2,1,0:T(8,128)} %bitcast.29, s32[32,128]{1,0:T(8,128)} %bitcast.30), custom_call_target="tpu_custom_call" | custom-call | tf_op jit(solution)/shard_map/pallas_call | solution.py:366
  3.4 8.6 %all-to-all-start.1 = ((f32[16,104,128]{2,1,0:T(8,128)}), f32[16,104,128]{2,1,0:T(8,128)S(1)}, u32[]{:S(2)}, u32[]{:S(2)}) async-start(f32[16,104,128]{2,1,0:T(8,128)} %get-tuple-element.37), calls=%async_computation.1 | async-start | bytes 1703936 | tf_op jit(solution)/shard_map/all_to_all | solution.py:376
  12.7 2.4 %shard_map.163 = (bf16[256,112]{1,0:T(8,128)(2,1)}, bf16[256,768]{1,0:T(8,128)(2,1)}, bf16[256,768]{1,0:T(8,128)(2,1)}, f32[256,1]{1,0:T(8,128)}, bf16[256,240]{...) custom-call(f32[32,256]{1,0:T(8,128)} %first_ref.1, f32[1,256]{1,0:T(1,128)} %bitcast.31, ...), custom_call_target="tpu_custom_call" | custom-call | tf_op jit(solution)/shard_map/pallas_call | solution.py:293
  15.1 0.0 copy-done.7
  15.1 0.0 copy-start
  15.1 0.0 copy-start.1
  15.1 0.0 copy-start.2
  15.1 0.0 copy-start.3
  15.1 0.0 copy-start.4
  15.1 0.0 copy-start.5
  15.1 0.0 copy-start.6
  15.2 10.2 %all-to-all-done.1.rays_ref = f32[16,104,128]{2,1,0:T(8,128)S(1)} async-done(((f32[16,104,128]{2,1,0:T(8,128)}), f32[16,104,128]{2,1,0:T(8,128)S(1)}, u32[]{:S(2)}, u32[]{:S(2)}) %all-to-all-start.1) | async-done | bytes 852000 | tf_op jit(solution)/shard_map/all_to_all | solution.py:376
  25.4 4.0 %all-to-all-start = ((f32[16,104,128]{2,1,0:T(8,128)}), f32[16,104,128]{2,1,0:T(8,128)S(1)}, u32[]{:S(2)}, u32[]{:S(2)}) async-start(f32[16,104,128]{2,1,0:T(8,128)} %get-tuple-element.29), calls=%async_computation | async-start | bytes 1703936 | tf_op jit(solution)/shard_map/all_to_all | solution.py:376
  29.4 0.0 copy-done
  29.4 0.0 copy-done.1
  29.4 0.0 copy-done.2
  29.4 0.0 copy-done.3
  29.4 0.0 copy-done.4
  29.4 0.0 copy-done.5
  29.4 0.0 copy-done.6
  29.4 16.9 %shard_map.164 = (f32[64,128]{1,0:T(8,128)S(1)}, f32[48,256]{1,0:T(8,128)S(1)}, f32[272,256]{1,0:T(8,128)S(1)}, f32[80,256]{1,0:T(8,128)S(1)}, f32[80,128]{1,0:T(8,128)S(1)}) custom-call(s32[1]{0:T(128)} %bitcast.1.flip_ref, f32[16,104,128]{2,1,0:T(8,128)S(1)} %all-to-all-done.1.rays_ref, f32[64,128]{1,0:T(8,128)S(1)} %get-tuple-element.51.target_ref, ...), custom_call_target="tpu_custom_call" | custom-call | flops 13690208256 | bytes 4194304 | tf_op jit(solution)/shard_map/pallas_call | solution.py:334
  46.4 0.0 all-to-all-done.rays_ref
  46.4 17.5 %shard_map.165 = (f32[64,256]{1,0:T(8,128)}, f32[1024,128]{1,0:T(8,128)S(1)}) custom-call(s32[1]{0:T(128)} %bitcast.1.flip_ref, f32[16,104,128]{2,1,0:T(8,128)S(1)} %all-to-all-done.rays_ref, f32[64,128]{1,0:T(8,128)S(1)} %get-tuple-element.52.target_ref, bf16[256,112]{1,0:T(8,128)(2,1)S(1)} %copy-done.5, bf16[256,768]{1,0:T(8,128)(2,1)S(1)} %copy-done, ...), custom_call_target="tpu_custom_call" | custom-call | flops 13690208256 | bytes 4194304 | tf_op jit(solution)/shard_map/pallas_call | solution.py:334
  63.8 25.2 %all_to_all.20 = f32[128,8,128]{2,1,0:T(8,128)S(1)} all-to-all(f32[128,8,128]{2,1,0:T(8,128)S(1)} %bitcast.25), channel_id=1, replica_groups=mesh['view'=8,'depth'=16] {'view','depth'}, dimensions={0} | all-to-all | bytes 1048576 | tf_op jit(solution)/shard_map/all_to_all | solution.py:385
  89.0 0.1 reduce_sum.9
  89.2 18.3 %all_to_all.21 = f32[128,8,128]{2,1,0:T(8,128)} all-to-all(f32[128,8,128]{2,1,0:T(8,128)S(1)} %broadcast_in_dim.22), channel_id=1, replica_groups=mesh['view'=8,'depth'=16] {'view','depth'}, dimensions={0} | all-to-all | bytes 1048576 | tf_op jit(solution)/shard_map/all_to_all | solution.py:387
  107.5 2.0 %shard_map.166 = (f32[32,256]{1,0:T(8,128)}, f32[1,256]{1,0:T(1,128)}, f32[256,256]{1,0:T(8,128)}, f32[1,256]{1,0:T(1,128)}, f32[65,256]{1,0:T(8,128)}, /*index=5*/f32[1,65]{1,0:T(1,128)}) custom-call(f32[1024,128]{1,0:T(8,128)} %bitcast.26), custom_call_target="tpu_custom_call" | custom-call | tf_op jit(solution)/shard_map/pallas_call | solution.py:388
  (2 shorter events, 0.0 us)
Async XLA Ops:
  0.6 14.4 %copy-start.7 = (f32[1,64,256]{2,1,0:T(8,128)S(1)}, f32[1,64,256]{2,1,0:T(8,128)}, u32[]{:S(2)}) copy-start(f32[1,64,256]{2,1,0:T(8,128)} %param.15) | copy-start | bytes 196612
  3.4 22.0 %all-to-all-start.1 = ((f32[16,104,128]{2,1,0:T(8,128)}), f32[16,104,128]{2,1,0:T(8,128)S(1)}, u32[]{:S(2)}, u32[]{:S(2)}) async-start(f32[16,104,128]{2,1,0:T(8,128)} %get-tuple-element.37), calls=%async_computation.1 | async-start | bytes 1703936 | tf_op jit(solution)/shard_map/all_to_all | solution.py:376
  15.1 14.3 %copy-start = (bf16[256,768]{1,0:T(8,128)(2,1)S(1)}, bf16[256,768]{1,0:T(8,128)(2,1)}, u32[]{:S(2)}) copy-start(bf16[256,768]{1,0:T(8,128)(2,1)} %get-tuple-element.31.refs_1_) | copy-start | bytes 1179652
  15.1 14.3 %copy-start.1 = (bf16[256,768]{1,0:T(8,128)(2,1)S(1)}, bf16[256,768]{1,0:T(8,128)(2,1)}, u32[]{:S(2)}) copy-start(bf16[256,768]{1,0:T(8,128)(2,1)} %get-tuple-element.32.refs_2_) | copy-start | bytes 1179652
  15.1 14.3 %copy-start.2 = (f32[256,1]{1,0:T(8,128)S(1)}, f32[256,1]{1,0:T(8,128)}, u32[]{:S(2)}) copy-start(f32[256,1]{1,0:T(8,128)} %get-tuple-element.33.refs_3_) | copy-start | bytes 3076
  15.1 14.3 %copy-start.3 = (bf16[256,240]{1,0:T(8,128)(2,1)S(1)}, bf16[256,240]{1,0:T(8,128)(2,1)}, u32[]{:S(2)}) copy-start(bf16[256,240]{1,0:T(8,128)(2,1)} %get-tuple-element.34.refs_4_) | copy-start | bytes 368644
  15.1 14.3 %copy-start.4 = (bf16[160,256]{1,0:T(8,128)(2,1)S(1)}, bf16[160,256]{1,0:T(8,128)(2,1)}, u32[]{:S(2)}) copy-start(bf16[160,256]{1,0:T(8,128)(2,1)} %get-tuple-element.35.refs_5_) | copy-start | bytes 245764
  15.1 14.3 %copy-start.5 = (bf16[256,112]{1,0:T(8,128)(2,1)S(1)}, bf16[256,112]{1,0:T(8,128)(2,1)}, u32[]{:S(2)}) copy-start(bf16[256,112]{1,0:T(8,128)(2,1)} %get-tuple-element.30.refs_0_) | copy-start | bytes 172036
  15.1 14.3 %copy-start.6 = (f32[80,1]{1,0:T(8,128)S(1)}, f32[80,1]{1,0:T(8,128)}, u32[]{:S(2)}) copy-start(f32[80,1]{1,0:T(8,128)} %get-tuple-element.36.refs_6_) | copy-start | bytes 964
  25.4 21.0 %all-to-all-start = ((f32[16,104,128]{2,1,0:T(8,128)}), f32[16,104,128]{2,1,0:T(8,128)S(1)}, u32[]{:S(2)}, u32[]{:S(2)}) async-start(f32[16,104,128]{2,1,0:T(8,128)} %get-tuple-element.29), calls=%async_computation | async-start | bytes 1703936 | tf_op jit(solution)/shard_map/all_to_all | solution.py:376

commit v3 on v2

--- a/solution.py
+++ b/solution.py
@@ -5,6 +5,7 @@
 from jax import lax
 from jax.experimental import pallas as pl
 from jax.experimental.pallas import tpu as pltpu
+from jax.sharding import Mesh
 from jax.sharding import PartitionSpec as P
 
 epsilon = 1e-05
@@ -18,7 +19,7 @@
 PARTS = 2
 TOGETHER = 4
 UNROLL = 1
-PACKED = 1024
+PACKED = 512
 
 
 def split(value):
@@ -38,25 +39,30 @@
     return 0.5 * jnp.tanh(0.5 * value) + 0.5
 
 
-def send_kernel(features_ref, spacing_ref, counts_ref, *sent_refs):
-    regions = sent_refs[0].shape[0]
-    parts = len(sent_refs)
-    lanes = sent_refs[0].shape[2]
-    lengths = [
-        jnp.where(counts_ref[...] > s, spacing_ref[s], 0.0) for s in range(SAMPLES)
-    ]
+def send_kernel(parts, i, features_ref, spacing_ref, counts_ref, sent_ref, lengths_ref, copies, small):
+    regions, _, lanes = sent_ref.shape
     wide = lanes // 128
+    started = []
     for j in range(regions):
-        for i, sent_ref in enumerate(sent_refs):
-            start = (j * parts + i) * lanes
-            sent_ref[j, : SAMPLES * FEAT, :] = features_ref[:, start : start + lanes]
-            row = (j * parts + i) * wide
-            for k in range(wide):
-                sent_ref[j, SAMPLES * FEAT :, k * 128 : (k + 1) * 128] = jnp.concatenate(
-                    [v[row + k : row + k + 1] for v in lengths]
-                    + [jnp.zeros((HEIGHT - SAMPLES * FEAT - SAMPLES, 128), f32)],
-                    axis=0,
-                )
+        start = (j * parts + i) * lanes
+        copy = pltpu.make_async_copy(
+            features_ref.at[:, start : start + lanes], sent_ref.at[j, : SAMPLES * FEAT, :], copies.at[j]
+        )
+        copy.start()
+        started.append(copy)
+    lengths = [jnp.where(counts_ref[...] > s, spacing_ref[s], 0.0) for s in range(SAMPLES)]
+    for j in range(regions):
+        row = (j * parts + i) * wide
+        for k in range(wide):
+            lengths_ref[j, :, k * 128 : (k + 1) * 128] = jnp.concatenate(
+                [v[row + k : row + k + 1] for v in lengths]
+                + [jnp.zeros((HEIGHT - SAMPLES * FEAT - SAMPLES, 128), f32)],
+                axis=0,
+            )
+    copy = pltpu.make_async_copy(lengths_ref, sent_ref.at[:, SAMPLES * FEAT :, :], small)
+    copy.start()
+    for done in started + [copy]:
+        done.wait()
 
 
 def weights_kernel(
@@ -99,22 +105,22 @@
     last_b[...] = column(row, 128)[:OUT_ROWS]
 
 
-def step_kernel(first, final, flip_ref, rays_ref, target_ref, *refs):
+def step_kernel(first, final, place_ref, rays_ref, target_ref, *refs):
     first_k, second_k, second_tk, second_b, last_k, last_thl, last_b = refs[:7]
     refs = refs[7:]
     if not first:
         pixels_in, grad1_in, grad2_in, grad3_in, bias3_in = refs[:5]
         refs = refs[5:]
     if final:
-        pixels_ref, grads_ref = refs[:2]
-        grad1, grad2, grad3, bias3 = refs[2:6]
-        refs = refs[6:]
+        pixels_ref, keep_ref, send_ref = refs[:3]
+        grad1, grad2, grad3, bias3 = refs[3:7]
+        refs = refs[7:]
     else:
         pixels_ref, grad1, grad2, grad3, bias3 = refs[:5]
         refs = refs[5:]
     act1_h, act1_l, act2_h, act2_l, colors, rows, misfit_ref = refs
     regions, _, segment = rays_ref.shape
-    flip = flip_ref[0]
+    flip = place_ref[0]
     pieces = [(g, s) for g in range(TOGETHER) for s in range(SAMPLES)]
     columns = len(pieces) * segment
 
@@ -250,36 +256,55 @@
         precision=lax.Precision.HIGHEST,
         preferred_element_type=f32,
     )
-    for side in range(2):
-        lanes = slice(side * half, (side + 1) * half)
-        grads_ref[side * 256 : side * 256 + 256] = grad2[:HIDDEN, lanes]
-        grads_ref[512 + side * 32 : 544 + side * 32] = grad1[:FEAT, lanes]
-        grads_ref[576 + side * 80 : 656 + side * 80] = grad3[:, lanes]
-        misc = [grad1[FEAT : FEAT + 1, lanes], grad2[HIDDEN : HIDDEN + 1, lanes], third[0:1]]
-        grads_ref[736 + side * 8 : 744 + side * 8] = jnp.concatenate(misc + [jnp.zeros((5, half), f32)], axis=0)
-    grads_ref[752:] = jnp.zeros((PACKED - 752, half), f32)
-
-
-def finish_kernel(sums_ref, first_ref, first_b_ref, second_ref, second_b_ref, last_t_ref, last_b_ref):
+
+    def pack(hidden_ref, others_ref):
+        for side in range(2):
+            lanes = slice(side * half, (side + 1) * half)
+            hidden_ref[side * 256 : side * 256 + 256] = grad2[:HIDDEN, lanes]
+            others_ref[side * 32 : 32 + side * 32] = grad1[:FEAT, lanes]
+            others_ref[64 + side * 80 : 144 + side * 80] = grad3[:, lanes]
+            misc = [grad1[FEAT : FEAT + 1, lanes], grad2[HIDDEN : HIDDEN + 1, lanes], third[0:1]]
+            others_ref[224 + side * 8 : 232 + side * 8] = jnp.concatenate(misc + [jnp.zeros((5, half), f32)], axis=0)
+        others_ref[240:] = jnp.zeros((PACKED - 240, half), f32)
+
+    @pl.when(place_ref[1] == 0)
+    def _():
+        pack(keep_ref, send_ref)
+
+    @pl.when(place_ref[1] == 1)
+    def _():
+        pack(send_ref, keep_ref)
+
+
+def finish_kernel(place_ref, own_ref, other_ref, first_ref, first_b_ref, second_ref, second_b_ref, last_t_ref, last_b_ref):
     def scale(parts, count):
         squares = sum(jnp.sum(part * part, keepdims=True) for part in parts)
         return 1.0 / jnp.sqrt(squares / count + epsilon)
 
-    def both(start, rows, stride):
-        return [sums_ref[start : start + rows, :], sums_ref[start + stride : start + stride + rows, :]]
-
-    parts = both(0, 256, 256)
-    second_ref[...] = jnp.concatenate(parts, axis=1) * scale(parts, HIDDEN * HIDDEN)
-    parts = both(512, 32, 32)
-    first_ref[...] = jnp.concatenate(parts, axis=1) * scale(parts, FEAT * HIDDEN)
-    parts = both(576, 80, 80)
-    last_t_ref[...] = jnp.concatenate(parts, axis=1)[:OUT] * scale(parts, HIDDEN * OUT)
-    parts = both(736, 1, 8)
-    first_b_ref[...] = jnp.concatenate(parts, axis=1) * scale(parts, HIDDEN)
-    parts = both(737, 1, 8)
-    second_b_ref[...] = jnp.concatenate(parts, axis=1) * scale(parts, HIDDEN)
-    part = sums_ref[738:739, :]
-    last_b_ref[...] = (part * scale([part], OUT))[:, :OUT]
+    def finish(hidden_ref, others_ref):
+        def both(ref, start, rows, stride):
+            return [ref[start : start + rows, :], ref[start + stride : start + stride + rows, :]]
+
+        parts = both(hidden_ref, 0, 256, 256)
+        second_ref[...] = jnp.concatenate(parts, axis=1) * scale(parts, HIDDEN * HIDDEN)
+        parts = both(others_ref, 0, 32, 32)
+        first_ref[...] = jnp.concatenate(parts, axis=1) * scale(parts, FEAT * HIDDEN)
+        parts = both(others_ref, 64, 80, 80)
+        last_t_ref[...] = jnp.concatenate(parts, axis=1)[:OUT] * scale(parts, HIDDEN * OUT)
+        parts = both(others_ref, 224, 1, 8)
+        first_b_ref[...] = jnp.concatenate(parts, axis=1) * scale(parts, HIDDEN)
+        parts = both(others_ref, 225, 1, 8)
+        second_b_ref[...] = jnp.concatenate(parts, axis=1) * scale(parts, HIDDEN)
+        part = others_ref[226:227, :]
+        last_b_ref[...] = (part * scale([part], OUT))[:, :OUT]
+
+    @pl.when(place_ref[1] == 0)
+    def _():
+        finish(own_ref, other_ref)
+
+    @pl.when(place_ref[1] == 1)
+    def _():
+        finish(other_ref, own_ref)
 
 
 vmem = pl.BlockSpec(memory_space=pltpu.VMEM)
@@ -303,10 +328,11 @@
             shaped(2 * OUT_ROWS, HIDDEN, dtype=bf16),
             shaped(OUT_ROWS, 1),
         ],
+        compiler_params=pltpu.CompilerParams(vmem_limit_bytes=8 * 2**20),
     )(first_weight, first_bias[None], second_weight, second_bias[None], last_weight.T, last_bias[None])
 
 
-def step(first, final, flip, rays, target, weights, carried):
+def step(first, final, place, rays, target, weights, carried):
     regions, _, segment = rays.shape
     columns = TOGETHER * SAMPLES * segment
     steps = regions // TOGETHER
@@ -327,7 +353,7 @@
     ]
     width = segment if first else 2 * segment
     if final:
-        out_shape = [shaped(CHANNELS, width), shaped(PACKED, 128)]
+        out_shape = [shaped(CHANNELS, width), shaped(PACKED, 128), shaped(PACKED, 128)]
         scratch = [pltpu.VMEM(s.shape, f32) for s in sums] + scratch
     else:
         out_shape = [shaped(CHANNELS, width)] + sums
@@ -339,9 +365,9 @@
         scratch_shapes=scratch,
         compiler_params=pltpu.CompilerParams(vmem_limit_bytes=44 * 2**20),
         cost_estimate=pl.CostEstimate(
-            flops=2 * 17 * 65536 * steps * columns, bytes_accessed=4 * 2**20, transcendentals=0
+            flops=2 * 17 * 65536 * steps * columns, bytes_accessed=2**20, transcendentals=0
         ),
-    )(flip, rays, target, *weights, *carried)
+    )(place, rays, target, *weights, *carried)
 
 
 def local(
@@ -358,36 +384,47 @@
     last_bias,
 ):
     regions = lax.axis_size("depth")
-    devices = regions * lax.axis_size("view")
+    chips = regions * lax.axis_size("chip")
     rays = features.shape[-1]
     lanes = rays // regions // PARTS
-    flip = jnp.bitwise_xor(depth_rank[0, 0], lax.axis_index("depth")).reshape(1)
-
-    sent = pl.pallas_call(
-        send_kernel,
-        in_specs=[vmem] * 3,
-        out_specs=[vmem] * PARTS,
-        out_shape=[shaped(regions, HEIGHT, lanes)] * PARTS,
-    )(
-        features[0, 0].transpose(1, 0, 2).reshape(SAMPLES * FEAT, rays),
-        spacing[0, 0].reshape(SAMPLES, rays // 128, 128),
-        counts[0, 0].reshape(rays // 128, 128),
-    )
-    got = [lax.all_to_all(part, "depth", 0, 0) for part in sent]
+    place = jnp.stack([jnp.bitwise_xor(depth_rank[0, 0], lax.axis_index("depth")), lax.axis_index("core")])
+
+    got = []
+    for i in range(PARTS):
+        sent = pl.pallas_call(
+            functools.partial(send_kernel, PARTS, i),
+            in_specs=[pl.BlockSpec(memory_space=pl.ANY), vmem, vmem],
+            out_specs=pl.BlockSpec(memory_space=pl.ANY),
+            out_shape=shaped(regions, HEIGHT, lanes),
+            scratch_shapes=[
+                pltpu.VMEM((regions, HEIGHT - SAMPLES * FEAT, lanes), f32),
+                pltpu.SemaphoreType.DMA((regions,)),
+                pltpu.SemaphoreType.DMA,
+            ],
+            cost_estimate=pl.CostEstimate(flops=0, bytes_accessed=2**20, transcendentals=0),
+        )(
+            features[0, 0].transpose(1, 0, 2).reshape(SAMPLES * FEAT, rays),
+            spacing[0, 0].reshape(SAMPLES, rays // 128, 128),
+            counts[0, 0].reshape(rays // 128, 128),
+        )
+        got.append(lax.all_to_all(sent, "depth", 0, 0))
     weights = prepare_weights(first_weight, first_bias, second_weight, second_bias, last_weight, last_bias)
     carried = []
     for i in range(PARTS):
         goal = target[0, :, i * lanes : (i + 1) * lanes]
-        carried = step(i == 0, i == PARTS - 1, flip, got[i], goal, weights, carried)
-    pixels, grads = carried
-
-    axes = ("view", "depth")
-    shares = lax.all_to_all(grads.reshape(devices, PACKED // devices, 128), axes, 0, 0)
+        carried = step(i == 0, i == PARTS - 1, place, got[i], goal, weights, carried)
+    pixels, keep, send = carried
+
+    swap = [(0, 1), (1, 0)]
+    axes = ("chip", "depth")
+    half = keep + lax.ppermute(send, "core", swap)
+    shares = lax.all_to_all(half.reshape(chips, PACKED // chips, 128), axes, 0, 0)
     share = jnp.sum(shares, axis=0)
-    sums = lax.all_to_all(jnp.broadcast_to(share[None], shares.shape), axes, 0, 0)
+    own = lax.all_to_all(jnp.broadcast_to(share[None], shares.shape), axes, 0, 0).reshape(PACKED, 128)
+    other = lax.ppermute(own, "core", swap)
     first_u, first_s, second_u, second_s, last_u, last_s = pl.pallas_call(
         finish_kernel,
-        in_specs=[vmem],
+        in_specs=[pl.BlockSpec(memory_space=pltpu.SMEM), vmem, vmem],
         out_specs=[vmem] * 6,
         out_shape=[
             shaped(FEAT, HIDDEN),
@@ -397,20 +434,25 @@
             shaped(OUT, HIDDEN),
             shaped(1, OUT),
         ],
-    )(sums.reshape(PACKED, 128))
+        compiler_params=pltpu.CompilerParams(vmem_limit_bytes=8 * 2**20),
+    )(place, own, other)
     return (pixels[None], first_u, first_s[0], second_u, second_s[0], last_u.T, last_s[0])
 
 
 def solution(mesh):
+    views, regions = mesh.devices.shape
+    cores = 2
+    mesh = Mesh(mesh.devices.reshape(views // cores, cores, regions), ("chip", "core", "depth"))
+    view = ("chip", "core")
     return jax.shard_map(
         local,
         mesh=mesh,
         in_specs=(
-            P("view", "depth", None, None, None),
-            P("view", "depth", None, None),
-            P("view", "depth", None),
-            P("view", "depth"),
-            P("view", None, "depth"),
+            P(view, "depth", None, None, None),
+            P(view, "depth", None, None),
+            P(view, "depth", None),
+            P(view, "depth"),
+            P(view, None, "depth"),
             P(),
             P(),
             P(),
@@ -418,6 +460,6 @@
             P(),
             P(),
         ),
-        out_specs=(P("view", None, "depth"), P(), P(), P(), P(), P(), P()),
+        out_specs=(P(view, None, "depth"), P(), P(), P(), P(), P(), P()),
         check_vma=False,
     )

time: 110 us -> 149 us (1.35)
  Pallas kernels: 41.5 us -> 91.2 us
  blocking collectives: 43.5 us -> 33.6 us
  waiting for transfers between devices: 10.2 us -> 2.33 us
  starting transfers between devices: 12.6 us -> 19.9 us
    pallas_call x2 -> x3, Pallas kernels: 4.75 us -> 53.4 us  [the longest x2 51.9 us: local(): pl.pallas_call(functools.partial(send_kernel, PARTS, i), in_specs=[pl.Blo...]
    all_to_all x2, waiting for transfers between devices: 10.2 us -> 0.01 us  [local(): got.append(lax.all_to_all(sent, 'depth', 0, 0))]
    all_to_all x1, blocking collectives: 25.2 us -> 19.5 us  [local(): lax.all_to_all(half.reshape(chips, PACKED // chips, 128), axes, 0, 0)]
    ppermute x0 -> x2, starting transfers between devices: none -> 4.59 us  [the longest x1 3.1 us: local(): other = lax.ppermute(own, 'core', swap)]
    all_to_all x1, blocking collectives: 18.3 us -> 14.1 us  [local(): lax.all_to_all(jnp.broadcast_to(share[None], shares.shape), axes, 0, 0)]
    pallas_call x2, Pallas kernels: 34.4 us -> 37.4 us  [step(): pl.pallas_call(functools.partial(step_kernel, first, final), in_specs=[pl...]
    all_to_all x2, starting transfers between devices: 12.6 us -> 15.3 us  [local(): got.append(lax.all_to_all(sent, 'depth', 0, 0))]
    ppermute x0 -> x2, waiting for transfers between devices: none -> 2.32 us  [the longest x1 1.16 us: local(): half = keep + lax.ppermute(send, 'core', swap)]
  transfers between devices with their start and end apart: 2 -> 4, of which waited for: 1 -> 2; matrix products, arithmetic and copies ran while one was open for 0% -> 0% of each run, Pallas kernels for 18% -> 30%
where the time goes in v3:
time: 149 us
  Pallas kernels  91.2 us (61%)
  blocking collectives  33.6 us (23%)
  starting transfers between devices  19.9 us (13%)
  waiting for transfers between devices  2.33 us (2%)
    pallas_call x2, Pallas kernels, local(): pl.pallas_call(functools.partial(send_kernel, PARTS, i), in_specs=[pl.Blo...  51.9 us
    pallas_call x2, Pallas kernels, step(): pl.pallas_call(functools.partial(step_kernel, first, final), in_specs=[pl...  37.4 us
    all_to_all x1, blocking collectives, local(): lax.all_to_all(half.reshape(chips, PACKED // chips, 128), axes, 0, 0)  19.5 us
    all_to_all x2, starting transfers between devices, local(): got.append(lax.all_to_all(sent, 'depth', 0, 0))  15.3 us
    all_to_all x1, blocking collectives, local(): lax.all_to_all(jnp.broadcast_to(share[None], shares.shape), axes, 0, 0)  14.1 us
    ppermute x1, starting transfers between devices, local(): other = lax.ppermute(own, 'core', swap)  3.1 us
  transfers between devices with their start and end apart: 4, of which 2 were waited for; matrix products, arithmetic and copies ran while one was open for 0% of the time, Pallas kernels for 30%

profile of v3, /device:TPU:1, one launch (start us, length us, event | category | flops | bytes accessed | tf_op | source)
XLA Modules:
  0.0 148.7 jit_solution(10447543740238013965)
XLA Ops:
  0.6 25.9 %shard_map.164 = f32[16,104,128]{2,1,0:T(8,128)} custom-call(f32[96,4096]{1,0:T(8,128)} %bitcast.33, f32[3,32,128]{2,1,0:T(8,128)} %bitcast.35, s32[32,128]{1,0:T(8,128)} %bitcast.37), custom_call_target="tpu_custom_call" | custom-call | bytes 1048576 | tf_op jit(solution)/shard_map/pallas_call | solution.py:394
  26.5 8.6 %all-to-all-start.1 = ((f32[16,104,128]{2,1,0:T(8,128)}), f32[16,104,128]{2,1,0:T(8,128)S(1)}, u32[]{:S(2)}, u32[]{:S(2)}) async-start(f32[16,104,128]{2,1,0:T(8,128)} %shard_map.164), calls=%async_computation.1 | async-start | bytes 1703936 | tf_op jit(solution)/shard_map/all_to_all | solution.py:410
  35.1 0.0 copy-start
  35.1 0.0 copy-start.1
  35.2 0.0 copy-start.2
  35.2 0.0 copy-start.3
  35.2 0.0 copy-start.4
  35.2 0.0 copy-start.5
  35.2 0.0 copy-start.6
  35.2 26.0 %shard_map.162 = f32[16,104,128]{2,1,0:T(8,128)} custom-call(f32[96,4096]{1,0:T(8,128)} %bitcast.34, f32[3,32,128]{2,1,0:T(8,128)} %bitcast.36, s32[32,128]{1,0:T(8,128)} %bitcast.38), custom_call_target="tpu_custom_call" | custom-call | bytes 1048576 | tf_op jit(solution)/shard_map/pallas_call | solution.py:394
  61.9 0.0 copy-done
  61.9 0.0 copy-done.1
  61.9 0.0 copy-done.2
  61.9 0.0 copy-done.3
  61.9 0.0 copy-done.4
  61.9 0.0 copy-done.5
  61.9 0.5 shard_map.163
  62.4 0.1 pad_add_fusion.place_ref
  62.5 0.0 copy-done.6
  62.5 0.0 all-to-all-done.1.rays_ref
  62.5 6.7 %all-to-all-start = ((f32[16,104,128]{2,1,0:T(8,128)}), f32[16,104,128]{2,1,0:T(8,128)S(1)}, u32[]{:S(2)}, u32[]{:S(2)}) async-start(f32[16,104,128]{2,1,0:T(8,128)} %shard_map.162), calls=%async_computation | async-start | bytes 1703936 | tf_op jit(solution)/shard_map/all_to_all | solution.py:410
  69.2 18.3 %shard_map.165 = (f32[64,128]{1,0:T(8,128)S(1)}, f32[48,256]{1,0:T(8,128)S(1)}, f32[272,256]{1,0:T(8,128)S(1)}, f32[80,256]{1,0:T(8,128)S(1)}, f32[80,128]{1,0:T(8,128)S(1)}) custom-call(s32[2]{0:T(128)S(1)} %pad_add_fusion.place_ref, f32[16,104,128]{2,1,0:T(8,128)S(1)} %all-to-all-done.1.rays_ref, f32[64,128]{1,0:T(8,128)S(1)} %get-tuple-element.49.target_ref, ...), custom_call_target="tpu_custom_call" | custom-call | flops 13690208256 | bytes 1048576 | tf_op jit(solution)/shard_map/pallas_call | solution.py:360
  87.4 0.0 all-to-all-done.rays_ref
  87.5 19.1 %shard_map.166 = (f32[64,256]{1,0:T(8,128)}, f32[512,128]{1,0:T(8,128)S(1)}, f32[512,128]{1,0:T(8,128)S(1)}) custom-call(s32[2]{0:T(128)S(1)} %pad_add_fusion.place_ref, f32[16,104,128]{2,1,0:T(8,128)S(1)} %all-to-all-done.rays_ref, f32[64,128]{1,0:T(8,128)S(1)} %get-tuple-element.50.target_ref, bf16[256,112]{1,0:T(8,128)(2,1)S(1)} %get-tuple-element.28.refs_0_, ...), custom_call_target="tpu_custom_call" | custom-call | flops 13690208256 | bytes 1048576 | tf_op jit(solution)/shard_map/pallas_call | solution.py:360
  106.6 1.5 %collective-permute-start = (f32[512,128]{1,0:T(8,128)S(1)}, f32[512,128]{1,0:T(8,128)S(1)}, u32[]{:S(2)}, u32[]{:S(2)}) collective-permute-start(f32[512,128]{1,0:T(8,128)S(1)} %get-tuple-element.42), channel_id=1, source_target_pairs={{0,16},{16,0},{1,17},{17,1},{2,18},{18,2},{3,19},{19,3},{4,20},{20... | collective-permute-start | bytes 786440 | tf_op jit(solution)/shard_map/ppermute | solution.py:420
  108.1 1.2 collective-permute-done
  109.3 19.5 %all_to_all.20 = f32[64,8,128]{2,1,0:T(8,128)S(1)} all-to-all(f32[64,8,128]{2,1,0:T(8,128)S(1)} %add_bitcast_fusion), channel_id=1, replica_groups=mesh['chip'=4,'core'=2,'depth'=16] {'chip','depth'}, dimensions={0} | all-to-all | bytes 524288 | tf_op jit(solution)/shard_map/all_to_all | solution.py:421
  128.8 0.1 reduce_sum.9
  128.9 14.1 %all_to_all.21 = f32[64,8,128]{2,1,0:T(8,128)S(1)} all-to-all(f32[64,8,128]{2,1,0:T(8,128)S(1)} %broadcast_in_dim.22), channel_id=1, replica_groups=mesh['chip'=4,'core'=2,'depth'=16] {'chip','depth'}, dimensions={0} | all-to-all | bytes 524288 | tf_op jit(solution)/shard_map/all_to_all | solution.py:423
  143.0 3.1 %collective-permute-start.1 = (f32[512,128]{1,0:T(8,128)S(1)}, f32[512,128]{1,0:T(8,128)S(1)}, u32[]{:S(2)}, u32[]{:S(2)}) collective-permute-start(f32[512,128]{1,0:T(8,128)S(1)} %bitcast.27), channel_id=1, source_target_pairs={{0,16},{16,0},{1,17},{17,1},{2,18},{18,2},{3,19},{19,3},{4,20},{20... | collective-permute-start | bytes 786440 | tf_op jit(solution)/shard_map/ppermute | solution.py:424
  146.1 1.2 collective-permute-done.1.other_ref
  147.2 1.5 %shard_map.167 = (f32[32,256]{1,0:T(8,128)}, f32[1,256]{1,0:T(1,128)}, f32[256,256]{1,0:T(8,128)}, f32[1,256]{1,0:T(1,128)}, f32[65,256]{1,0:T(8,128)}, /*index=5*/f32[1,65]{1,0:T(1,128)}) custom-call(s32[2]{0:T(128)S(1)} %pad_add_fusion.place_ref, f32[512,128]{1,0:T(8,128)S(1)} %bitcast.28, f32[512,128]{1,0:T(8,128)S(1)} %collective-permute-done.1.other_ref), custom_call_target="tpu_custom_call" | custom-call | tf_op jit(solution)/shard_map/pallas_call | solution.py:425
  (3 shorter events, 0.1 us)
Async XLA Ops:
  26.5 36.0 %all-to-all-start.1 = ((f32[16,104,128]{2,1,0:T(8,128)}), f32[16,104,128]{2,1,0:T(8,128)S(1)}, u32[]{:S(2)}, u32[]{:S(2)}) async-start(f32[16,104,128]{2,1,0:T(8,128)} %shard_map.164), calls=%async_computation.1 | async-start | bytes 1703936 | tf_op jit(solution)/shard_map/all_to_all | solution.py:410
  35.1 26.8 %copy-start = (f32[256,256]{1,0:T(8,128)S(1)}, f32[256,256]{1,0:T(8,128)}, u32[]{:S(2)}) copy-start(f32[256,256]{1,0:T(8,128)} %second_ref.1) | copy-start | bytes 786436
  35.1 26.7 %copy-start.1 = (f32[256,65]{0,1:T(8,128)S(1)}, f32[256,65]{0,1:T(8,128)}, u32[]{:S(2)}) copy-start(f32[256,65]{0,1:T(8,128)} %param.20) | copy-start | bytes 199684
  35.2 26.7 %copy-start.2 = (f32[32,256]{1,0:T(8,128)S(1)}, f32[32,256]{1,0:T(8,128)}, u32[]{:S(2)}) copy-start(f32[32,256]{1,0:T(8,128)} %first_ref.1) | copy-start | bytes 98308
  35.2 26.7 %copy-start.3 = (f32[256]{0:T(256)S(1)}, f32[256]{0:T(256)}, u32[]{:S(2)}) copy-start(f32[256]{0:T(256)} %param.17) | copy-start | bytes 3076
  35.2 26.7 %copy-start.4 = (f32[256]{0:T(256)S(1)}, f32[256]{0:T(256)}, u32[]{:S(2)}) copy-start(f32[256]{0:T(256)} %param.19) | copy-start | bytes 3076
  35.2 26.7 %copy-start.5 = (f32[65]{0:T(128)S(1)}, f32[65]{0:T(128)}, u32[]{:S(2)}) copy-start(f32[65]{0:T(128)} %param.21) | copy-start | bytes 784
  35.2 27.3 %copy-start.6 = (f32[1,64,256]{2,1,0:T(8,128)S(1)}, f32[1,64,256]{2,1,0:T(8,128)}, u32[]{:S(2)}) copy-start(f32[1,64,256]{2,1,0:T(8,128)} %param.15) | copy-start | bytes 196612
  62.5 24.9 %all-to-all-start = ((f32[16,104,128]{2,1,0:T(8,128)}), f32[16,104,128]{2,1,0:T(8,128)S(1)}, u32[]{:S(2)}, u32[]{:S(2)}) async-start(f32[16,104,128]{2,1,0:T(8,128)} %shard_map.162), calls=%async_computation | async-start | bytes 1703936 | tf_op jit(solution)/shard_map/all_to_all | solution.py:410
  106.6 2.7 %collective-permute-start = (f32[512,128]{1,0:T(8,128)S(1)}, f32[512,128]{1,0:T(8,128)S(1)}, u32[]{:S(2)}, u32[]{:S(2)}) collective-permute-start(f32[512,128]{1,0:T(8,128)S(1)} %get-tuple-element.42), channel_id=1, source_target_pairs={{0,16},{16,0},{1,17},{17,1},{2,18},{18,2},{3,19},{19,3},{4,20},{20... | collective-permute-start | bytes 786440 | tf_op jit(solution)/shard_map/ppermute | solution.py:420
  143.0 4.3 %collective-permute-start.1 = (f32[512,128]{1,0:T(8,128)S(1)}, f32[512,128]{1,0:T(8,128)S(1)}, u32[]{:S(2)}, u32[]{:S(2)}) collective-permute-start(f32[512,128]{1,0:T(8,128)S(1)} %bitcast.27), channel_id=1, source_target_pairs={{0,16},{16,0},{1,17},{17,1},{2,18},{18,2},{3,19},{19,3},{4,20},{20... | collective-permute-start | bytes 786440 | tf_op jit(solution)/shard_map/ppermute | solution.py:424

commit v4 on v3

--- a/solution.py
+++ b/solution.py
@@ -39,7 +39,7 @@
     return 0.5 * jnp.tanh(0.5 * value) + 0.5
 
 
-def send_kernel(parts, i, features_ref, spacing_ref, counts_ref, sent_ref, lengths_ref, copies, small):
+def send_kernel(parts, i, features_ref, spacing_ref, counts_ref, sent_ref, copies):
     regions, _, lanes = sent_ref.shape
     wide = lanes // 128
     started = []
@@ -54,15 +54,13 @@
     for j in range(regions):
         row = (j * parts + i) * wide
         for k in range(wide):
-            lengths_ref[j, :, k * 128 : (k + 1) * 128] = jnp.concatenate(
+            sent_ref[j, SAMPLES * FEAT :, k * 128 : (k + 1) * 128] = jnp.concatenate(
                 [v[row + k : row + k + 1] for v in lengths]
                 + [jnp.zeros((HEIGHT - SAMPLES * FEAT - SAMPLES, 128), f32)],
                 axis=0,
             )
-    copy = pltpu.make_async_copy(lengths_ref, sent_ref.at[:, SAMPLES * FEAT :, :], small)
-    copy.start()
-    for done in started + [copy]:
-        done.wait()
+    for copy in started:
+        copy.wait()
 
 
 def weights_kernel(
@@ -394,13 +392,9 @@
         sent = pl.pallas_call(
             functools.partial(send_kernel, PARTS, i),
             in_specs=[pl.BlockSpec(memory_space=pl.ANY), vmem, vmem],
-            out_specs=pl.BlockSpec(memory_space=pl.ANY),
+            out_specs=vmem,
             out_shape=shaped(regions, HEIGHT, lanes),
-            scratch_shapes=[
-                pltpu.VMEM((regions, HEIGHT - SAMPLES * FEAT, lanes), f32),
-                pltpu.SemaphoreType.DMA((regions,)),
-                pltpu.SemaphoreType.DMA,
-            ],
+            scratch_shapes=[pltpu.SemaphoreType.DMA((regions,))],
             cost_estimate=pl.CostEstimate(flops=0, bytes_accessed=2**20, transcendentals=0),
         )(
             features[0, 0].transpose(1, 0, 2).reshape(SAMPLES * FEAT, rays),

time: 149 us -> 111 us (0.74)
  Pallas kernels: 91.2 us -> 45.5 us
  waiting for transfers between devices: 2.33 us -> 11.2 us
  starting transfers between devices: 19.9 us -> 18.1 us
    pallas_call x2, Pallas kernels: 51.9 us -> 6.12 us  [local(): pl.pallas_call(functools.partial(send_kernel, PARTS, i), in_specs=[pl.Blo...]
    all_to_all x2, waiting for transfers between devices: 0.01 us -> 8.93 us  [local(): got.append(lax.all_to_all(sent, 'depth', 0, 0))]
    all_to_all x2, starting transfers between devices: 15.3 us -> 12.6 us  [local(): got.append(lax.all_to_all(sent, 'depth', 0, 0))]
  transfers between devices with their start and end apart: 4 -> 4, of which waited for: 2 -> 3; matrix products, arithmetic and copies ran while one was open for 0% -> 0% of each run, Pallas kernels for 30% -> 20%
where the time goes in v4:
time: 111 us; the launch traced here: 110 us
  Pallas kernels  45.5 us (41%)
  blocking collectives  33.5 us (30%)
  starting transfers between devices  18.1 us (16%)
  waiting for transfers between devices  11.2 us (10%)
  between operations  1.46 us (1%)
    pallas_call x2, Pallas kernels, step(): pl.pallas_call(functools.partial(step_kernel, first, final), in_specs=[pl...  37.4 us
    all_to_all x1, blocking collectives, local(): lax.all_to_all(half.reshape(chips, PACKED // chips, 128), axes, 0, 0)  19.5 us
    all_to_all x1, blocking collectives, local(): lax.all_to_all(jnp.broadcast_to(share[None], shares.shape), axes, 0, 0)  14.1 us
    all_to_all x2, starting transfers between devices, local(): got.append(lax.all_to_all(sent, 'depth', 0, 0))  12.6 us
    all_to_all x2, waiting for transfers between devices, local(): got.append(lax.all_to_all(sent, 'depth', 0, 0))  8.93 us
    pallas_call x2, Pallas kernels, local(): pl.pallas_call(functools.partial(send_kernel, PARTS, i), in_specs=[pl.Blo...  6.12 us
    ppermute x1, starting transfers between devices, local(): other = lax.ppermute(own, 'core', swap)  3.1 us
    ppermute x1, starting transfers between devices, local(): half = keep + lax.ppermute(send, 'core', swap)  2.38 us
  transfers between devices with their start and end apart: 4, of which 3 were waited for; matrix products, arithmetic and copies ran while one was open for 0% of the time, Pallas kernels for 20%

profile of v4, /device:TPU:1, one launch (start us, length us, event | category | flops | bytes accessed | tf_op | source)
XLA Modules:
  0.0 110.0 jit_solution(10107370886030948000)
XLA Ops:
  0.6 3.0 %shard_map.164 = f32[16,104,128]{2,1,0:T(8,128)} custom-call(f32[96,4096]{1,0:T(8,128)} %bitcast.33, f32[3,32,128]{2,1,0:T(8,128)} %bitcast.35, s32[32,128]{1,0:T(8,128)} %bitcast.37), custom_call_target="tpu_custom_call" | custom-call | bytes 1048576 | tf_op jit(solution)/shard_map/pallas_call | solution.py:392
  3.7 8.6 %all-to-all-start.1 = ((f32[16,104,128]{2,1,0:T(8,128)}), f32[16,104,128]{2,1,0:T(8,128)S(1)}, u32[]{:S(2)}, u32[]{:S(2)}) async-start(f32[16,104,128]{2,1,0:T(8,128)} %shard_map.164), calls=%async_computation.1 | async-start | bytes 1703936 | tf_op jit(solution)/shard_map/all_to_all | solution.py:404
  12.3 0.0 copy-start
  12.3 0.0 copy-start.1
  12.3 0.0 copy-start.2
  12.3 0.0 copy-start.3
  12.3 0.0 copy-start.4
  12.3 0.0 copy-start.5
  12.3 0.0 copy-start.6
  12.4 3.1 %shard_map.162 = f32[16,104,128]{2,1,0:T(8,128)} custom-call(f32[96,4096]{1,0:T(8,128)} %bitcast.34, f32[3,32,128]{2,1,0:T(8,128)} %bitcast.36, s32[32,128]{1,0:T(8,128)} %bitcast.38), custom_call_target="tpu_custom_call" | custom-call | bytes 1048576 | tf_op jit(solution)/shard_map/pallas_call | solution.py:392
  16.1 0.0 copy-done
  16.1 0.0 copy-done.1
  16.1 0.0 copy-done.2
  16.2 0.0 copy-done.3
  16.2 0.0 copy-done.4
  16.2 0.0 copy-done.5
  16.2 0.5 shard_map.163
  16.7 0.1 pad_add_fusion.place_ref
  16.7 0.0 copy-done.6
  16.7 8.9 %all-to-all-done.1.rays_ref = f32[16,104,128]{2,1,0:T(8,128)S(1)} async-done(((f32[16,104,128]{2,1,0:T(8,128)}), f32[16,104,128]{2,1,0:T(8,128)S(1)}, u32[]{:S(2)}, u32[]{:S(2)}) %all-to-all-start.1) | async-done | bytes 852000 | tf_op jit(solution)/shard_map/all_to_all | solution.py:404
  25.7 4.0 %all-to-all-start = ((f32[16,104,128]{2,1,0:T(8,128)}), f32[16,104,128]{2,1,0:T(8,128)S(1)}, u32[]{:S(2)}, u32[]{:S(2)}) async-start(f32[16,104,128]{2,1,0:T(8,128)} %shard_map.162), calls=%async_computation | async-start | bytes 1703936 | tf_op jit(solution)/shard_map/all_to_all | solution.py:404
  29.6 18.2 %shard_map.165 = (f32[64,128]{1,0:T(8,128)S(1)}, f32[48,256]{1,0:T(8,128)S(1)}, f32[272,256]{1,0:T(8,128)S(1)}, f32[80,256]{1,0:T(8,128)S(1)}, f32[80,128]{1,0:T(8,128)S(1)}) custom-call(s32[2]{0:T(128)S(1)} %pad_add_fusion.place_ref, f32[16,104,128]{2,1,0:T(8,128)S(1)} %all-to-all-done.1.rays_ref, f32[64,128]{1,0:T(8,128)S(1)} %get-tuple-element.49.target_ref, ...), custom_call_target="tpu_custom_call" | custom-call | flops 13690208256 | bytes 1048576 | tf_op jit(solution)/shard_map/pallas_call | solution.py:358
  47.9 0.0 all-to-all-done.rays_ref
  47.9 19.1 %shard_map.166 = (f32[64,256]{1,0:T(8,128)}, f32[512,128]{1,0:T(8,128)S(1)}, f32[512,128]{1,0:T(8,128)S(1)}) custom-call(s32[2]{0:T(128)S(1)} %pad_add_fusion.place_ref, f32[16,104,128]{2,1,0:T(8,128)S(1)} %all-to-all-done.rays_ref, f32[64,128]{1,0:T(8,128)S(1)} %get-tuple-element.50.target_ref, bf16[256,112]{1,0:T(8,128)(2,1)S(1)} %get-tuple-element.28.refs_0_, ...), custom_call_target="tpu_custom_call" | custom-call | flops 13690208256 | bytes 1048576 | tf_op jit(solution)/shard_map/pallas_call | solution.py:358
  67.0 2.4 %collective-permute-start = (f32[512,128]{1,0:T(8,128)S(1)}, f32[512,128]{1,0:T(8,128)S(1)}, u32[]{:S(2)}, u32[]{:S(2)}) collective-permute-start(f32[512,128]{1,0:T(8,128)S(1)} %get-tuple-element.42), channel_id=1, source_target_pairs={{0,16},{16,0},{1,17},{17,1},{2,18},{18,2},{3,19},{19,3},{4,20},{20... | collective-permute-start | bytes 786440 | tf_op jit(solution)/shard_map/ppermute | solution.py:414
  69.4 1.2 %collective-permute-done = f32[512,128]{1,0:T(8,128)S(1)} collective-permute-done((f32[512,128]{1,0:T(8,128)S(1)}, f32[512,128]{1,0:T(8,128)S(1)}, u32[]{:S(2)}, u32[]{:S(2)}) %collective-permute-start) | collective-permute-done | bytes 262176 | tf_op jit(solution)/shard_map/ppermute | solution.py:414
  70.6 19.5 %all_to_all.20 = f32[64,8,128]{2,1,0:T(8,128)S(1)} all-to-all(f32[64,8,128]{2,1,0:T(8,128)S(1)} %add_bitcast_fusion), channel_id=1, replica_groups=mesh['chip'=4,'core'=2,'depth'=16] {'chip','depth'}, dimensions={0} | all-to-all | bytes 524288 | tf_op jit(solution)/shard_map/all_to_all | solution.py:415
  90.1 0.1 reduce_sum.9
  90.2 14.1 %all_to_all.21 = f32[64,8,128]{2,1,0:T(8,128)S(1)} all-to-all(f32[64,8,128]{2,1,0:T(8,128)S(1)} %broadcast_in_dim.22), channel_id=1, replica_groups=mesh['chip'=4,'core'=2,'depth'=16] {'chip','depth'}, dimensions={0} | all-to-all | bytes 524288 | tf_op jit(solution)/shard_map/all_to_all | solution.py:417
  104.2 3.1 %collective-permute-start.1 = (f32[512,128]{1,0:T(8,128)S(1)}, f32[512,128]{1,0:T(8,128)S(1)}, u32[]{:S(2)}, u32[]{:S(2)}) collective-permute-start(f32[512,128]{1,0:T(8,128)S(1)} %bitcast.27), channel_id=1, source_target_pairs={{0,16},{16,0},{1,17},{17,1},{2,18},{18,2},{3,19},{19,3},{4,20},{20... | collective-permute-start | bytes 786440 | tf_op jit(solution)/shard_map/ppermute | solution.py:418
  107.3 1.2 %collective-permute-done.1.other_ref = f32[512,128]{1,0:T(8,128)S(1)} collective-permute-done((f32[512,128]{1,0:T(8,128)S(1)}, f32[512,128]{1,0:T(8,128)S(1)}, u32[]{:S(2)}, u32[]{:S(2)}) %collective-permute-start.1) | collective-permute-done | bytes 262176 | tf_op jit(solution)/shard_map/ppermute | solution.py:418
  108.5 1.5 %shard_map.167 = (f32[32,256]{1,0:T(8,128)}, f32[1,256]{1,0:T(1,128)}, f32[256,256]{1,0:T(8,128)}, f32[1,256]{1,0:T(1,128)}, f32[65,256]{1,0:T(8,128)}, /*index=5*/f32[1,65]{1,0:T(1,128)}) custom-call(s32[2]{0:T(128)S(1)} %pad_add_fusion.place_ref, f32[512,128]{1,0:T(8,128)S(1)} %bitcast.28, f32[512,128]{1,0:T(8,128)S(1)} %collective-permute-done.1.other_ref), custom_call_target="tpu_custom_call" | custom-call | tf_op jit(solution)/shard_map/pallas_call | solution.py:419
  (3 shorter events, 0.1 us)
Async XLA Ops:
  3.7 22.0 %all-to-all-start.1 = ((f32[16,104,128]{2,1,0:T(8,128)}), f32[16,104,128]{2,1,0:T(8,128)S(1)}, u32[]{:S(2)}, u32[]{:S(2)}) async-start(f32[16,104,128]{2,1,0:T(8,128)} %shard_map.164), calls=%async_computation.1 | async-start | bytes 1703936 | tf_op jit(solution)/shard_map/all_to_all | solution.py:404
  12.3 3.9 %copy-start = (f32[256,256]{1,0:T(8,128)S(1)}, f32[256,256]{1,0:T(8,128)}, u32[]{:S(2)}) copy-start(f32[256,256]{1,0:T(8,128)} %second_ref.1) | copy-start | bytes 786436
  12.3 3.9 %copy-start.1 = (f32[256,65]{0,1:T(8,128)S(1)}, f32[256,65]{0,1:T(8,128)}, u32[]{:S(2)}) copy-start(f32[256,65]{0,1:T(8,128)} %param.20) | copy-start | bytes 199684
  12.3 3.9 %copy-start.2 = (f32[32,256]{1,0:T(8,128)S(1)}, f32[32,256]{1,0:T(8,128)}, u32[]{:S(2)}) copy-start(f32[32,256]{1,0:T(8,128)} %first_ref.1) | copy-start | bytes 98308
  12.3 3.8 %copy-start.3 = (f32[256]{0:T(256)S(1)}, f32[256]{0:T(256)}, u32[]{:S(2)}) copy-start(f32[256]{0:T(256)} %param.17) | copy-start | bytes 3076
  12.3 3.8 %copy-start.4 = (f32[256]{0:T(256)S(1)}, f32[256]{0:T(256)}, u32[]{:S(2)}) copy-start(f32[256]{0:T(256)} %param.19) | copy-start | bytes 3076
  12.3 3.8 %copy-start.5 = (f32[65]{0:T(128)S(1)}, f32[65]{0:T(128)}, u32[]{:S(2)}) copy-start(f32[65]{0:T(128)} %param.21) | copy-start | bytes 784
  12.3 4.4 %copy-start.6 = (f32[1,64,256]{2,1,0:T(8,128)S(1)}, f32[1,64,256]{2,1,0:T(8,128)}, u32[]{:S(2)}) copy-start(f32[1,64,256]{2,1,0:T(8,128)} %param.15) | copy-start | bytes 196612
  25.7 22.2 %all-to-all-start = ((f32[16,104,128]{2,1,0:T(8,128)}), f32[16,104,128]{2,1,0:T(8,128)S(1)}, u32[]{:S(2)}, u32[]{:S(2)}) async-start(f32[16,104,128]{2,1,0:T(8,128)} %shard_map.162), calls=%async_computation | async-start | bytes 1703936 | tf_op jit(solution)/shard_map/all_to_all | solution.py:404
  67.0 3.5 %collective-permute-start = (f32[512,128]{1,0:T(8,128)S(1)}, f32[512,128]{1,0:T(8,128)S(1)}, u32[]{:S(2)}, u32[]{:S(2)}) collective-permute-start(f32[512,128]{1,0:T(8,128)S(1)} %get-tuple-element.42), channel_id=1, source_target_pairs={{0,16},{16,0},{1,17},{17,1},{2,18},{18,2},{3,19},{19,3},{4,20},{20... | collective-permute-start | bytes 786440 | tf_op jit(solution)/shard_map/ppermute | solution.py:414
  104.2 4.3 %collective-permute-start.1 = (f32[512,128]{1,0:T(8,128)S(1)}, f32[512,128]{1,0:T(8,128)S(1)}, u32[]{:S(2)}, u32[]{:S(2)}) collective-permute-start(f32[512,128]{1,0:T(8,128)S(1)} %bitcast.27), channel_id=1, source_target_pairs={{0,16},{16,0},{1,17},{17,1},{2,18},{18,2},{3,19},{19,3},{4,20},{20... | collective-permute-start | bytes 786440 | tf_op jit(solution)/shard_map/ppermute | solution.py:418

commit v5 on v4

--- a/solution.py
+++ b/solution.py
@@ -18,7 +18,8 @@
 HEIGHT = 104
 PARTS = 2
 TOGETHER = 4
-UNROLL = 1
+UNROLL = 2
+WIDTH = 512
 PACKED = 512
 
 
@@ -39,19 +40,13 @@
     return 0.5 * jnp.tanh(0.5 * value) + 0.5
 
 
-def send_kernel(parts, i, features_ref, spacing_ref, counts_ref, sent_ref, copies):
+def send_kernel(parts, i, features_ref, spacing_ref, counts_ref, sent_ref):
     regions, _, lanes = sent_ref.shape
     wide = lanes // 128
-    started = []
+    lengths = [jnp.where(counts_ref[...] > s, spacing_ref[s], 0.0) for s in range(SAMPLES)]
     for j in range(regions):
         start = (j * parts + i) * lanes
-        copy = pltpu.make_async_copy(
-            features_ref.at[:, start : start + lanes], sent_ref.at[j, : SAMPLES * FEAT, :], copies.at[j]
-        )
-        copy.start()
-        started.append(copy)
-    lengths = [jnp.where(counts_ref[...] > s, spacing_ref[s], 0.0) for s in range(SAMPLES)]
-    for j in range(regions):
+        sent_ref[j, : SAMPLES * FEAT, :] = features_ref[:, start : start + lanes]
         row = (j * parts + i) * wide
         for k in range(wide):
             sent_ref[j, SAMPLES * FEAT :, k * 128 : (k + 1) * 128] = jnp.concatenate(
@@ -59,8 +54,6 @@
                 + [jnp.zeros((HEIGHT - SAMPLES * FEAT - SAMPLES, 128), f32)],
                 axis=0,
             )
-    for copy in started:
-        copy.wait()
 
 
 def weights_kernel(
@@ -116,7 +109,7 @@
     else:
         pixels_ref, grad1, grad2, grad3, bias3 = refs[:5]
         refs = refs[5:]
-    act1_h, act1_l, act2_h, act2_l, colors, rows, misfit_ref = refs
+    act1_h, act1_l, act2_h, act2_l, colors, rows, misfit_ref, logit, d3_hl, d2_h, d2_l, d1_h, d1_l = refs
     regions, _, segment = rays_ref.shape
     flip = place_ref[0]
     pieces = [(g, s) for g in range(TOGETHER) for s in range(SAMPLES)]
@@ -133,8 +126,6 @@
         grad3[...] = grad3_in[...]
         bias3[...] = bias3_in[...]
     misfit_ref[...] = jnp.zeros_like(misfit_ref)
-    ones = jnp.ones((ONES, columns), bf16)
-
     def part(value, g, s):
         start = (g * SAMPLES + s) * segment
         return value[:, start : start + segment]
@@ -142,26 +133,48 @@
     def region(step, g):
         return jnp.bitwise_xor(step * TOGETHER + g, flip)
 
-    def inputs(step):
-        x = [rays_ref[region(step, g), s * FEAT : (s + 1) * FEAT, :] for g, s in pieces]
+    per = WIDTH // segment
+    tiles = columns // WIDTH
+
+    def inputs(step, tile):
+        x = [
+            rays_ref[region(step, g), s * FEAT : (s + 1) * FEAT, :]
+            for g, s in pieces[tile * per : (tile + 1) * per]
+        ]
         return split(jnp.concatenate(x, axis=1))
 
+    def at(tile):
+        return slice(tile * WIDTH, (tile + 1) * WIDTH)
+
     def forward(step, cum):
-        xh, xl = inputs(step)
-        a1 = jnp.maximum(dot(first_k[...], jnp.concatenate([xh, xl, xh, ones], axis=0)), 0.0)
-        a1h, a1l = split(a1)
-        act1_h[step, :HIDDEN] = a1h
-        act1_h[step, HIDDEN:] = ones
-        act1_l[step] = a1l
-        z2 = dot(second_tk[...], jnp.concatenate([a1h, a1h, a1l], axis=0))
-        a2h, a2l = split(jnp.maximum(z2 + second_b[...], 0.0))
-        act2_h[step] = a2h
-        act2_l[step] = a2l
-        both = dot(last_thl[...], a2h)
-        raw = both[:OUT_ROWS] + (both[OUT_ROWS:] + dot(last_thl[:OUT_ROWS], a2l)) + last_b[...]
-        sc = sigmoid(raw[:CHANNELS])
-        colors[step] = sc
-        t = raw[CHANNELS : CHANNELS + 1]
+        ones = jnp.ones((ONES, WIDTH), bf16)
+
+        def first_layer(tile):
+            xh, xl = inputs(step, tile)
+            a1 = jnp.maximum(dot(first_k[...], jnp.concatenate([xh, xl, xh, ones], axis=0)), 0.0)
+            a1h, a1l = split(a1)
+            act1_h[step, :HIDDEN, at(tile)] = a1h
+            act1_h[step, HIDDEN:, at(tile)] = ones
+            act1_l[step, :, at(tile)] = a1l
+
+        def second_layer(tile):
+            a1h = act1_h[step, :HIDDEN, at(tile)]
+            z2 = dot(second_tk[...], jnp.concatenate([a1h, a1h, act1_l[step, :, at(tile)]], axis=0))
+            a2h, a2l = split(jnp.maximum(z2 + second_b[...], 0.0))
+            act2_h[step, :, at(tile)] = a2h
+            act2_l[step, :, at(tile)] = a2l
+
+        def last_layer(tile):
+            both = dot(last_thl[...], act2_h[step, :, at(tile)])
+            low = dot(last_thl[:OUT_ROWS], act2_l[step, :, at(tile)])
+            raw = both[:OUT_ROWS] + (both[OUT_ROWS:] + low) + last_b[...]
+            colors[step, :, at(tile)] = sigmoid(raw[:CHANNELS])
+            logit[:, at(tile)] = raw[CHANNELS : CHANNELS + 8]
+
+        for stage in (first_layer, second_layer, last_layer):
+            for tile in range(tiles):
+                stage(tile)
+        t = logit[0:1]
         density = jnp.maximum(t, 0.0) + jnp.log1p(jnp.exp(-jnp.abs(t)))
         slope = sigmoid(t)
         image = misfit_ref[...]
@@ -172,12 +185,13 @@
             total = jnp.zeros_like(cum)
             rows[step, g, 9:10, :] = passed
             for s in range(SAMPLES):
+                i = g * SAMPLES + s
                 length = rays_ref[d, SAMPLES * FEAT + s : SAMPLES * FEAT + s + 1, :]
                 optical = part(density, g, s) * length
                 weight = before * (1.0 - jnp.exp(-optical))
                 total = total + optical
                 before = jnp.exp(-total)
-                image = image + (passed * weight) * part(sc, g, s)
+                image = image + (passed * weight) * colors[step, :, i * segment : (i + 1) * segment]
                 rows[step, g, s : s + 1, :] = weight
                 rows[step, g, SAMPLES + s : SAMPLES + s + 1, :] = before
                 rows[step, g, 2 * SAMPLES + s : 2 * SAMPLES + s + 1, :] = part(slope, g, s) * length
@@ -213,33 +227,63 @@
                 slopes[i] = (value * after + later) * rows[step, g, 2 * SAMPLES + s : 2 * SAMPLES + s + 1, :]
                 later = later - weight * value
             behind = -later
-        d3 = jnp.concatenate(
-            [
-                jnp.concatenate(parts, axis=1),
-                jnp.concatenate(slopes, axis=1),
-                jnp.zeros((OUT_ROWS - OUT, columns), f32),
-            ],
-            axis=0,
-        )
-        bias3[...] += sum(part(d3, g, s) for g, s in pieces)
-        d3h, d3l = split(d3)
-        a2h = act2_h[step]
-        d2 = dot(last_k[...], jnp.concatenate([d3h, d3l, d3h], axis=0))
-        d2 = jnp.where(a2h > 0, d2, 0.0)
-        d2h, d2l = split(d2)
-        both = dot_columns(jnp.concatenate([d3h, d3l], axis=0), a2h)
-        grad3[...] += both[:OUT_ROWS] + (both[OUT_ROWS:] + dot_columns(d3h, act2_l[step]))
-        a1h = act1_h[step]
-        d1 = dot(second_k[...], jnp.concatenate([d2h, d2h, d2l], axis=0))
-        d1 = jnp.where(a1h[:HIDDEN] > 0, d1, 0.0)
-        grad2[...] += dot_columns(a1h, d2h) + dot_columns(a1h, d2l)
-        grad2[:HIDDEN] += dot_columns(act1_l[step], d2h)
-        d1h, d1l = split(d1)
-        xh, xl = inputs(step)
-        both = dot_columns(jnp.concatenate([xh, ones, xl], axis=0), d1h)
-        other = dot_columns(jnp.concatenate([xh, ones], axis=0), d1l)
-        grad1[...] += both[: FEAT + ONES] + other
-        grad1[:FEAT] += both[FEAT + ONES :]
+        def output(tile):
+            mine = slice(tile * per, (tile + 1) * per)
+            d3 = jnp.concatenate(
+                [
+                    jnp.concatenate(parts[mine], axis=1),
+                    jnp.concatenate(slopes[mine], axis=1),
+                    jnp.zeros((OUT_ROWS - OUT, WIDTH), f32),
+                ],
+                axis=0,
+            )
+            high, low = split(d3)
+            d3_hl[:OUT_ROWS, at(tile)] = high
+            d3_hl[OUT_ROWS:, at(tile)] = low
+            bias3[...] += sum(d3[:, i * segment : (i + 1) * segment] for i in range(per))
+
+        def last_layer(tile):
+            d3h = d3_hl[:OUT_ROWS, at(tile)]
+            d2 = dot(last_k[...], jnp.concatenate([d3h, d3_hl[OUT_ROWS:, at(tile)], d3h], axis=0))
+            high, low = split(d2)
+            live = act2_h[step, :, at(tile)] > 0
+            d2_h[:, at(tile)] = jnp.where(live, high, jnp.zeros_like(high))
+            d2_l[:, at(tile)] = jnp.where(live, low, jnp.zeros_like(low))
+
+        def second_layer(tile):
+            high = d2_h[:, at(tile)]
+            d1 = dot(second_k[...], jnp.concatenate([high, high, d2_l[:, at(tile)]], axis=0))
+            high, low = split(d1)
+            live = act1_h[step, :HIDDEN, at(tile)] > 0
+            d1_h[:, at(tile)] = jnp.where(live, high, jnp.zeros_like(high))
+            d1_l[:, at(tile)] = jnp.where(live, low, jnp.zeros_like(low))
+
+        def sum_last():
+            both = dot_columns(d3_hl[...], act2_h[step])
+            low = dot_columns(d3_hl[:OUT_ROWS], act2_l[step])
+            grad3[...] += both[:OUT_ROWS] + (both[OUT_ROWS:] + low)
+
+        def sum_second():
+            a1h = act1_h[step]
+            grad2[...] += dot_columns(a1h, d2_h[...]) + dot_columns(a1h, d2_l[...])
+            grad2[:HIDDEN] += dot_columns(act1_l[step], d2_h[...])
+
+        def sum_first():
+            x = [inputs(step, tile) for tile in range(tiles)]
+            xh = jnp.concatenate([h for h, _ in x], axis=1)
+            xl = jnp.concatenate([l for _, l in x], axis=1)
+            ones = jnp.ones((ONES, columns), bf16)
+            both = dot_columns(jnp.concatenate([xh, ones, xl], axis=0), d1_h[...])
+            other = dot_columns(jnp.concatenate([xh, ones], axis=0), d1_l[...])
+            grad1[...] += both[: FEAT + ONES] + other
+            grad1[:FEAT] += both[FEAT + ONES :]
+
+        for stage in (output, last_layer, second_layer):
+            for tile in range(tiles):
+                stage(tile)
+        sum_last()
+        sum_second()
+        sum_first()
         return behind
 
     lax.fori_loop(0, steps, backward, jnp.zeros((1, segment), f32), unroll=UNROLL)
@@ -348,6 +392,12 @@
         pltpu.VMEM((steps, CHANNELS, columns), f32),
         pltpu.VMEM((steps, TOGETHER, 16, segment), f32),
         pltpu.VMEM((CHANNELS, segment), f32),
+        pltpu.VMEM((8, columns), f32),
+        pltpu.VMEM((2 * OUT_ROWS, columns), bf16),
+        pltpu.VMEM((HIDDEN, columns), bf16),
+        pltpu.VMEM((HIDDEN, columns), bf16),
+        pltpu.VMEM((HIDDEN, columns), bf16),
+        pltpu.VMEM((HIDDEN, columns), bf16),
     ]
     width = segment if first else 2 * segment
     if final:
@@ -391,10 +441,9 @@
     for i in range(PARTS):
         sent = pl.pallas_call(
             functools.partial(send_kernel, PARTS, i),
-            in_specs=[pl.BlockSpec(memory_space=pl.ANY), vmem, vmem],
+            in_specs=[vmem] * 3,
             out_specs=vmem,
             out_shape=shaped(regions, HEIGHT, lanes),
-            scratch_shapes=[pltpu.SemaphoreType.DMA((regions,))],
             cost_estimate=pl.CostEstimate(flops=0, bytes_accessed=2**20, transcendentals=0),
         )(
             features[0, 0].transpose(1, 0, 2).reshape(SAMPLES * FEAT, rays),

time: 111 us -> 106 us (0.955)
  Pallas kernels: 45.5 us -> 40.2 us
    pallas_call x2, Pallas kernels: 37.4 us -> 33.3 us  [step(): pl.pallas_call(functools.partial(step_kernel, first, final), in_specs=[pl...]
    pallas_call x2, Pallas kernels: 6.12 us -> 4.98 us  [local(): pl.pallas_call(functools.partial(send_kernel, PARTS, i), in_specs=[vmem]...]
  transfers between devices with their start and end apart: 4 -> 4, of which waited for: 3 -> 3; matrix products, arithmetic and copies ran while one was open for 0% -> 0% of each run, Pallas kernels for 20% -> 18%
where the time goes in v5:
time: 106 us; the launch traced here: 105 us
  Pallas kernels  40.2 us (38%)
  blocking collectives  33.5 us (32%)
  starting transfers between devices  18 us (17%)
  waiting for transfers between devices  11.8 us (11%)
  between operations  1.44 us (1%)
    pallas_call x2, Pallas kernels, step(): pl.pallas_call(functools.partial(step_kernel, first, final), in_specs=[pl...  33.3 us
    all_to_all x1, blocking collectives, local(): lax.all_to_all(half.reshape(chips, PACKED // chips, 128), axes, 0, 0)  19.5 us
    all_to_all x1, blocking collectives, local(): lax.all_to_all(jnp.broadcast_to(share[None], shares.shape), axes, 0, 0)  14.1 us
    all_to_all x2, starting transfers between devices, local(): got.append(lax.all_to_all(sent, 'depth', 0, 0))  12.6 us
    all_to_all x2, waiting for transfers between devices, local(): got.append(lax.all_to_all(sent, 'depth', 0, 0))  9.5 us
    pallas_call x2, Pallas kernels, local(): pl.pallas_call(functools.partial(send_kernel, PARTS, i), in_specs=[vmem]...  4.98 us
    ppermute x1, starting transfers between devices, local(): other = lax.ppermute(own, 'core', swap)  3.1 us
    ppermute x1, starting transfers between devices, local(): half = keep + lax.ppermute(send, 'core', swap)  2.37 us
  transfers between devices with their start and end apart: 4, of which 3 were waited for; matrix products, arithmetic and copies ran while one was open for 0% of the time, Pallas kernels for 18%

profile of v5, /device:TPU:1, one launch (start us, length us, event | category | flops | bytes accessed | tf_op | source)
XLA Modules:
  0.0 105.3 jit_solution(15051246488126621353)
XLA Ops:
  0.6 2.4 %shard_map.164 = f32[16,104,128]{2,1,0:T(8,128)} custom-call(f32[96,4096]{1,0:T(8,128)} %bitcast.33, f32[3,32,128]{2,1,0:T(8,128)} %bitcast.35, s32[32,128]{1,0:T(8,128)} %bitcast.37), custom_call_target="tpu_custom_call" | custom-call | bytes 1048576 | tf_op jit(solution)/shard_map/pallas_call | solution.py:442
  3.1 8.6 %all-to-all-start.1 = ((f32[16,104,128]{2,1,0:T(8,128)}), f32[16,104,128]{2,1,0:T(8,128)S(1)}, u32[]{:S(2)}, u32[]{:S(2)}) async-start(f32[16,104,128]{2,1,0:T(8,128)} %shard_map.164), calls=%async_computation.1 | async-start | bytes 1703936 | tf_op jit(solution)/shard_map/all_to_all | solution.py:453
  11.7 0.0 copy-start
  11.7 0.0 copy-start.1
  11.7 0.0 copy-start.2
  11.7 0.0 copy-start.3
  11.7 0.0 copy-start.4
  11.7 0.0 copy-start.5
  11.8 0.0 copy-start.6
  11.8 2.5 %shard_map.162 = f32[16,104,128]{2,1,0:T(8,128)} custom-call(f32[96,4096]{1,0:T(8,128)} %bitcast.34, f32[3,32,128]{2,1,0:T(8,128)} %bitcast.36, s32[32,128]{1,0:T(8,128)} %bitcast.38), custom_call_target="tpu_custom_call" | custom-call | bytes 1048576 | tf_op jit(solution)/shard_map/pallas_call | solution.py:442
  15.0 0.0 copy-done
  15.0 0.0 copy-done.1
  15.0 0.0 copy-done.2
  15.0 0.0 copy-done.3
  15.0 0.0 copy-done.4
  15.0 0.0 copy-done.5
  15.0 0.5 shard_map.163
  15.5 0.1 pad_add_fusion.place_ref
  15.6 0.0 copy-done.6
  15.6 9.5 %all-to-all-done.1.rays_ref = f32[16,104,128]{2,1,0:T(8,128)S(1)} async-done(((f32[16,104,128]{2,1,0:T(8,128)}), f32[16,104,128]{2,1,0:T(8,128)S(1)}, u32[]{:S(2)}, u32[]{:S(2)}) %all-to-all-start.1) | async-done | bytes 852000 | tf_op jit(solution)/shard_map/all_to_all | solution.py:453
  25.1 4.0 %all-to-all-start = ((f32[16,104,128]{2,1,0:T(8,128)}), f32[16,104,128]{2,1,0:T(8,128)S(1)}, u32[]{:S(2)}, u32[]{:S(2)}) async-start(f32[16,104,128]{2,1,0:T(8,128)} %shard_map.162), calls=%async_computation | async-start | bytes 1703936 | tf_op jit(solution)/shard_map/all_to_all | solution.py:453
  29.0 16.1 %shard_map.165 = (f32[64,128]{1,0:T(8,128)S(1)}, f32[48,256]{1,0:T(8,128)S(1)}, f32[272,256]{1,0:T(8,128)S(1)}, f32[80,256]{1,0:T(8,128)S(1)}, f32[80,128]{1,0:T(8,128)S(1)}) custom-call(s32[2]{0:T(128)S(1)} %pad_add_fusion.place_ref, f32[16,104,128]{2,1,0:T(8,128)S(1)} %all-to-all-done.1.rays_ref, f32[64,128]{1,0:T(8,128)S(1)} %get-tuple-element.49.target_ref, ...), custom_call_target="tpu_custom_call" | custom-call | flops 13690208256 | bytes 1048576 | tf_op jit(solution)/shard_map/pallas_call | solution.py:408
  45.1 0.0 all-to-all-done.rays_ref
  45.1 17.2 %shard_map.166 = (f32[64,256]{1,0:T(8,128)}, f32[512,128]{1,0:T(8,128)S(1)}, f32[512,128]{1,0:T(8,128)S(1)}) custom-call(s32[2]{0:T(128)S(1)} %pad_add_fusion.place_ref, f32[16,104,128]{2,1,0:T(8,128)S(1)} %all-to-all-done.rays_ref, f32[64,128]{1,0:T(8,128)S(1)} %get-tuple-element.50.target_ref, bf16[256,112]{1,0:T(8,128)(2,1)S(1)} %get-tuple-element.28.refs_0_, ...), custom_call_target="tpu_custom_call" | custom-call | flops 13690208256 | bytes 1048576 | tf_op jit(solution)/shard_map/pallas_call | solution.py:408
  62.3 2.4 %collective-permute-start = (f32[512,128]{1,0:T(8,128)S(1)}, f32[512,128]{1,0:T(8,128)S(1)}, u32[]{:S(2)}, u32[]{:S(2)}) collective-permute-start(f32[512,128]{1,0:T(8,128)S(1)} %get-tuple-element.42), channel_id=1, source_target_pairs={{0,16},{16,0},{1,17},{17,1},{2,18},{18,2},{3,19},{19,3},{4,20},{20... | collective-permute-start | bytes 786440 | tf_op jit(solution)/shard_map/ppermute | solution.py:463
  64.7 1.2 %collective-permute-done = f32[512,128]{1,0:T(8,128)S(1)} collective-permute-done((f32[512,128]{1,0:T(8,128)S(1)}, f32[512,128]{1,0:T(8,128)S(1)}, u32[]{:S(2)}, u32[]{:S(2)}) %collective-permute-start) | collective-permute-done | bytes 262176 | tf_op jit(solution)/shard_map/ppermute | solution.py:463
  65.9 19.5 %all_to_all.20 = f32[64,8,128]{2,1,0:T(8,128)S(1)} all-to-all(f32[64,8,128]{2,1,0:T(8,128)S(1)} %add_bitcast_fusion), channel_id=1, replica_groups=mesh['chip'=4,'core'=2,'depth'=16] {'chip','depth'}, dimensions={0} | all-to-all | bytes 524288 | tf_op jit(solution)/shard_map/all_to_all | solution.py:464
  85.4 0.1 reduce_sum.9
  85.5 14.1 %all_to_all.21 = f32[64,8,128]{2,1,0:T(8,128)S(1)} all-to-all(f32[64,8,128]{2,1,0:T(8,128)S(1)} %broadcast_in_dim.22), channel_id=1, replica_groups=mesh['chip'=4,'core'=2,'depth'=16] {'chip','depth'}, dimensions={0} | all-to-all | bytes 524288 | tf_op jit(solution)/shard_map/all_to_all | solution.py:466
  99.5 3.1 %collective-permute-start.1 = (f32[512,128]{1,0:T(8,128)S(1)}, f32[512,128]{1,0:T(8,128)S(1)}, u32[]{:S(2)}, u32[]{:S(2)}) collective-permute-start(f32[512,128]{1,0:T(8,128)S(1)} %bitcast.27), channel_id=1, source_target_pairs={{0,16},{16,0},{1,17},{17,1},{2,18},{18,2},{3,19},{19,3},{4,20},{20... | collective-permute-start | bytes 786440 | tf_op jit(solution)/shard_map/ppermute | solution.py:467
  102.6 1.2 %collective-permute-done.1.other_ref = f32[512,128]{1,0:T(8,128)S(1)} collective-permute-done((f32[512,128]{1,0:T(8,128)S(1)}, f32[512,128]{1,0:T(8,128)S(1)}, u32[]{:S(2)}, u32[]{:S(2)}) %collective-permute-start.1) | collective-permute-done | bytes 262176 | tf_op jit(solution)/shard_map/ppermute | solution.py:467
  103.8 1.5 %shard_map.167 = (f32[32,256]{1,0:T(8,128)}, f32[1,256]{1,0:T(1,128)}, f32[256,256]{1,0:T(8,128)}, f32[1,256]{1,0:T(1,128)}, f32[65,256]{1,0:T(8,128)}, /*index=5*/f32[1,65]{1,0:T(1,128)}) custom-call(s32[2]{0:T(128)S(1)} %pad_add_fusion.place_ref, f32[512,128]{1,0:T(8,128)S(1)} %bitcast.28, f32[512,128]{1,0:T(8,128)S(1)} %collective-permute-done.1.other_ref), custom_call_target="tpu_custom_call" | custom-call | tf_op jit(solution)/shard_map/pallas_call | solution.py:468
  (3 shorter events, 0.1 us)
Async XLA Ops:
  3.1 22.0 %all-to-all-start.1 = ((f32[16,104,128]{2,1,0:T(8,128)}), f32[16,104,128]{2,1,0:T(8,128)S(1)}, u32[]{:S(2)}, u32[]{:S(2)}) async-start(f32[16,104,128]{2,1,0:T(8,128)} %shard_map.164), calls=%async_computation.1 | async-start | bytes 1703936 | tf_op jit(solution)/shard_map/all_to_all | solution.py:453
  11.7 3.3 %copy-start = (f32[256,256]{1,0:T(8,128)S(1)}, f32[256,256]{1,0:T(8,128)}, u32[]{:S(2)}) copy-start(f32[256,256]{1,0:T(8,128)} %second_ref.1) | copy-start | bytes 786436
  11.7 3.3 %copy-start.1 = (f32[256,65]{0,1:T(8,128)S(1)}, f32[256,65]{0,1:T(8,128)}, u32[]{:S(2)}) copy-start(f32[256,65]{0,1:T(8,128)} %param.20) | copy-start | bytes 199684
  11.7 3.3 %copy-start.2 = (f32[32,256]{1,0:T(8,128)S(1)}, f32[32,256]{1,0:T(8,128)}, u32[]{:S(2)}) copy-start(f32[32,256]{1,0:T(8,128)} %first_ref.1) | copy-start | bytes 98308
  11.7 3.3 %copy-start.3 = (f32[256]{0:T(256)S(1)}, f32[256]{0:T(256)}, u32[]{:S(2)}) copy-start(f32[256]{0:T(256)} %param.17) | copy-start | bytes 3076
  11.7 3.3 %copy-start.4 = (f32[256]{0:T(256)S(1)}, f32[256]{0:T(256)}, u32[]{:S(2)}) copy-start(f32[256]{0:T(256)} %param.19) | copy-start | bytes 3076
  11.7 3.3 %copy-start.5 = (f32[65]{0:T(128)S(1)}, f32[65]{0:T(128)}, u32[]{:S(2)}) copy-start(f32[65]{0:T(128)} %param.21) | copy-start | bytes 784
  11.8 3.8 %copy-start.6 = (f32[1,64,256]{2,1,0:T(8,128)S(1)}, f32[1,64,256]{2,1,0:T(8,128)}, u32[]{:S(2)}) copy-start(f32[1,64,256]{2,1,0:T(8,128)} %param.15) | copy-start | bytes 196612
  25.1 20.1 %all-to-all-start = ((f32[16,104,128]{2,1,0:T(8,128)}), f32[16,104,128]{2,1,0:T(8,128)S(1)}, u32[]{:S(2)}, u32[]{:S(2)}) async-start(f32[16,104,128]{2,1,0:T(8,128)} %shard_map.162), calls=%async_computation | async-start | bytes 1703936 | tf_op jit(solution)/shard_map/all_to_all | solution.py:453
  62.3 3.5 %collective-permute-start = (f32[512,128]{1,0:T(8,128)S(1)}, f32[512,128]{1,0:T(8,128)S(1)}, u32[]{:S(2)}, u32[]{:S(2)}) collective-permute-start(f32[512,128]{1,0:T(8,128)S(1)} %get-tuple-element.42), channel_id=1, source_target_pairs={{0,16},{16,0},{1,17},{17,1},{2,18},{18,2},{3,19},{19,3},{4,20},{20... | collective-permute-start | bytes 786440 | tf_op jit(solution)/shard_map/ppermute | solution.py:463
  99.5 4.3 %collective-permute-start.1 = (f32[512,128]{1,0:T(8,128)S(1)}, f32[512,128]{1,0:T(8,128)S(1)}, u32[]{:S(2)}, u32[]{:S(2)}) collective-permute-start(f32[512,128]{1,0:T(8,128)S(1)} %bitcast.27), channel_id=1, source_target_pairs={{0,16},{16,0},{1,17},{17,1},{2,18},{18,2},{3,19},{19,3},{4,20},{20... | collective-permute-start | bytes 786440 | tf_op jit(solution)/shard_map/ppermute | solution.py:467

commit v6 on v5

--- a/solution.py
+++ b/solution.py
@@ -83,7 +83,7 @@
     pad = jnp.zeros((HIDDEN, ONES - 3), bf16)
     first_k[...] = jnp.concatenate([high, high, low, bias_h, bias_m, bias_l, pad], axis=1)
     high, low = split(second_ref[...])
-    second_k[...] = jnp.concatenate([high, low, high], axis=1)
+    second_k[...] = jnp.concatenate([high, low], axis=1)
     high, low = split(jnp.transpose(second_ref[...]))
     second_tk[...] = jnp.concatenate([high, low, high], axis=1)
     second_b[...] = column(second_bias_ref[...], HIDDEN)
@@ -109,7 +109,7 @@
     else:
         pixels_ref, grad1, grad2, grad3, bias3 = refs[:5]
         refs = refs[5:]
-    act1_h, act1_l, act2_h, act2_l, colors, rows, misfit_ref, logit, d3_hl, d2_h, d2_l, d1_h, d1_l = refs
+    act1_h, act1_l, act2_h, act2_l, colors, rows, misfit_ref, logit, d3_hl, d2_h, d1_h = refs
     regions, _, segment = rays_ref.shape
     flip = place_ref[0]
     pieces = [(g, s) for g in range(TOGETHER) for s in range(SAMPLES)]
@@ -244,28 +244,21 @@
 
         def last_layer(tile):
             d3h = d3_hl[:OUT_ROWS, at(tile)]
-            d2 = dot(last_k[...], jnp.concatenate([d3h, d3_hl[OUT_ROWS:, at(tile)], d3h], axis=0))
-            high, low = split(d2)
-            live = act2_h[step, :, at(tile)] > 0
-            d2_h[:, at(tile)] = jnp.where(live, high, jnp.zeros_like(high))
-            d2_l[:, at(tile)] = jnp.where(live, low, jnp.zeros_like(low))
+            d2 = dot(last_k[...], jnp.concatenate([d3h, d3_hl[OUT_ROWS:, at(tile)], d3h], axis=0)).astype(bf16)
+            d2_h[:, at(tile)] = jnp.where(act2_h[step, :, at(tile)] > 0, d2, jnp.zeros_like(d2))
 
         def second_layer(tile):
             high = d2_h[:, at(tile)]
-            d1 = dot(second_k[...], jnp.concatenate([high, high, d2_l[:, at(tile)]], axis=0))
-            high, low = split(d1)
-            live = act1_h[step, :HIDDEN, at(tile)] > 0
-            d1_h[:, at(tile)] = jnp.where(live, high, jnp.zeros_like(high))
-            d1_l[:, at(tile)] = jnp.where(live, low, jnp.zeros_like(low))
+            d1 = dot(second_k[...], jnp.concatenate([high, high], axis=0)).astype(bf16)
+            d1_h[:, at(tile)] = jnp.where(act1_h[step, :HIDDEN, at(tile)] > 0, d1, jnp.zeros_like(d1))
 
         def sum_last():
-            both = dot_columns(d3_hl[...], act2_h[step])
-            low = dot_columns(d3_hl[:OUT_ROWS], act2_l[step])
-            grad3[...] += both[:OUT_ROWS] + (both[OUT_ROWS:] + low)
+            d3h = d3_hl[:OUT_ROWS]
+            grad3[...] += dot_columns(d3h, act2_h[step]) + dot_columns(d3h, act2_l[step])
 
         def sum_second():
             a1h = act1_h[step]
-            grad2[...] += dot_columns(a1h, d2_h[...]) + dot_columns(a1h, d2_l[...])
+            grad2[...] += dot_columns(a1h, d2_h[...])
             grad2[:HIDDEN] += dot_columns(act1_l[step], d2_h[...])
 
         def sum_first():
@@ -274,8 +267,7 @@
             xl = jnp.concatenate([l for _, l in x], axis=1)
             ones = jnp.ones((ONES, columns), bf16)
             both = dot_columns(jnp.concatenate([xh, ones, xl], axis=0), d1_h[...])
-            other = dot_columns(jnp.concatenate([xh, ones], axis=0), d1_l[...])
-            grad1[...] += both[: FEAT + ONES] + other
+            grad1[...] += both[: FEAT + ONES]
             grad1[:FEAT] += both[FEAT + ONES :]
 
         for stage in (output, last_layer, second_layer):
@@ -363,7 +355,7 @@
         out_specs=[vmem] * 7,
         out_shape=[
             shaped(HIDDEN, 3 * FEAT + ONES, dtype=bf16),
-            shaped(HIDDEN, 3 * HIDDEN, dtype=bf16),
+            shaped(HIDDEN, 2 * HIDDEN, dtype=bf16),
             shaped(HIDDEN, 3 * HIDDEN, dtype=bf16),
             shaped(HIDDEN, 1),
             shaped(HIDDEN, 3 * OUT_ROWS, dtype=bf16),
@@ -396,8 +388,6 @@
         pltpu.VMEM((2 * OUT_ROWS, columns), bf16),
         pltpu.VMEM((HIDDEN, columns), bf16),
         pltpu.VMEM((HIDDEN, columns), bf16),
-        pltpu.VMEM((HIDDEN, columns), bf16),
-        pltpu.VMEM((HIDDEN, columns), bf16),
     ]
     width = segment if first else 2 * segment
     if final:

time: 106 us -> 99.3 us (0.937)
  Pallas kernels: 40.2 us -> 33.8 us
    pallas_call x2, Pallas kernels: 33.3 us -> 26.9 us  [step(): pl.pallas_call(functools.partial(step_kernel, first, final), in_specs=[pl...]
  transfers between devices with their start and end apart: 4 -> 4, of which waited for: 3 -> 3; matrix products, arithmetic and copies ran while one was open for 0% -> 0% of each run, Pallas kernels for 18% -> 16%
where the time goes in v6:
time: 99.3 us; the launch traced here: 98.9 us
  Pallas kernels  33.8 us (34%)
  blocking collectives  33 us (33%)
  starting transfers between devices  18.6 us (19%)
  waiting for transfers between devices  11.8 us (12%)
  between operations  1.44 us (1%)
    pallas_call x2, Pallas kernels, step(): pl.pallas_call(functools.partial(step_kernel, first, final), in_specs=[pl...  26.9 us
    all_to_all x1, blocking collectives, local(): lax.all_to_all(half.reshape(chips, PACKED // chips, 128), axes, 0, 0)  18.9 us
    all_to_all x1, blocking collectives, local(): lax.all_to_all(jnp.broadcast_to(share[None], shares.shape), axes, 0, 0)  14.1 us
    all_to_all x2, starting transfers between devices, local(): got.append(lax.all_to_all(sent, 'depth', 0, 0))  12.6 us
    all_to_all x2, waiting for transfers between devices, local(): got.append(lax.all_to_all(sent, 'depth', 0, 0))  9.5 us
    pallas_call x2, Pallas kernels, local(): pl.pallas_call(functools.partial(send_kernel, PARTS, i), in_specs=[vmem]...  4.98 us
    ppermute x1, starting transfers between devices, local(): other = lax.ppermute(own, 'core', swap)  3.1 us
    ppermute x1, starting transfers between devices, local(): half = keep + lax.ppermute(send, 'core', swap)  2.91 us
  transfers between devices with their start and end apart: 4, of which 3 were waited for; matrix products, arithmetic and copies ran while one was open for 0% of the time, Pallas kernels for 16%

profile of v6, /device:TPU:1, one launch (start us, length us, event | category | flops | bytes accessed | tf_op | source)
XLA Modules:
  0.0 98.9 jit_solution(9486101954858656943)
XLA Ops:
  0.6 2.4 %shard_map.164 = f32[16,104,128]{2,1,0:T(8,128)} custom-call(f32[96,4096]{1,0:T(8,128)} %bitcast.33, f32[3,32,128]{2,1,0:T(8,128)} %bitcast.35, s32[32,128]{1,0:T(8,128)} %bitcast.37), custom_call_target="tpu_custom_call" | custom-call | bytes 1048576 | tf_op jit(solution)/shard_map/pallas_call | solution.py:432
  3.1 8.6 %all-to-all-start.1 = ((f32[16,104,128]{2,1,0:T(8,128)}), f32[16,104,128]{2,1,0:T(8,128)S(1)}, u32[]{:S(2)}, u32[]{:S(2)}) async-start(f32[16,104,128]{2,1,0:T(8,128)} %shard_map.164), calls=%async_computation.1 | async-start | bytes 1703936 | tf_op jit(solution)/shard_map/all_to_all | solution.py:443
  11.7 0.0 copy-start
  11.7 0.0 copy-start.1
  11.7 0.0 copy-start.2
  11.7 0.0 copy-start.3
  11.7 0.0 copy-start.4
  11.7 0.0 copy-start.5
  11.8 0.0 copy-start.6
  11.8 2.5 %shard_map.162 = f32[16,104,128]{2,1,0:T(8,128)} custom-call(f32[96,4096]{1,0:T(8,128)} %bitcast.34, f32[3,32,128]{2,1,0:T(8,128)} %bitcast.36, s32[32,128]{1,0:T(8,128)} %bitcast.38), custom_call_target="tpu_custom_call" | custom-call | bytes 1048576 | tf_op jit(solution)/shard_map/pallas_call | solution.py:432
  15.0 0.0 copy-done
  15.0 0.0 copy-done.1
  15.0 0.0 copy-done.2
  15.0 0.0 copy-done.3
  15.0 0.0 copy-done.4
  15.0 0.0 copy-done.5
  15.0 0.5 shard_map.163
  15.5 0.1 pad_add_fusion.place_ref
  15.6 0.0 copy-done.6
  15.6 9.5 %all-to-all-done.1.rays_ref = f32[16,104,128]{2,1,0:T(8,128)S(1)} async-done(((f32[16,104,128]{2,1,0:T(8,128)}), f32[16,104,128]{2,1,0:T(8,128)S(1)}, u32[]{:S(2)}, u32[]{:S(2)}) %all-to-all-start.1) | async-done | bytes 852000 | tf_op jit(solution)/shard_map/all_to_all | solution.py:443
  25.1 4.0 %all-to-all-start = ((f32[16,104,128]{2,1,0:T(8,128)}), f32[16,104,128]{2,1,0:T(8,128)S(1)}, u32[]{:S(2)}, u32[]{:S(2)}) async-start(f32[16,104,128]{2,1,0:T(8,128)} %shard_map.162), calls=%async_computation | async-start | bytes 1703936 | tf_op jit(solution)/shard_map/all_to_all | solution.py:443
  29.0 13.0 %shard_map.165 = (f32[64,128]{1,0:T(8,128)S(1)}, f32[48,256]{1,0:T(8,128)S(1)}, f32[272,256]{1,0:T(8,128)S(1)}, f32[80,256]{1,0:T(8,128)S(1)}, f32[80,128]{1,0:T(8,128)S(1)}) custom-call(s32[2]{0:T(128)S(1)} %pad_add_fusion.place_ref, f32[16,104,128]{2,1,0:T(8,128)S(1)} %all-to-all-done.1.rays_ref, f32[64,128]{1,0:T(8,128)S(1)} %get-tuple-element.49.target_ref, ...), custom_call_target="tpu_custom_call" | custom-call | flops 13690208256 | bytes 1048576 | tf_op jit(solution)/shard_map/pallas_call | solution.py:398
  42.1 0.0 all-to-all-done.rays_ref
  42.1 13.8 %shard_map.166 = (f32[64,256]{1,0:T(8,128)}, f32[512,128]{1,0:T(8,128)S(1)}, f32[512,128]{1,0:T(8,128)S(1)}) custom-call(s32[2]{0:T(128)S(1)} %pad_add_fusion.place_ref, f32[16,104,128]{2,1,0:T(8,128)S(1)} %all-to-all-done.rays_ref, f32[64,128]{1,0:T(8,128)S(1)} %get-tuple-element.50.target_ref, bf16[256,112]{1,0:T(8,128)(2,1)S(1)} %get-tuple-element.28.refs_0_, ...), custom_call_target="tpu_custom_call" | custom-call | flops 13690208256 | bytes 1048576 | tf_op jit(solution)/shard_map/pallas_call | solution.py:398
  55.9 2.9 %collective-permute-start = (f32[512,128]{1,0:T(8,128)S(1)}, f32[512,128]{1,0:T(8,128)S(1)}, u32[]{:S(2)}, u32[]{:S(2)}) collective-permute-start(f32[512,128]{1,0:T(8,128)S(1)} %get-tuple-element.42), channel_id=1, source_target_pairs={{0,16},{16,0},{1,17},{17,1},{2,18},{18,2},{3,19},{19,3},{4,20},{20... | collective-permute-start | bytes 786440 | tf_op jit(solution)/shard_map/ppermute | solution.py:453
  58.8 1.2 %collective-permute-done = f32[512,128]{1,0:T(8,128)S(1)} collective-permute-done((f32[512,128]{1,0:T(8,128)S(1)}, f32[512,128]{1,0:T(8,128)S(1)}, u32[]{:S(2)}, u32[]{:S(2)}) %collective-permute-start) | collective-permute-done | bytes 262176 | tf_op jit(solution)/shard_map/ppermute | solution.py:453
  60.0 18.9 %all_to_all.20 = f32[64,8,128]{2,1,0:T(8,128)S(1)} all-to-all(f32[64,8,128]{2,1,0:T(8,128)S(1)} %add_bitcast_fusion), channel_id=1, replica_groups=mesh['chip'=4,'core'=2,'depth'=16] {'chip','depth'}, dimensions={0} | all-to-all | bytes 524288 | tf_op jit(solution)/shard_map/all_to_all | solution.py:454
  79.0 0.1 reduce_sum.9
  79.1 14.1 %all_to_all.21 = f32[64,8,128]{2,1,0:T(8,128)S(1)} all-to-all(f32[64,8,128]{2,1,0:T(8,128)S(1)} %broadcast_in_dim.22), channel_id=1, replica_groups=mesh['chip'=4,'core'=2,'depth'=16] {'chip','depth'}, dimensions={0} | all-to-all | bytes 524288 | tf_op jit(solution)/shard_map/all_to_all | solution.py:456
  93.1 3.1 %collective-permute-start.1 = (f32[512,128]{1,0:T(8,128)S(1)}, f32[512,128]{1,0:T(8,128)S(1)}, u32[]{:S(2)}, u32[]{:S(2)}) collective-permute-start(f32[512,128]{1,0:T(8,128)S(1)} %bitcast.27), channel_id=1, source_target_pairs={{0,16},{16,0},{1,17},{17,1},{2,18},{18,2},{3,19},{19,3},{4,20},{20... | collective-permute-start | bytes 786440 | tf_op jit(solution)/shard_map/ppermute | solution.py:457
  96.2 1.2 %collective-permute-done.1.other_ref = f32[512,128]{1,0:T(8,128)S(1)} collective-permute-done((f32[512,128]{1,0:T(8,128)S(1)}, f32[512,128]{1,0:T(8,128)S(1)}, u32[]{:S(2)}, u32[]{:S(2)}) %collective-permute-start.1) | collective-permute-done | bytes 262176 | tf_op jit(solution)/shard_map/ppermute | solution.py:457
  97.4 1.5 %shard_map.167 = (f32[32,256]{1,0:T(8,128)}, f32[1,256]{1,0:T(1,128)}, f32[256,256]{1,0:T(8,128)}, f32[1,256]{1,0:T(1,128)}, f32[65,256]{1,0:T(8,128)}, /*index=5*/f32[1,65]{1,0:T(1,128)}) custom-call(s32[2]{0:T(128)S(1)} %pad_add_fusion.place_ref, f32[512,128]{1,0:T(8,128)S(1)} %bitcast.28, f32[512,128]{1,0:T(8,128)S(1)} %collective-permute-done.1.other_ref), custom_call_target="tpu_custom_call" | custom-call | tf_op jit(solution)/shard_map/pallas_call | solution.py:458
  (3 shorter events, 0.1 us)
Async XLA Ops:
  3.1 22.0 %all-to-all-start.1 = ((f32[16,104,128]{2,1,0:T(8,128)}), f32[16,104,128]{2,1,0:T(8,128)S(1)}, u32[]{:S(2)}, u32[]{:S(2)}) async-start(f32[16,104,128]{2,1,0:T(8,128)} %shard_map.164), calls=%async_computation.1 | async-start | bytes 1703936 | tf_op jit(solution)/shard_map/all_to_all | solution.py:443
  11.7 3.3 %copy-start = (f32[256,256]{1,0:T(8,128)S(1)}, f32[256,256]{1,0:T(8,128)}, u32[]{:S(2)}) copy-start(f32[256,256]{1,0:T(8,128)} %second_ref.1) | copy-start | bytes 786436
  11.7 3.3 %copy-start.1 = (f32[256,65]{0,1:T(8,128)S(1)}, f32[256,65]{0,1:T(8,128)}, u32[]{:S(2)}) copy-start(f32[256,65]{0,1:T(8,128)} %param.20) | copy-start | bytes 199684
  11.7 3.3 %copy-start.2 = (f32[32,256]{1,0:T(8,128)S(1)}, f32[32,256]{1,0:T(8,128)}, u32[]{:S(2)}) copy-start(f32[32,256]{1,0:T(8,128)} %first_ref.1) | copy-start | bytes 98308
  11.7 3.3 %copy-start.3 = (f32[256]{0:T(256)S(1)}, f32[256]{0:T(256)}, u32[]{:S(2)}) copy-start(f32[256]{0:T(256)} %param.17) | copy-start | bytes 3076
  11.7 3.3 %copy-start.4 = (f32[256]{0:T(256)S(1)}, f32[256]{0:T(256)}, u32[]{:S(2)}) copy-start(f32[256]{0:T(256)} %param.19) | copy-start | bytes 3076
  11.7 3.3 %copy-start.5 = (f32[65]{0:T(128)S(1)}, f32[65]{0:T(128)}, u32[]{:S(2)}) copy-start(f32[65]{0:T(128)} %param.21) | copy-start | bytes 784
  11.8 3.8 %copy-start.6 = (f32[1,64,256]{2,1,0:T(8,128)S(1)}, f32[1,64,256]{2,1,0:T(8,128)}, u32[]{:S(2)}) copy-start(f32[1,64,256]{2,1,0:T(8,128)} %param.15) | copy-start | bytes 196612
  25.1 17.0 %all-to-all-start = ((f32[16,104,128]{2,1,0:T(8,128)}), f32[16,104,128]{2,1,0:T(8,128)S(1)}, u32[]{:S(2)}, u32[]{:S(2)}) async-start(f32[16,104,128]{2,1,0:T(8,128)} %shard_map.162), calls=%async_computation | async-start | bytes 1703936 | tf_op jit(solution)/shard_map/all_to_all | solution.py:443
  55.9 4.1 %collective-permute-start = (f32[512,128]{1,0:T(8,128)S(1)}, f32[512,128]{1,0:T(8,128)S(1)}, u32[]{:S(2)}, u32[]{:S(2)}) collective-permute-start(f32[512,128]{1,0:T(8,128)S(1)} %get-tuple-element.42), channel_id=1, source_target_pairs={{0,16},{16,0},{1,17},{17,1},{2,18},{18,2},{3,19},{19,3},{4,20},{20... | collective-permute-start | bytes 786440 | tf_op jit(solution)/shard_map/ppermute | solution.py:453
  93.1 4.3 %collective-permute-start.1 = (f32[512,128]{1,0:T(8,128)S(1)}, f32[512,128]{1,0:T(8,128)S(1)}, u32[]{:S(2)}, u32[]{:S(2)}) collective-permute-start(f32[512,128]{1,0:T(8,128)S(1)} %bitcast.27), channel_id=1, source_target_pairs={{0,16},{16,0},{1,17},{17,1},{2,18},{18,2},{3,19},{19,3},{4,20},{20... | collective-permute-start | bytes 786440 | tf_op jit(solution)/shard_map/ppermute | solution.py:457

commit v7 on v6

--- a/solution.py
+++ b/solution.py
@@ -148,6 +148,7 @@
 
     def forward(step, cum):
         ones = jnp.ones((ONES, WIDTH), bf16)
+        slot = step % 2
 
         def first_layer(tile):
             xh, xl = inputs(step, tile)
@@ -155,18 +156,18 @@
             a1h, a1l = split(a1)
             act1_h[step, :HIDDEN, at(tile)] = a1h
             act1_h[step, HIDDEN:, at(tile)] = ones
-            act1_l[step, :, at(tile)] = a1l
+            act1_l[slot, :, at(tile)] = a1l
 
         def second_layer(tile):
             a1h = act1_h[step, :HIDDEN, at(tile)]
-            z2 = dot(second_tk[...], jnp.concatenate([a1h, a1h, act1_l[step, :, at(tile)]], axis=0))
+            z2 = dot(second_tk[...], jnp.concatenate([a1h, a1h, act1_l[slot, :, at(tile)]], axis=0))
             a2h, a2l = split(jnp.maximum(z2 + second_b[...], 0.0))
             act2_h[step, :, at(tile)] = a2h
-            act2_l[step, :, at(tile)] = a2l
+            act2_l[slot, :, at(tile)] = a2l
 
         def last_layer(tile):
             both = dot(last_thl[...], act2_h[step, :, at(tile)])
-            low = dot(last_thl[:OUT_ROWS], act2_l[step, :, at(tile)])
+            low = dot(last_thl[:OUT_ROWS], act2_l[slot, :, at(tile)])
             raw = both[:OUT_ROWS] + (both[OUT_ROWS:] + low) + last_b[...]
             colors[step, :, at(tile)] = sigmoid(raw[:CHANNELS])
             logit[:, at(tile)] = raw[CHANNELS : CHANNELS + 8]
@@ -253,13 +254,10 @@
             d1_h[:, at(tile)] = jnp.where(act1_h[step, :HIDDEN, at(tile)] > 0, d1, jnp.zeros_like(d1))
 
         def sum_last():
-            d3h = d3_hl[:OUT_ROWS]
-            grad3[...] += dot_columns(d3h, act2_h[step]) + dot_columns(d3h, act2_l[step])
+            grad3[...] += dot_columns(d3_hl[:OUT_ROWS], act2_h[step])
 
         def sum_second():
-            a1h = act1_h[step]
-            grad2[...] += dot_columns(a1h, d2_h[...])
-            grad2[:HIDDEN] += dot_columns(act1_l[step], d2_h[...])
+            grad2[...] += dot_columns(act1_h[step], d2_h[...])
 
         def sum_first():
             x = [inputs(step, tile) for tile in range(tiles)]
@@ -378,9 +376,9 @@
     ]
     scratch = [
         pltpu.VMEM((steps, HIDDEN + ONES, columns), bf16),
+        pltpu.VMEM((2, HIDDEN, columns), bf16),
         pltpu.VMEM((steps, HIDDEN, columns), bf16),
-        pltpu.VMEM((steps, HIDDEN, columns), bf16),
-        pltpu.VMEM((steps, HIDDEN, columns), bf16),
+        pltpu.VMEM((2, HIDDEN, columns), bf16),
         pltpu.VMEM((steps, CHANNELS, columns), f32),
         pltpu.VMEM((steps, TOGETHER, 16, segment), f32),
         pltpu.VMEM((CHANNELS, segment), f32),

time: 99.3 us -> 95.9 us (0.966)
  Pallas kernels: 33.8 us -> 30.4 us
  blocking collectives: 33 us -> 31.3 us
  waiting for transfers between devices: 11.8 us -> 13.1 us
    pallas_call x2, Pallas kernels: 26.9 us -> 23.4 us  [step(): pl.pallas_call(functools.partial(step_kernel, first, final), in_specs=[pl...]
    all_to_all x1, blocking collectives: 18.9 us -> 17.2 us  [local(): lax.all_to_all(half.reshape(chips, PACKED // chips, 128), axes, 0, 0)]
    all_to_all x2, waiting for transfers between devices: 9.5 us -> 10.8 us  [local(): got.append(lax.all_to_all(sent, 'depth', 0, 0))]
  transfers between devices with their start and end apart: 4 -> 4, of which waited for: 3 -> 4; matrix products, arithmetic and copies ran while one was open for 0% -> 0% of each run, Pallas kernels for 16% -> 15%
where the time goes in v7:
time: 95.9 us; the launch traced here: 95.5 us
  blocking collectives  31.3 us (33%)
  Pallas kernels  30.4 us (32%)
  starting transfers between devices  19 us (20%)
  waiting for transfers between devices  13.1 us (14%)
  between operations  1.44 us (2%)
    pallas_call x2, Pallas kernels, step(): pl.pallas_call(functools.partial(step_kernel, first, final), in_specs=[pl...  23.4 us
    all_to_all x1, blocking collectives, local(): lax.all_to_all(half.reshape(chips, PACKED // chips, 128), axes, 0, 0)  17.2 us
    all_to_all x1, blocking collectives, local(): lax.all_to_all(jnp.broadcast_to(share[None], shares.shape), axes, 0, 0)  14.1 us
    all_to_all x2, starting transfers between devices, local(): got.append(lax.all_to_all(sent, 'depth', 0, 0))  12.6 us
    all_to_all x2, waiting for transfers between devices, local(): got.append(lax.all_to_all(sent, 'depth', 0, 0))  10.8 us
    pallas_call x2, Pallas kernels, local(): pl.pallas_call(functools.partial(send_kernel, PARTS, i), in_specs=[vmem]...  4.98 us
    ppermute x1, starting transfers between devices, local(): half = keep + lax.ppermute(send, 'core', swap)  3.34 us
    ppermute x1, starting transfers between devices, local(): other = lax.ppermute(own, 'core', swap)  3.1 us
  transfers between devices with their start and end apart: 4, of which 4 were waited for; matrix products, arithmetic and copies ran while one was open for 0% of the time, Pallas kernels for 15%

profile of v7, /device:TPU:1, one launch (start us, length us, event | category | flops | bytes accessed | tf_op | source)
XLA Modules:
  0.0 95.5 jit_solution(13694595628634701899)
XLA Ops:
  0.6 2.4 %shard_map.164 = f32[16,104,128]{2,1,0:T(8,128)} custom-call(f32[96,4096]{1,0:T(8,128)} %bitcast.33, f32[3,32,128]{2,1,0:T(8,128)} %bitcast.35, s32[32,128]{1,0:T(8,128)} %bitcast.37), custom_call_target="tpu_custom_call" | custom-call | bytes 1048576 | tf_op jit(solution)/shard_map/pallas_call | solution.py:430
  3.1 8.6 %all-to-all-start.1 = ((f32[16,104,128]{2,1,0:T(8,128)}), f32[16,104,128]{2,1,0:T(8,128)S(1)}, u32[]{:S(2)}, u32[]{:S(2)}) async-start(f32[16,104,128]{2,1,0:T(8,128)} %shard_map.164), calls=%async_computation.1 | async-start | bytes 1703936 | tf_op jit(solution)/shard_map/all_to_all | solution.py:441
  11.7 0.0 copy-start
  11.7 0.0 copy-start.1
  11.7 0.0 copy-start.2
  11.7 0.0 copy-start.3
  11.7 0.0 copy-start.4
  11.7 0.0 copy-start.5
  11.8 0.0 copy-start.6
  11.8 2.5 %shard_map.162 = f32[16,104,128]{2,1,0:T(8,128)} custom-call(f32[96,4096]{1,0:T(8,128)} %bitcast.34, f32[3,32,128]{2,1,0:T(8,128)} %bitcast.36, s32[32,128]{1,0:T(8,128)} %bitcast.38), custom_call_target="tpu_custom_call" | custom-call | bytes 1048576 | tf_op jit(solution)/shard_map/pallas_call | solution.py:430
  15.0 0.0 copy-done
  15.0 0.0 copy-done.1
  15.0 0.0 copy-done.2
  15.0 0.0 copy-done.3
  15.0 0.0 copy-done.4
  15.0 0.0 copy-done.5
  15.0 0.5 shard_map.163
  15.5 0.1 pad_add_fusion.place_ref
  15.6 0.0 copy-done.6
  15.6 9.5 %all-to-all-done.1.rays_ref = f32[16,104,128]{2,1,0:T(8,128)S(1)} async-done(((f32[16,104,128]{2,1,0:T(8,128)}), f32[16,104,128]{2,1,0:T(8,128)S(1)}, u32[]{:S(2)}, u32[]{:S(2)}) %all-to-all-start.1) | async-done | bytes 852000 | tf_op jit(solution)/shard_map/all_to_all | solution.py:441
  25.1 4.0 %all-to-all-start = ((f32[16,104,128]{2,1,0:T(8,128)}), f32[16,104,128]{2,1,0:T(8,128)S(1)}, u32[]{:S(2)}, u32[]{:S(2)}) async-start(f32[16,104,128]{2,1,0:T(8,128)} %shard_map.162), calls=%async_computation | async-start | bytes 1703936 | tf_op jit(solution)/shard_map/all_to_all | solution.py:441
  29.0 11.3 %shard_map.165 = (f32[64,128]{1,0:T(8,128)S(1)}, f32[48,256]{1,0:T(8,128)S(1)}, f32[272,256]{1,0:T(8,128)S(1)}, f32[80,256]{1,0:T(8,128)S(1)}, f32[80,128]{1,0:T(8,128)S(1)}) custom-call(s32[2]{0:T(128)S(1)} %pad_add_fusion.place_ref, f32[16,104,128]{2,1,0:T(8,128)S(1)} %all-to-all-done.1.rays_ref, f32[64,128]{1,0:T(8,128)S(1)} %get-tuple-element.49.target_ref, ...), custom_call_target="tpu_custom_call" | custom-call | flops 13690208256 | bytes 1048576 | tf_op jit(solution)/shard_map/pallas_call | solution.py:396
  40.3 1.3 %all-to-all-done.rays_ref = f32[16,104,128]{2,1,0:T(8,128)S(1)} async-done(((f32[16,104,128]{2,1,0:T(8,128)}), f32[16,104,128]{2,1,0:T(8,128)S(1)}, u32[]{:S(2)}, u32[]{:S(2)}) %all-to-all-start) | async-done | bytes 852000 | tf_op jit(solution)/shard_map/all_to_all | solution.py:441
  41.6 12.2 %shard_map.166 = (f32[64,256]{1,0:T(8,128)}, f32[512,128]{1,0:T(8,128)S(1)}, f32[512,128]{1,0:T(8,128)S(1)}) custom-call(s32[2]{0:T(128)S(1)} %pad_add_fusion.place_ref, f32[16,104,128]{2,1,0:T(8,128)S(1)} %all-to-all-done.rays_ref, f32[64,128]{1,0:T(8,128)S(1)} %get-tuple-element.50.target_ref, bf16[256,112]{1,0:T(8,128)(2,1)S(1)} %get-tuple-element.28.refs_0_, ...), custom_call_target="tpu_custom_call" | custom-call | flops 13690208256 | bytes 1048576 | tf_op jit(solution)/shard_map/pallas_call | solution.py:396
  53.8 3.3 %collective-permute-start = (f32[512,128]{1,0:T(8,128)S(1)}, f32[512,128]{1,0:T(8,128)S(1)}, u32[]{:S(2)}, u32[]{:S(2)}) collective-permute-start(f32[512,128]{1,0:T(8,128)S(1)} %get-tuple-element.42), channel_id=1, source_target_pairs={{0,16},{16,0},{1,17},{17,1},{2,18},{18,2},{3,19},{19,3},{4,20},{20... | collective-permute-start | bytes 786440 | tf_op jit(solution)/shard_map/ppermute | solution.py:451
  57.1 1.2 %collective-permute-done = f32[512,128]{1,0:T(8,128)S(1)} collective-permute-done((f32[512,128]{1,0:T(8,128)S(1)}, f32[512,128]{1,0:T(8,128)S(1)}, u32[]{:S(2)}, u32[]{:S(2)}) %collective-permute-start) | collective-permute-done | bytes 262176 | tf_op jit(solution)/shard_map/ppermute | solution.py:451
  58.3 17.2 %all_to_all.20 = f32[64,8,128]{2,1,0:T(8,128)S(1)} all-to-all(f32[64,8,128]{2,1,0:T(8,128)S(1)} %add_bitcast_fusion), channel_id=1, replica_groups=mesh['chip'=4,'core'=2,'depth'=16] {'chip','depth'}, dimensions={0} | all-to-all | bytes 524288 | tf_op jit(solution)/shard_map/all_to_all | solution.py:452
  75.6 0.1 reduce_sum.9
  75.7 14.1 %all_to_all.21 = f32[64,8,128]{2,1,0:T(8,128)S(1)} all-to-all(f32[64,8,128]{2,1,0:T(8,128)S(1)} %broadcast_in_dim.22), channel_id=1, replica_groups=mesh['chip'=4,'core'=2,'depth'=16] {'chip','depth'}, dimensions={0} | all-to-all | bytes 524288 | tf_op jit(solution)/shard_map/all_to_all | solution.py:454
  89.7 3.1 %collective-permute-start.1 = (f32[512,128]{1,0:T(8,128)S(1)}, f32[512,128]{1,0:T(8,128)S(1)}, u32[]{:S(2)}, u32[]{:S(2)}) collective-permute-start(f32[512,128]{1,0:T(8,128)S(1)} %bitcast.27), channel_id=1, source_target_pairs={{0,16},{16,0},{1,17},{17,1},{2,18},{18,2},{3,19},{19,3},{4,20},{20... | collective-permute-start | bytes 786440 | tf_op jit(solution)/shard_map/ppermute | solution.py:455
  92.8 1.2 %collective-permute-done.1.other_ref = f32[512,128]{1,0:T(8,128)S(1)} collective-permute-done((f32[512,128]{1,0:T(8,128)S(1)}, f32[512,128]{1,0:T(8,128)S(1)}, u32[]{:S(2)}, u32[]{:S(2)}) %collective-permute-start.1) | collective-permute-done | bytes 262176 | tf_op jit(solution)/shard_map/ppermute | solution.py:455
  94.0 1.5 %shard_map.167 = (f32[32,256]{1,0:T(8,128)}, f32[1,256]{1,0:T(1,128)}, f32[256,256]{1,0:T(8,128)}, f32[1,256]{1,0:T(1,128)}, f32[65,256]{1,0:T(8,128)}, /*index=5*/f32[1,65]{1,0:T(1,128)}) custom-call(s32[2]{0:T(128)S(1)} %pad_add_fusion.place_ref, f32[512,128]{1,0:T(8,128)S(1)} %bitcast.28, f32[512,128]{1,0:T(8,128)S(1)} %collective-permute-done.1.other_ref), custom_call_target="tpu_custom_call" | custom-call | tf_op jit(solution)/shard_map/pallas_call | solution.py:456
  (3 shorter events, 0.1 us)
Async XLA Ops:
  3.1 22.0 %all-to-all-start.1 = ((f32[16,104,128]{2,1,0:T(8,128)}), f32[16,104,128]{2,1,0:T(8,128)S(1)}, u32[]{:S(2)}, u32[]{:S(2)}) async-start(f32[16,104,128]{2,1,0:T(8,128)} %shard_map.164), calls=%async_computation.1 | async-start | bytes 1703936 | tf_op jit(solution)/shard_map/all_to_all | solution.py:441
  11.7 3.3 %copy-start = (f32[256,256]{1,0:T(8,128)S(1)}, f32[256,256]{1,0:T(8,128)}, u32[]{:S(2)}) copy-start(f32[256,256]{1,0:T(8,128)} %second_ref.1) | copy-start | bytes 786436
  11.7 3.3 %copy-start.1 = (f32[256,65]{0,1:T(8,128)S(1)}, f32[256,65]{0,1:T(8,128)}, u32[]{:S(2)}) copy-start(f32[256,65]{0,1:T(8,128)} %param.20) | copy-start | bytes 199684
  11.7 3.3 %copy-start.2 = (f32[32,256]{1,0:T(8,128)S(1)}, f32[32,256]{1,0:T(8,128)}, u32[]{:S(2)}) copy-start(f32[32,256]{1,0:T(8,128)} %first_ref.1) | copy-start | bytes 98308
  11.7 3.3 %copy-start.3 = (f32[256]{0:T(256)S(1)}, f32[256]{0:T(256)}, u32[]{:S(2)}) copy-start(f32[256]{0:T(256)} %param.17) | copy-start | bytes 3076
  11.7 3.3 %copy-start.4 = (f32[256]{0:T(256)S(1)}, f32[256]{0:T(256)}, u32[]{:S(2)}) copy-start(f32[256]{0:T(256)} %param.19) | copy-start | bytes 3076
  11.7 3.3 %copy-start.5 = (f32[65]{0:T(128)S(1)}, f32[65]{0:T(128)}, u32[]{:S(2)}) copy-start(f32[65]{0:T(128)} %param.21) | copy-start | bytes 784
  11.8 3.8 %copy-start.6 = (f32[1,64,256]{2,1,0:T(8,128)S(1)}, f32[1,64,256]{2,1,0:T(8,128)}, u32[]{:S(2)}) copy-start(f32[1,64,256]{2,1,0:T(8,128)} %param.15) | copy-start | bytes 196612
  25.1 16.6 %all-to-all-start = ((f32[16,104,128]{2,1,0:T(8,128)}), f32[16,104,128]{2,1,0:T(8,128)S(1)}, u32[]{:S(2)}, u32[]{:S(2)}) async-start(f32[16,104,128]{2,1,0:T(8,128)} %shard_map.162), calls=%async_computation | async-start | bytes 1703936 | tf_op jit(solution)/shard_map/all_to_all | solution.py:441
  53.8 4.5 %collective-permute-start = (f32[512,128]{1,0:T(8,128)S(1)}, f32[512,128]{1,0:T(8,128)S(1)}, u32[]{:S(2)}, u32[]{:S(2)}) collective-permute-start(f32[512,128]{1,0:T(8,128)S(1)} %get-tuple-element.42), channel_id=1, source_target_pairs={{0,16},{16,0},{1,17},{17,1},{2,18},{18,2},{3,19},{19,3},{4,20},{20... | collective-permute-start | bytes 786440 | tf_op jit(solution)/shard_map/ppermute | solution.py:451
  89.7 4.3 %collective-permute-start.1 = (f32[512,128]{1,0:T(8,128)S(1)}, f32[512,128]{1,0:T(8,128)S(1)}, u32[]{:S(2)}, u32[]{:S(2)}) collective-permute-start(f32[512,128]{1,0:T(8,128)S(1)} %bitcast.27), channel_id=1, source_target_pairs={{0,16},{16,0},{1,17},{17,1},{2,18},{18,2},{3,19},{19,3},{4,20},{20... | collective-permute-start | bytes 786440 | tf_op jit(solution)/shard_map/ppermute | solution.py:455

commit v8 on v7

--- a/solution.py
+++ b/solution.py
@@ -18,7 +18,8 @@
 HEIGHT = 104
 PARTS = 2
 TOGETHER = 4
-UNROLL = 2
+FORWARD_UNROLL = 2
+BACKWARD_UNROLL = 4
 WIDTH = 512
 PACKED = 512
 
@@ -201,7 +202,7 @@
         return cum
 
     steps = regions // TOGETHER
-    lax.fori_loop(0, steps, forward, jnp.zeros((1, segment), f32), unroll=UNROLL)
+    lax.fori_loop(0, steps, forward, jnp.zeros((1, segment), f32), unroll=FORWARD_UNROLL)
     pixels = misfit_ref[...]
     misfit_ref[...] = pixels - target_ref[...]
     if first:
@@ -276,7 +277,7 @@
         sum_first()
         return behind
 
-    lax.fori_loop(0, steps, backward, jnp.zeros((1, segment), f32), unroll=UNROLL)
+    lax.fori_loop(0, steps, backward, jnp.zeros((1, segment), f32), unroll=BACKWARD_UNROLL)
     if not final:
         return
 

time: 95.9 us -> 95.2 us (level)
  no operation moved by 1% of the time
where the time goes in v8:
time: 95.2 us; the launch traced here: 94.8 us
  blocking collectives  31 us (33%)
  Pallas kernels  29.6 us (31%)
  starting transfers between devices  19 us (20%)
  waiting for transfers between devices  13.4 us (14%)
  between operations  1.44 us (2%)
    pallas_call x2, Pallas kernels, step(): pl.pallas_call(functools.partial(step_kernel, first, final), in_specs=[pl...  22.7 us
    all_to_all x1, blocking collectives, local(): lax.all_to_all(half.reshape(chips, PACKED // chips, 128), axes, 0, 0)  16.9 us
    all_to_all x1, blocking collectives, local(): lax.all_to_all(jnp.broadcast_to(share[None], shares.shape), axes, 0, 0)  14.1 us
    all_to_all x2, starting transfers between devices, local(): got.append(lax.all_to_all(sent, 'depth', 0, 0))  12.6 us
    all_to_all x2, waiting for transfers between devices, local(): got.append(lax.all_to_all(sent, 'depth', 0, 0))  11.1 us
    pallas_call x2, Pallas kernels, local(): pl.pallas_call(functools.partial(send_kernel, PARTS, i), in_specs=[vmem]...  4.98 us
    ppermute x1, starting transfers between devices, local(): half = keep + lax.ppermute(send, 'core', swap)  3.35 us
    ppermute x1, starting transfers between devices, local(): other = lax.ppermute(own, 'core', swap)  3.1 us
  transfers between devices with their start and end apart: 4, of which 4 were waited for; matrix products, arithmetic and copies ran while one was open for 0% of the time, Pallas kernels for 15%

profile of v8, /device:TPU:1, one launch (start us, length us, event | category | flops | bytes accessed | tf_op | source)
XLA Modules:
  0.0 94.8 jit_solution(9160629647718095250)
XLA Ops:
  0.6 2.4 %shard_map.164 = f32[16,104,128]{2,1,0:T(8,128)} custom-call(f32[96,4096]{1,0:T(8,128)} %bitcast.33, f32[3,32,128]{2,1,0:T(8,128)} %bitcast.35, s32[32,128]{1,0:T(8,128)} %bitcast.37), custom_call_target="tpu_custom_call" | custom-call | bytes 1048576 | tf_op jit(solution)/shard_map/pallas_call | solution.py:431
  3.1 8.6 %all-to-all-start.1 = ((f32[16,104,128]{2,1,0:T(8,128)}), f32[16,104,128]{2,1,0:T(8,128)S(1)}, u32[]{:S(2)}, u32[]{:S(2)}) async-start(f32[16,104,128]{2,1,0:T(8,128)} %shard_map.164), calls=%async_computation.1 | async-start | bytes 1703936 | tf_op jit(solution)/shard_map/all_to_all | solution.py:442
  11.7 0.0 copy-start
  11.7 0.0 copy-start.1
  11.7 0.0 copy-start.2
  11.7 0.0 copy-start.3
  11.7 0.0 copy-start.4
  11.7 0.0 copy-start.5
  11.8 0.0 copy-start.6
  11.8 2.5 %shard_map.162 = f32[16,104,128]{2,1,0:T(8,128)} custom-call(f32[96,4096]{1,0:T(8,128)} %bitcast.34, f32[3,32,128]{2,1,0:T(8,128)} %bitcast.36, s32[32,128]{1,0:T(8,128)} %bitcast.38), custom_call_target="tpu_custom_call" | custom-call | bytes 1048576 | tf_op jit(solution)/shard_map/pallas_call | solution.py:431
  15.0 0.0 copy-done
  15.0 0.0 copy-done.1
  15.0 0.0 copy-done.2
  15.0 0.0 copy-done.3
  15.0 0.0 copy-done.4
  15.0 0.0 copy-done.5
  15.0 0.5 shard_map.163
  15.5 0.1 pad_add_fusion.place_ref
  15.6 0.0 copy-done.6
  15.6 9.5 %all-to-all-done.1.rays_ref = f32[16,104,128]{2,1,0:T(8,128)S(1)} async-done(((f32[16,104,128]{2,1,0:T(8,128)}), f32[16,104,128]{2,1,0:T(8,128)S(1)}, u32[]{:S(2)}, u32[]{:S(2)}) %all-to-all-start.1) | async-done | bytes 852000 | tf_op jit(solution)/shard_map/all_to_all | solution.py:442
  25.1 4.0 %all-to-all-start = ((f32[16,104,128]{2,1,0:T(8,128)}), f32[16,104,128]{2,1,0:T(8,128)S(1)}, u32[]{:S(2)}, u32[]{:S(2)}) async-start(f32[16,104,128]{2,1,0:T(8,128)} %shard_map.162), calls=%async_computation | async-start | bytes 1703936 | tf_op jit(solution)/shard_map/all_to_all | solution.py:442
  29.0 11.0 %shard_map.165 = (f32[64,128]{1,0:T(8,128)S(1)}, f32[48,256]{1,0:T(8,128)S(1)}, f32[272,256]{1,0:T(8,128)S(1)}, f32[80,256]{1,0:T(8,128)S(1)}, f32[80,128]{1,0:T(8,128)S(1)}) custom-call(s32[2]{0:T(128)S(1)} %pad_add_fusion.place_ref, f32[16,104,128]{2,1,0:T(8,128)S(1)} %all-to-all-done.1.rays_ref, f32[64,128]{1,0:T(8,128)S(1)} %get-tuple-element.49.target_ref, ...), custom_call_target="tpu_custom_call" | custom-call | flops 13690208256 | bytes 1048576 | tf_op jit(solution)/shard_map/pallas_call | solution.py:397
  40.0 1.6 %all-to-all-done.rays_ref = f32[16,104,128]{2,1,0:T(8,128)S(1)} async-done(((f32[16,104,128]{2,1,0:T(8,128)}), f32[16,104,128]{2,1,0:T(8,128)S(1)}, u32[]{:S(2)}, u32[]{:S(2)}) %all-to-all-start) | async-done | bytes 852000 | tf_op jit(solution)/shard_map/all_to_all | solution.py:442
  41.6 11.7 %shard_map.166 = (f32[64,256]{1,0:T(8,128)}, f32[512,128]{1,0:T(8,128)S(1)}, f32[512,128]{1,0:T(8,128)S(1)}) custom-call(s32[2]{0:T(128)S(1)} %pad_add_fusion.place_ref, f32[16,104,128]{2,1,0:T(8,128)S(1)} %all-to-all-done.rays_ref, f32[64,128]{1,0:T(8,128)S(1)} %get-tuple-element.50.target_ref, bf16[256,112]{1,0:T(8,128)(2,1)S(1)} %get-tuple-element.28.refs_0_, ...), custom_call_target="tpu_custom_call" | custom-call | flops 13690208256 | bytes 1048576 | tf_op jit(solution)/shard_map/pallas_call | solution.py:397
  53.4 3.3 %collective-permute-start = (f32[512,128]{1,0:T(8,128)S(1)}, f32[512,128]{1,0:T(8,128)S(1)}, u32[]{:S(2)}, u32[]{:S(2)}) collective-permute-start(f32[512,128]{1,0:T(8,128)S(1)} %get-tuple-element.42), channel_id=1, source_target_pairs={{0,16},{16,0},{1,17},{17,1},{2,18},{18,2},{3,19},{19,3},{4,20},{20... | collective-permute-start | bytes 786440 | tf_op jit(solution)/shard_map/ppermute | solution.py:452
  56.7 1.2 %collective-permute-done = f32[512,128]{1,0:T(8,128)S(1)} collective-permute-done((f32[512,128]{1,0:T(8,128)S(1)}, f32[512,128]{1,0:T(8,128)S(1)}, u32[]{:S(2)}, u32[]{:S(2)}) %collective-permute-start) | collective-permute-done | bytes 262176 | tf_op jit(solution)/shard_map/ppermute | solution.py:452
  57.9 16.9 %all_to_all.20 = f32[64,8,128]{2,1,0:T(8,128)S(1)} all-to-all(f32[64,8,128]{2,1,0:T(8,128)S(1)} %add_bitcast_fusion), channel_id=1, replica_groups=mesh['chip'=4,'core'=2,'depth'=16] {'chip','depth'}, dimensions={0} | all-to-all | bytes 524288 | tf_op jit(solution)/shard_map/all_to_all | solution.py:453
  74.8 0.1 reduce_sum.9
  74.9 14.1 %all_to_all.21 = f32[64,8,128]{2,1,0:T(8,128)S(1)} all-to-all(f32[64,8,128]{2,1,0:T(8,128)S(1)} %broadcast_in_dim.22), channel_id=1, replica_groups=mesh['chip'=4,'core'=2,'depth'=16] {'chip','depth'}, dimensions={0} | all-to-all | bytes 524288 | tf_op jit(solution)/shard_map/all_to_all | solution.py:455
  89.0 3.1 %collective-permute-start.1 = (f32[512,128]{1,0:T(8,128)S(1)}, f32[512,128]{1,0:T(8,128)S(1)}, u32[]{:S(2)}, u32[]{:S(2)}) collective-permute-start(f32[512,128]{1,0:T(8,128)S(1)} %bitcast.27), channel_id=1, source_target_pairs={{0,16},{16,0},{1,17},{17,1},{2,18},{18,2},{3,19},{19,3},{4,20},{20... | collective-permute-start | bytes 786440 | tf_op jit(solution)/shard_map/ppermute | solution.py:456
  92.1 1.2 %collective-permute-done.1.other_ref = f32[512,128]{1,0:T(8,128)S(1)} collective-permute-done((f32[512,128]{1,0:T(8,128)S(1)}, f32[512,128]{1,0:T(8,128)S(1)}, u32[]{:S(2)}, u32[]{:S(2)}) %collective-permute-start.1) | collective-permute-done | bytes 262176 | tf_op jit(solution)/shard_map/ppermute | solution.py:456
  93.3 1.5 %shard_map.167 = (f32[32,256]{1,0:T(8,128)}, f32[1,256]{1,0:T(1,128)}, f32[256,256]{1,0:T(8,128)}, f32[1,256]{1,0:T(1,128)}, f32[65,256]{1,0:T(8,128)}, /*index=5*/f32[1,65]{1,0:T(1,128)}) custom-call(s32[2]{0:T(128)S(1)} %pad_add_fusion.place_ref, f32[512,128]{1,0:T(8,128)S(1)} %bitcast.28, f32[512,128]{1,0:T(8,128)S(1)} %collective-permute-done.1.other_ref), custom_call_target="tpu_custom_call" | custom-call | tf_op jit(solution)/shard_map/pallas_call | solution.py:457
  (3 shorter events, 0.1 us)
Async XLA Ops:
  3.1 22.0 %all-to-all-start.1 = ((f32[16,104,128]{2,1,0:T(8,128)}), f32[16,104,128]{2,1,0:T(8,128)S(1)}, u32[]{:S(2)}, u32[]{:S(2)}) async-start(f32[16,104,128]{2,1,0:T(8,128)} %shard_map.164), calls=%async_computation.1 | async-start | bytes 1703936 | tf_op jit(solution)/shard_map/all_to_all | solution.py:442
  11.7 3.3 %copy-start = (f32[256,256]{1,0:T(8,128)S(1)}, f32[256,256]{1,0:T(8,128)}, u32[]{:S(2)}) copy-start(f32[256,256]{1,0:T(8,128)} %second_ref.1) | copy-start | bytes 786436
  11.7 3.3 %copy-start.1 = (f32[256,65]{0,1:T(8,128)S(1)}, f32[256,65]{0,1:T(8,128)}, u32[]{:S(2)}) copy-start(f32[256,65]{0,1:T(8,128)} %param.20) | copy-start | bytes 199684
  11.7 3.3 %copy-start.2 = (f32[32,256]{1,0:T(8,128)S(1)}, f32[32,256]{1,0:T(8,128)}, u32[]{:S(2)}) copy-start(f32[32,256]{1,0:T(8,128)} %first_ref.1) | copy-start | bytes 98308
  11.7 3.3 %copy-start.3 = (f32[256]{0:T(256)S(1)}, f32[256]{0:T(256)}, u32[]{:S(2)}) copy-start(f32[256]{0:T(256)} %param.17) | copy-start | bytes 3076
  11.7 3.3 %copy-start.4 = (f32[256]{0:T(256)S(1)}, f32[256]{0:T(256)}, u32[]{:S(2)}) copy-start(f32[256]{0:T(256)} %param.19) | copy-start | bytes 3076
  11.7 3.3 %copy-start.5 = (f32[65]{0:T(128)S(1)}, f32[65]{0:T(128)}, u32[]{:S(2)}) copy-start(f32[65]{0:T(128)} %param.21) | copy-start | bytes 784
  11.8 3.8 %copy-start.6 = (f32[1,64,256]{2,1,0:T(8,128)S(1)}, f32[1,64,256]{2,1,0:T(8,128)}, u32[]{:S(2)}) copy-start(f32[1,64,256]{2,1,0:T(8,128)} %param.15) | copy-start | bytes 196612
  25.1 16.6 %all-to-all-start = ((f32[16,104,128]{2,1,0:T(8,128)}), f32[16,104,128]{2,1,0:T(8,128)S(1)}, u32[]{:S(2)}, u32[]{:S(2)}) async-start(f32[16,104,128]{2,1,0:T(8,128)} %shard_map.162), calls=%async_computation | async-start | bytes 1703936 | tf_op jit(solution)/shard_map/all_to_all | solution.py:442
  53.4 4.5 %collective-permute-start = (f32[512,128]{1,0:T(8,128)S(1)}, f32[512,128]{1,0:T(8,128)S(1)}, u32[]{:S(2)}, u32[]{:S(2)}) collective-permute-start(f32[512,128]{1,0:T(8,128)S(1)} %get-tuple-element.42), channel_id=1, source_target_pairs={{0,16},{16,0},{1,17},{17,1},{2,18},{18,2},{3,19},{19,3},{4,20},{20... | collective-permute-start | bytes 786440 | tf_op jit(solution)/shard_map/ppermute | solution.py:452
  89.0 4.3 %collective-permute-start.1 = (f32[512,128]{1,0:T(8,128)S(1)}, f32[512,128]{1,0:T(8,128)S(1)}, u32[]{:S(2)}, u32[]{:S(2)}) collective-permute-start(f32[512,128]{1,0:T(8,128)S(1)} %bitcast.27), channel_id=1, source_target_pairs={{0,16},{16,0},{1,17},{17,1},{2,18},{18,2},{3,19},{19,3},{4,20},{20... | collective-permute-start | bytes 786440 | tf_op jit(solution)/shard_map/ppermute | solution.py:456

commit v9 on v8

--- a/solution.py
+++ b/solution.py
@@ -48,11 +48,11 @@
     for j in range(regions):
         start = (j * parts + i) * lanes
         sent_ref[j, : SAMPLES * FEAT, :] = features_ref[:, start : start + lanes]
-        row = (j * parts + i) * wide
-        for k in range(wide):
+        row = j * parts * wide
+        for k in range(wide if i == 0 else 0):
             sent_ref[j, SAMPLES * FEAT :, k * 128 : (k + 1) * 128] = jnp.concatenate(
-                [v[row + k : row + k + 1] for v in lengths]
-                + [jnp.zeros((HEIGHT - SAMPLES * FEAT - SAMPLES, 128), f32)],
+                [v[row + q * wide + k : row + q * wide + k + 1] for q in range(parts) for v in lengths]
+                + [jnp.zeros((HEIGHT - SAMPLES * (FEAT + parts), 128), f32)],
                 axis=0,
             )
 
@@ -101,8 +101,11 @@
     first_k, second_k, second_tk, second_b, last_k, last_thl, last_b = refs[:7]
     refs = refs[7:]
     if not first:
-        pixels_in, grad1_in, grad2_in, grad3_in, bias3_in = refs[:5]
-        refs = refs[5:]
+        lengths_ref, pixels_in, grad1_in, grad2_in, grad3_in, bias3_in = refs[:6]
+        refs = refs[6:]
+    else:
+        lengths_ref = rays_ref
+    top = SAMPLES * FEAT if first else SAMPLES * (FEAT + 1)
     if final:
         pixels_ref, keep_ref, send_ref = refs[:3]
         grad1, grad2, grad3, bias3 = refs[3:7]
@@ -188,7 +191,7 @@
             rows[step, g, 9:10, :] = passed
             for s in range(SAMPLES):
                 i = g * SAMPLES + s
-                length = rays_ref[d, SAMPLES * FEAT + s : SAMPLES * FEAT + s + 1, :]
+                length = lengths_ref[d, top + s : top + s + 1, :]
                 optical = part(density, g, s) * length
                 weight = before * (1.0 - jnp.exp(-optical))
                 total = total + optical
@@ -432,7 +435,7 @@
             functools.partial(send_kernel, PARTS, i),
             in_specs=[vmem] * 3,
             out_specs=vmem,
-            out_shape=shaped(regions, HEIGHT, lanes),
+            out_shape=shaped(regions, HEIGHT if i == 0 else SAMPLES * FEAT, lanes),
             cost_estimate=pl.CostEstimate(flops=0, bytes_accessed=2**20, transcendentals=0),
         )(
             features[0, 0].transpose(1, 0, 2).reshape(SAMPLES * FEAT, rays),
@@ -444,7 +447,7 @@
     carried = []
     for i in range(PARTS):
         goal = target[0, :, i * lanes : (i + 1) * lanes]
-        carried = step(i == 0, i == PARTS - 1, place, got[i], goal, weights, carried)
+        carried = step(i == 0, i == PARTS - 1, place, got[i], goal, weights, [got[0], *carried] if i else [])
     pixels, keep, send = carried
 
     swap = [(0, 1), (1, 0)]

time: 95.2 us -> 95.2 us (level)
  waiting for transfers between devices: 13.4 us -> 11.8 us
    all_to_all x2, waiting for transfers between devices: 11.1 us -> 9.51 us  [local(): got.append(lax.all_to_all(sent, 'depth', 0, 0))]
  transfers between devices with their start and end apart: 4 -> 4, of which waited for: 4 -> 3; matrix products, arithmetic and copies ran while one was open for 0% -> 0% of each run, Pallas kernels for 15% -> 15%
where the time goes in v9:
time: 95.2 us; the launch traced here: 94.8 us
  blocking collectives  31.7 us (33%)
  Pallas kernels  29.6 us (31%)
  starting transfers between devices  19.9 us (21%)
  waiting for transfers between devices  11.8 us (12%)
  between operations  1.44 us (2%)
    pallas_call x2, Pallas kernels, step(): pl.pallas_call(functools.partial(step_kernel, first, final), in_specs=[pl...  22.8 us
    all_to_all x1, blocking collectives, local(): lax.all_to_all(half.reshape(chips, PACKED // chips, 128), axes, 0, 0)  17.7 us
    all_to_all x1, blocking collectives, local(): lax.all_to_all(jnp.broadcast_to(share[None], shares.shape), axes, 0, 0)  14.1 us
    all_to_all x2, starting transfers between devices, local(): got.append(lax.all_to_all(sent, 'depth', 0, 0))  12.6 us
    all_to_all x2, waiting for transfers between devices, local(): got.append(lax.all_to_all(sent, 'depth', 0, 0))  9.51 us
    pallas_call x2, Pallas kernels, local(): pl.pallas_call(functools.partial(send_kernel, PARTS, i), in_specs=[vmem]...  4.94 us
    ppermute x1, starting transfers between devices, local(): half = keep + lax.ppermute(send, 'core', swap)  4.2 us
    ppermute x1, starting transfers between devices, local(): other = lax.ppermute(own, 'core', swap)  3.1 us
  transfers between devices with their start and end apart: 4, of which 3 were waited for; matrix products, arithmetic and copies ran while one was open for 0% of the time, Pallas kernels for 15%

profile of v9, /device:TPU:1, one launch (start us, length us, event | category | flops | bytes accessed | tf_op | source)
XLA Modules:
  0.0 94.8 jit_solution(12471818162937617914)
XLA Ops:
  0.6 2.4 %shard_map.164 = f32[16,104,128]{2,1,0:T(8,128)} custom-call(f32[96,4096]{1,0:T(8,128)} %bitcast.33, f32[3,32,128]{2,1,0:T(8,128)} %bitcast.35, s32[32,128]{1,0:T(8,128)} %bitcast.37), custom_call_target="tpu_custom_call" | custom-call | bytes 1048576 | tf_op jit(solution)/shard_map/pallas_call | solution.py:434
  3.0 8.6 %all-to-all-start.1 = ((f32[16,104,128]{2,1,0:T(8,128)}), f32[16,104,128]{2,1,0:T(8,128)S(1)}, u32[]{:S(2)}, u32[]{:S(2)}) async-start(f32[16,104,128]{2,1,0:T(8,128)} %shard_map.164), calls=%async_computation.1 | async-start | bytes 1703936 | tf_op jit(solution)/shard_map/all_to_all | solution.py:445
  11.7 0.0 copy-start
  11.7 0.0 copy-start.1
  11.7 0.0 copy-start.2
  11.7 0.0 copy-start.3
  11.7 0.0 copy-start.4
  11.7 0.0 copy-start.5
  11.7 0.0 copy-start.6
  11.7 2.5 %shard_map.162 = f32[16,96,128]{2,1,0:T(8,128)} custom-call(f32[96,4096]{1,0:T(8,128)} %bitcast.34, f32[3,32,128]{2,1,0:T(8,128)} %bitcast.36, s32[32,128]{1,0:T(8,128)} %bitcast.38), custom_call_target="tpu_custom_call" | custom-call | bytes 1048576 | tf_op jit(solution)/shard_map/pallas_call | solution.py:434
  14.9 0.0 copy-done
  14.9 0.0 copy-done.1
  14.9 0.0 copy-done.2
  14.9 0.0 copy-done.3
  15.0 0.0 copy-done.4
  15.0 0.0 copy-done.5
  15.0 0.5 shard_map.163
  15.4 0.1 pad_add_fusion.place_ref
  15.5 0.0 copy-done.6
  15.5 9.5 %all-to-all-done.1.rays_ref.refs_7_ = f32[16,104,128]{2,1,0:T(8,128)S(1)} async-done(((f32[16,104,128]{2,1,0:T(8,128)}), f32[16,104,128]{2,1,0:T(8,128)S(1)}, u32[]{:S(2)}, u32[]{:S(2)}) %all-to-all-start.1) | async-done | bytes 852000 | tf_op jit(solution)/shard_map/all_to_all | solution.py:445
  25.0 4.0 %all-to-all-start = ((f32[16,96,128]{2,1,0:T(8,128)}), f32[16,96,128]{2,1,0:T(8,128)S(1)}, u32[]{:S(2)}, u32[]{:S(2)}) async-start(f32[16,96,128]{2,1,0:T(8,128)} %shard_map.162), calls=%async_computation | async-start | bytes 1572864 | tf_op jit(solution)/shard_map/all_to_all | solution.py:445
  29.0 11.0 %shard_map.165 = (f32[64,128]{1,0:T(8,128)S(1)}, f32[48,256]{1,0:T(8,128)S(1)}, f32[272,256]{1,0:T(8,128)S(1)}, f32[80,256]{1,0:T(8,128)S(1)}, f32[80,128]{1,0:T(8,128)S(1)}) custom-call(s32[2]{0:T(128)S(1)} %pad_add_fusion.place_ref, f32[16,104,128]{2,1,0:T(8,128)S(1)} %all-to-all-done.1.rays_ref.refs_7_, f32[64,128]{1,0:T(8,128)S(1)} %get-tuple-element.49.target_ref, ...), custom_call_target="tpu_custom_call" | custom-call | flops 13690208256 | bytes 1048576 | tf_op jit(solution)/shard_map/pallas_call | solution.py:400
  40.0 0.0 all-to-all-done.rays_ref
  40.0 11.8 %shard_map.166 = (f32[64,256]{1,0:T(8,128)}, f32[512,128]{1,0:T(8,128)S(1)}, f32[512,128]{1,0:T(8,128)S(1)}) custom-call(s32[2]{0:T(128)S(1)} %pad_add_fusion.place_ref, f32[16,96,128]{2,1,0:T(8,128)S(1)} %all-to-all-done.rays_ref, f32[64,128]{1,0:T(8,128)S(1)} %get-tuple-element.50.target_ref, bf16[256,112]{1,0:T(8,128)(2,1)S(1)} %get-tuple-element.28.refs_0_, ...), custom_call_target="tpu_custom_call" | custom-call | flops 13690208256 | bytes 1048576 | tf_op jit(solution)/shard_map/pallas_call | solution.py:400
  51.8 4.2 %collective-permute-start = (f32[512,128]{1,0:T(8,128)S(1)}, f32[512,128]{1,0:T(8,128)S(1)}, u32[]{:S(2)}, u32[]{:S(2)}) collective-permute-start(f32[512,128]{1,0:T(8,128)S(1)} %get-tuple-element.42), channel_id=1, source_target_pairs={{0,16},{16,0},{1,17},{17,1},{2,18},{18,2},{3,19},{19,3},{4,20},{20... | collective-permute-start | bytes 786440 | tf_op jit(solution)/shard_map/ppermute | solution.py:455
  56.0 1.2 %collective-permute-done = f32[512,128]{1,0:T(8,128)S(1)} collective-permute-done((f32[512,128]{1,0:T(8,128)S(1)}, f32[512,128]{1,0:T(8,128)S(1)}, u32[]{:S(2)}, u32[]{:S(2)}) %collective-permute-start) | collective-permute-done | bytes 262176 | tf_op jit(solution)/shard_map/ppermute | solution.py:455
  57.2 17.7 %all_to_all.20 = f32[64,8,128]{2,1,0:T(8,128)S(1)} all-to-all(f32[64,8,128]{2,1,0:T(8,128)S(1)} %add_bitcast_fusion), channel_id=1, replica_groups=mesh['chip'=4,'core'=2,'depth'=16] {'chip','depth'}, dimensions={0} | all-to-all | bytes 524288 | tf_op jit(solution)/shard_map/all_to_all | solution.py:456
  74.8 0.1 reduce_sum.9
  74.9 14.1 %all_to_all.21 = f32[64,8,128]{2,1,0:T(8,128)S(1)} all-to-all(f32[64,8,128]{2,1,0:T(8,128)S(1)} %broadcast_in_dim.22), channel_id=1, replica_groups=mesh['chip'=4,'core'=2,'depth'=16] {'chip','depth'}, dimensions={0} | all-to-all | bytes 524288 | tf_op jit(solution)/shard_map/all_to_all | solution.py:458
  89.0 3.1 %collective-permute-start.1 = (f32[512,128]{1,0:T(8,128)S(1)}, f32[512,128]{1,0:T(8,128)S(1)}, u32[]{:S(2)}, u32[]{:S(2)}) collective-permute-start(f32[512,128]{1,0:T(8,128)S(1)} %bitcast.27), channel_id=1, source_target_pairs={{0,16},{16,0},{1,17},{17,1},{2,18},{18,2},{3,19},{19,3},{4,20},{20... | collective-permute-start | bytes 786440 | tf_op jit(solution)/shard_map/ppermute | solution.py:459
  92.1 1.2 %collective-permute-done.1.other_ref = f32[512,128]{1,0:T(8,128)S(1)} collective-permute-done((f32[512,128]{1,0:T(8,128)S(1)}, f32[512,128]{1,0:T(8,128)S(1)}, u32[]{:S(2)}, u32[]{:S(2)}) %collective-permute-start.1) | collective-permute-done | bytes 262176 | tf_op jit(solution)/shard_map/ppermute | solution.py:459
  93.3 1.5 %shard_map.167 = (f32[32,256]{1,0:T(8,128)}, f32[1,256]{1,0:T(1,128)}, f32[256,256]{1,0:T(8,128)}, f32[1,256]{1,0:T(1,128)}, f32[65,256]{1,0:T(8,128)}, /*index=5*/f32[1,65]{1,0:T(1,128)}) custom-call(s32[2]{0:T(128)S(1)} %pad_add_fusion.place_ref, f32[512,128]{1,0:T(8,128)S(1)} %bitcast.28, f32[512,128]{1,0:T(8,128)S(1)} %collective-permute-done.1.other_ref), custom_call_target="tpu_custom_call" | custom-call | tf_op jit(solution)/shard_map/pallas_call | solution.py:460
  (3 shorter events, 0.1 us)
Async XLA Ops:
  3.0 22.0 %all-to-all-start.1 = ((f32[16,104,128]{2,1,0:T(8,128)}), f32[16,104,128]{2,1,0:T(8,128)S(1)}, u32[]{:S(2)}, u32[]{:S(2)}) async-start(f32[16,104,128]{2,1,0:T(8,128)} %shard_map.164), calls=%async_computation.1 | async-start | bytes 1703936 | tf_op jit(solution)/shard_map/all_to_all | solution.py:445
  11.7 3.3 %copy-start = (f32[256,256]{1,0:T(8,128)S(1)}, f32[256,256]{1,0:T(8,128)}, u32[]{:S(2)}) copy-start(f32[256,256]{1,0:T(8,128)} %second_ref.1) | copy-start | bytes 786436
  11.7 3.3 %copy-start.1 = (f32[256,65]{0,1:T(8,128)S(1)}, f32[256,65]{0,1:T(8,128)}, u32[]{:S(2)}) copy-start(f32[256,65]{0,1:T(8,128)} %param.20) | copy-start | bytes 199684
  11.7 3.3 %copy-start.2 = (f32[32,256]{1,0:T(8,128)S(1)}, f32[32,256]{1,0:T(8,128)}, u32[]{:S(2)}) copy-start(f32[32,256]{1,0:T(8,128)} %first_ref.1) | copy-start | bytes 98308
  11.7 3.3 %copy-start.3 = (f32[256]{0:T(256)S(1)}, f32[256]{0:T(256)}, u32[]{:S(2)}) copy-start(f32[256]{0:T(256)} %param.17) | copy-start | bytes 3076
  11.7 3.3 %copy-start.4 = (f32[256]{0:T(256)S(1)}, f32[256]{0:T(256)}, u32[]{:S(2)}) copy-start(f32[256]{0:T(256)} %param.19) | copy-start | bytes 3076
  11.7 3.3 %copy-start.5 = (f32[65]{0:T(128)S(1)}, f32[65]{0:T(128)}, u32[]{:S(2)}) copy-start(f32[65]{0:T(128)} %param.21) | copy-start | bytes 784
  11.7 3.8 %copy-start.6 = (f32[1,64,256]{2,1,0:T(8,128)S(1)}, f32[1,64,256]{2,1,0:T(8,128)}, u32[]{:S(2)}) copy-start(f32[1,64,256]{2,1,0:T(8,128)} %param.15) | copy-start | bytes 196612
  25.0 15.0 %all-to-all-start = ((f32[16,96,128]{2,1,0:T(8,128)}), f32[16,96,128]{2,1,0:T(8,128)S(1)}, u32[]{:S(2)}, u32[]{:S(2)}) async-start(f32[16,96,128]{2,1,0:T(8,128)} %shard_map.162), calls=%async_computation | async-start | bytes 1572864 | tf_op jit(solution)/shard_map/all_to_all | solution.py:445
  51.8 5.4 %collective-permute-start = (f32[512,128]{1,0:T(8,128)S(1)}, f32[512,128]{1,0:T(8,128)S(1)}, u32[]{:S(2)}, u32[]{:S(2)}) collective-permute-start(f32[512,128]{1,0:T(8,128)S(1)} %get-tuple-element.42), channel_id=1, source_target_pairs={{0,16},{16,0},{1,17},{17,1},{2,18},{18,2},{3,19},{19,3},{4,20},{20... | collective-permute-start | bytes 786440 | tf_op jit(solution)/shard_map/ppermute | solution.py:455
  89.0 4.3 %collective-permute-start.1 = (f32[512,128]{1,0:T(8,128)S(1)}, f32[512,128]{1,0:T(8,128)S(1)}, u32[]{:S(2)}, u32[]{:S(2)}) collective-permute-start(f32[512,128]{1,0:T(8,128)S(1)} %bitcast.27), channel_id=1, source_target_pairs={{0,16},{16,0},{1,17},{17,1},{2,18},{18,2},{3,19},{19,3},{4,20},{20... | collective-permute-start | bytes 786440 | tf_op jit(solution)/shard_map/ppermute | solution.py:459
